TPU v7x, 32 devices: a whole 2x2x4 slice. The times are simulated.
32 devices in a mesh: section: 8 (over y, x, core), dp: 4 (over z).
Axes of the slice: x: 2, y: 2, z: 4, core: 2. Of those that a mesh axis runs over, the one named last changes fastest.
Arguments:
- inputs: bfloat16 [512, 4096], P(None, 'dp'), may hold values from -6 to 6
- targets: int32 [4096], P('dp'), may hold values from 0 to 255
- mel: bfloat16 [80, 16], P(None, 'dp'), may hold values from -6 to 6
- speakers: int32 [16, 2], P('dp'), may hold values from 0 to 108
- speaker_sample_counts: int32 [109], replicated, may hold values from 16 to 4111
- segment_offsets: int32 [16, 2], P('dp'), may hold values from 64 to 256, as said below
- dilations: int32 [8], P('section'), may hold values from 1 to 32, as said below
- dilated_kernel: bfloat16 [8, 1024, 1024], P('section'), may hold values from -0.1875 to 0.1875
- conditioning_projection: bfloat16 [8, 1024, 80], P('section'), may hold values from -0.5 to 0.5
- dilated_gate_bias: bfloat16 [8, 1024], P('section'), may hold values from -3 to 3
- residual_projection: bfloat16 [8, 512, 512], P('section'), may hold values from -0.75 to 0.75
- skip_projection: bfloat16 [8, 512, 512], P('section'), may hold values from -0.75 to 0.75
- upsample_weight: bfloat16 [256, 80, 80], replicated, may hold values from -0.625 to 0.625
- speaker_table: bfloat16 [80, 109], replicated, may hold values from -5 to 5
- first_output_projection: bfloat16 [512, 512], replicated, may hold values from -0.5 to 0.5
- class_projection: bfloat16 [256, 512], replicated, may hold values from -0.75 to 0.75
Outputs:
- loss: float32 [], replicated
- grad_inputs: bfloat16 [512, 4096], P('section', 'dp')
- grad_w_dil: float32 [8, 1024, 1024], P('section')
- grad_w_cond: float32 [8, 1024, 80], P('section')
- grad_b_gate: float32 [8, 1024], P('section')
- grad_w_res: float32 [8, 512, 512], P('section')
- grad_w_skip: float32 [8, 512, 512], P('section')
- grad_w_up: float32 [256, 80, 80], replicated
- grad_spk_table: float32 [80, 109], replicated
- grad_w_post: float32 [512, 512], replicated
- grad_w_out: float32 [256, 512], replicated
Inputs may be any that keep to these rules, and one draw needn't show every extreme that they name: `segment_offsets`: per micro-batch: the second segment begins after 256 // 4 to 128 samples and has 64 to 128 samples; the second column is where it ends. `dilations`: each a power of two.
All inputs are finite; a program needn't handle non-finite values.
Results may differ from a plain program's by a relative error of at most 0.03.
Values may be sent and summed in bfloat16 or wider, within the bound.
A program may use at most 128 MiB of HBM per device.

v0:
```python
import math

import jax
import jax.numpy as jnp
from jax import lax
from jax.sharding import PartitionSpec as P

HALF_ROOT = 0.7071067811865476
WEIGHT_SCALE = 64.0
HIGHEST_LEVEL = lax.Precision.HIGHEST


def broadcast(block, axis, source):
    block = jnp.where(lax.axis_index(axis) == source, block, jnp.zeros_like(block))
    return lax.psum(block, axis)


def shifted_2(value, axis, steps):
    count = lax.axis_size(axis)
    leading, last = (max(0, -steps), min(count, count - steps))
    return lax.ppermute(value, axis, [(source, source + steps) for source in range(leading, last)])


def delayed(values, dilation_factor):
    length = values.shape[-1]
    padded = jnp.concatenate([jnp.zeros_like(values), values], axis=-1)
    return lax.dynamic_slice_in_dim(padded, length - dilation_factor, length, axis=values.ndim - 1)


def advanced(values, dilation_factor):
    length = values.shape[-1]
    padded = jnp.concatenate([values, jnp.zeros_like(values)], axis=-1)
    return lax.dynamic_slice_in_dim(padded, dilation_factor, length, axis=values.ndim - 1)


def transposed_product(left, right):
    return lax.dot_general(
        left, right, (((0,), (0,)), ((), ())), preferred_element_type=jnp.float32
    )


def outer_product(left, right):
    return lax.dot_general(
        left, right, (((1,), (1,)), ((), ())), preferred_element_type=jnp.float32
    )


def silu_slope(values):
    sig_part = jax.nn.sigmoid(values)
    return sig_part * (1.0 + values * (1.0 - sig_part))


def up_grad(grad_three, mel_f32):
    return jnp.einsum("cfk,af->kca", grad_three, mel_f32, precision=HIGHEST_LEVEL)


def table_grad(grad_four, later_four, seg_onehot):
    second_sum = jnp.einsum("cbfk,bfk->cb", grad_four, later_four, precision=HIGHEST_LEVEL)
    first_sum = jnp.einsum("cbfk,bfk->cb", grad_four, 1.0 - later_four, precision=HIGHEST_LEVEL)
    seg_sums = jnp.stack([first_sum, second_sum], axis=2).reshape(grad_four.shape[0], -1)
    return jnp.dot(seg_sums, seg_onehot, precision=HIGHEST_LEVEL)


def local(
    inputs,
    targets,
    mel,
    speakers,
    speaker_sample_counts,
    segment_offsets,
    dilations,
    dilated_kernel,
    conditioning_projection,
    dilated_gate_bias,
    residual_projection,
    skip_projection,
    upsample_weight,
    speaker_table,
    first_output_projection,
    class_projection,
):
    section_count = lax.axis_size("section")
    section_index = lax.axis_index("section")
    micro_count = segment_offsets.shape[0]
    res_ch, tok_count = inputs.shape
    length = tok_count // micro_count
    mel_ch, frames_dev = mel.shape
    hop_size = upsample_weight.shape[0]
    per_micro = length // hop_size
    dilated_weight = dilated_kernel[0]
    conditioning_weight = conditioning_projection[0]
    bias_of_gate = dilated_gate_bias[0].astype(jnp.float32)
    residual_weight = residual_projection[0]
    skip_matrix = skip_projection[0]
    half_gate = residual_weight.shape[1]
    skip_ch = skip_matrix.shape[0]
    dilation_factor = dilations[0]
    time_index = jnp.arange(length, dtype=jnp.int32)
    later_mask = time_index[None, :] >= segment_offsets[:, 0:1]
    seg_start = jnp.where(later_mask, segment_offsets[:, 0:1], 0)
    keep_mask = time_index[None, :] - dilation_factor >= seg_start
    live_mask = (time_index[None, :] < segment_offsets[:, 1:2]).astype(jnp.float32)
    speaker_index = jnp.arange(speaker_table.shape[1], dtype=jnp.int32)
    seg_onehot = (speakers.reshape(-1)[:, None] == speaker_index[None, :]).astype(jnp.float32)
    seg_counts = jnp.sum(seg_onehot * speaker_sample_counts.astype(jnp.float32)[None, :], axis=1)
    seg_weight = (WEIGHT_SCALE * lax.rsqrt(seg_counts)).reshape(micro_count, 2)
    weight_rows = jnp.where(later_mask, seg_weight[:, 1:2], seg_weight[:, 0:1]) * live_mask
    target_rows = targets.reshape(micro_count, length)
    head_scale = 1.0 / math.sqrt(section_count)
    classes = jnp.arange(class_projection.shape[0], dtype=jnp.int32)
    is_last = section_index == section_count - 1

    def local_cond():
        up_sampled = jnp.einsum(
            "kca,af->cfk", upsample_weight, mel, preferred_element_type=jnp.float32
        ).reshape(mel_ch, tok_count)
        seg_columns = jnp.dot(
            speaker_table.astype(jnp.float32), seg_onehot.T, precision=HIGHEST_LEVEL
        ).reshape(mel_ch, micro_count, 2)
        spk_vectors = jnp.where(
            later_mask[None], seg_columns[:, :, 1:2], seg_columns[:, :, 0:1]
        ).reshape(mel_ch, tok_count)
        return (up_sampled + spk_vectors).astype(jnp.bfloat16)

    root_cond = lax.cond(
        section_index == 0, local_cond, lambda: jnp.zeros((mel_ch, tok_count), jnp.bfloat16)
    )
    cond_all = broadcast(root_cond, "section", 0)

    def layer_forward(layer_in, skip_from, cond_slot, keep_row):
        shifted = jnp.where(
            keep_row[None, :], delayed(layer_in, dilation_factor), jnp.zeros((), jnp.bfloat16)
        )
        stacked_layers = jnp.concatenate([shifted, layer_in], axis=0)
        gate_preactivation = jnp.dot(
            dilated_weight, stacked_layers, preferred_element_type=jnp.float32
        )
        gate_preactivation = (
            gate_preactivation
            + jnp.dot(conditioning_weight, cond_slot, preferred_element_type=jnp.float32)
            + bias_of_gate[:, None]
        )
        hidden = (
            jnp.tanh(gate_preactivation[:half_gate])
            * jax.nn.sigmoid(gate_preactivation[half_gate:])
        ).astype(jnp.bfloat16)
        residual = jnp.dot(residual_weight, hidden, preferred_element_type=jnp.float32)
        skipped = jnp.dot(skip_matrix, hidden, preferred_element_type=jnp.float32)
        out_res = ((layer_in.astype(jnp.float32) + residual) * HALF_ROOT).astype(jnp.bfloat16)
        out_skip = skip_from + skipped
        return (out_res, out_skip, gate_preactivation)

    def head_pass(total_row, target_row, weight_row):
        scaled = total_row.astype(jnp.float32) * head_scale
        first_act = jax.nn.silu(scaled).astype(jnp.bfloat16)
        post_pre = jnp.dot(first_output_projection, first_act, preferred_element_type=jnp.float32)
        second_act = jax.nn.silu(post_pre).astype(jnp.bfloat16)
        logits = jnp.dot(class_projection, second_act, preferred_element_type=jnp.float32)
        top_logit = jnp.max(logits, axis=0, keepdims=True)
        expo_logit = jnp.exp(logits - top_logit)
        denominator = jnp.sum(expo_logit, axis=0, keepdims=True)
        log_norm = top_logit[0] + jnp.log(denominator[0])
        hit_mask = target_row[None, :] == classes[:, None]
        picked = jnp.sum(jnp.where(hit_mask, logits, 0.0), axis=0)
        loss_part = jnp.sum(weight_row * (log_norm - picked))
        grad_logits = (
            weight_row[None, :] * (expo_logit / denominator - hit_mask.astype(jnp.float32))
        ).astype(jnp.bfloat16)
        grad_outw = outer_product(grad_logits, second_act)
        grad_post = (
            transposed_product(class_projection, grad_logits) * silu_slope(post_pre)
        ).astype(jnp.bfloat16)
        grad_postw = outer_product(grad_post, first_act)
        grad_first = transposed_product(first_output_projection, grad_post)
        grad_total = (grad_first * silu_slope(scaled) * head_scale).astype(jnp.bfloat16)
        return (grad_total, grad_postw, grad_outw, loss_part)

    zero_res = jnp.zeros((res_ch, length), jnp.bfloat16)
    zero_skip = jnp.zeros((skip_ch, length), jnp.float32)
    kept_fields = jnp.zeros((micro_count, res_ch, length), jnp.bfloat16)
    kept_gates = jnp.zeros((micro_count, 2 * half_gate, length), jnp.float32)
    skip_store = jnp.zeros((micro_count, skip_ch, length), jnp.bfloat16)
    head_state = (
        skip_store,
        jnp.zeros(first_output_projection.shape, jnp.float32),
        jnp.zeros(class_projection.shape, jnp.float32),
        jnp.zeros((), jnp.float32),
    )

    def forward_step(step_index, state_carry):
        res_in, skip_in, kept_fields, kept_gates, head_state = state_carry
        micro_index = step_index - section_index
        is_valid = (micro_index >= 0) & (micro_index < micro_count)
        slot_index = jnp.clip(micro_index, 0, micro_count - 1)
        own_input = lax.dynamic_slice_in_dim(inputs, slot_index * length, length, axis=1)
        layer_in = jnp.where(section_index == 0, own_input, res_in)
        skip_from = jnp.where(section_index == 0, jnp.zeros_like(skip_in), skip_in)
        cond_slot = lax.dynamic_slice_in_dim(cond_all, slot_index * length, length, axis=1)
        keep_row = keep_mask[slot_index]

        def run_layer(operands):
            layer_in, skip_from, kept_fields, kept_gates = operands
            out_res, out_skip, gate_preactivation = layer_forward(
                layer_in, skip_from, cond_slot, keep_row
            )
            kept_fields = lax.dynamic_update_index_in_dim(kept_fields, layer_in, slot_index, 0)
            kept_gates = lax.dynamic_update_index_in_dim(
                kept_gates, gate_preactivation, slot_index, 0
            )
            return (out_res, out_skip, kept_fields, kept_gates)

        def pass_layer(operands):
            return (
                jnp.zeros_like(operands[0]),
                jnp.zeros_like(operands[1]),
                operands[2],
                operands[3],
            )

        out_res, out_skip, kept_fields, kept_gates = lax.cond(
            is_valid, run_layer, pass_layer, (layer_in, skip_from, kept_fields, kept_gates)
        )
        res_next = shifted_2(out_res, "section", 1)
        at_head = is_valid & is_last
        total_low = out_skip.astype(jnp.bfloat16)

        def run_head(operands):
            grad_store, grad_postw, grad_outw, loss_sum = operands
            grad_total, post_part, out_part, loss_part = head_pass(
                total_low, target_rows[slot_index], weight_rows[slot_index]
            )
            grad_store = lax.dynamic_update_index_in_dim(grad_store, grad_total, slot_index, 0)
            return (grad_store, grad_postw + post_part, grad_outw + out_part, loss_sum + loss_part)

        def pass_head(operands):
            return operands

        head_state = lax.cond(at_head, run_head, pass_head, head_state)
        skip_next = shifted_2(out_skip, "section", 1)
        return (res_next, skip_next, kept_fields, kept_gates, head_state)

    step_count = micro_count + section_count - 1
    state_carry = (zero_res, zero_skip, kept_fields, kept_gates, head_state)
    unused_res, unused_skip, kept_fields, kept_gates, head_state = lax.fori_loop(
        0, step_count, forward_step, state_carry
    )
    grad_totals = broadcast(head_state[0], "section", section_count - 1)
    grad_postw, grad_outw, loss_sum = (head_state[1], head_state[2], head_state[3])
    accum_init = (
        jnp.zeros(dilated_weight.shape, jnp.float32),
        jnp.zeros(conditioning_weight.shape, jnp.float32),
        jnp.zeros(bias_of_gate.shape, jnp.float32),
        jnp.zeros(residual_weight.shape, jnp.float32),
        jnp.zeros(skip_matrix.shape, jnp.float32),
    )
    grad_fields = jnp.zeros((res_ch, tok_count), jnp.bfloat16)
    grad_cond = jnp.zeros((mel_ch, tok_count), jnp.float32)

    def backward_step(step_index, state_carry):
        grad_in, grad_fields, grad_cond, accumulators = state_carry
        micro_index = step_index - (section_count - 1 - section_index)
        is_valid = (micro_index >= 0) & (micro_index < micro_count)
        slot_index = jnp.clip(micro_index, 0, micro_count - 1)

        def run_back(operands):
            grad_in, grad_fields, grad_cond, accumulators = operands
            layer_in = lax.dynamic_index_in_dim(kept_fields, slot_index, 0, keepdims=False)
            gate_preactivation = lax.dynamic_index_in_dim(kept_gates, slot_index, 0, keepdims=False)
            grad_total = lax.dynamic_index_in_dim(grad_totals, slot_index, 0, keepdims=False)
            cond_slot = lax.dynamic_slice_in_dim(cond_all, slot_index * length, length, axis=1)
            keep_row = keep_mask[slot_index]
            shifted = jnp.where(
                keep_row[None, :], delayed(layer_in, dilation_factor), jnp.zeros((), jnp.bfloat16)
            )
            stacked_layers = jnp.concatenate([shifted, layer_in], axis=0)
            tanh_part = jnp.tanh(gate_preactivation[:half_gate])
            sig_part = jax.nn.sigmoid(gate_preactivation[half_gate:])
            hidden = (tanh_part * sig_part).astype(jnp.bfloat16)
            grad_hidden = HALF_ROOT * transposed_product(
                residual_weight, grad_in
            ) + transposed_product(skip_matrix, grad_total)
            gate_gradient = jnp.concatenate(
                [
                    grad_hidden * sig_part * (1.0 - tanh_part * tanh_part),
                    grad_hidden * tanh_part * sig_part * (1.0 - sig_part),
                ],
                axis=0,
            ).astype(jnp.bfloat16)
            (
                dilated_accumulator,
                conditioning_accumulator,
                bias_accumulator,
                residual_accumulator,
                skip_accumulator,
            ) = accumulators
            dilated_accumulator = dilated_accumulator + outer_product(gate_gradient, stacked_layers)
            conditioning_accumulator = conditioning_accumulator + outer_product(
                gate_gradient, cond_slot
            )
            bias_accumulator = bias_accumulator + jnp.sum(gate_gradient.astype(jnp.float32), axis=1)
            residual_accumulator = residual_accumulator + HALF_ROOT * outer_product(grad_in, hidden)
            skip_accumulator = skip_accumulator + outer_product(grad_total, hidden)
            stacked_gradient = transposed_product(dilated_weight, gate_gradient)
            grad_delay = jnp.where(keep_row[None, :], stacked_gradient[:res_ch], 0.0)
            grad_field = (
                HALF_ROOT * grad_in.astype(jnp.float32)
                + stacked_gradient[res_ch:]
                + advanced(grad_delay, dilation_factor)
            )
            grad_out = grad_field.astype(jnp.bfloat16)
            grad_fields = lax.dynamic_update_slice_in_dim(
                grad_fields, grad_out, slot_index * length, axis=1
            )
            grad_cond_slot = transposed_product(conditioning_weight, gate_gradient)
            grad_cond = lax.dynamic_update_slice_in_dim(
                grad_cond, grad_cond_slot, slot_index * length, axis=1
            )
            return (
                grad_out,
                grad_fields,
                grad_cond,
                (
                    dilated_accumulator,
                    conditioning_accumulator,
                    bias_accumulator,
                    residual_accumulator,
                    skip_accumulator,
                ),
            )

        def pass_back(operands):
            return (jnp.zeros_like(operands[0]),) + tuple(operands[1:])

        grad_out, grad_fields, grad_cond, accumulators = lax.cond(
            is_valid, run_back, pass_back, (grad_in, grad_fields, grad_cond, accumulators)
        )
        grad_next = shifted_2(grad_out, "section", -1)
        return (grad_next, grad_fields, grad_cond, accumulators)

    back_state = (zero_res, grad_fields, grad_cond, accum_init)
    unused_grad, grad_fields, grad_cond, accumulators = lax.fori_loop(
        0, step_count, backward_step, back_state
    )
    input_term = jnp.where(section_index == 0, grad_fields.astype(jnp.float32), 0.0)
    grad_inputs = lax.psum_scatter(
        input_term.astype(jnp.bfloat16), "section", scatter_dimension=0, tiled=True
    )
    dilated_sum, conditioning_sum, bias_sum_total, residual_sum, skip_sum_total = (
        lax.psum(accumulators[0].astype(jnp.bfloat16), "dp").astype(jnp.float32),
        lax.psum(accumulators[1].astype(jnp.bfloat16), "dp").astype(jnp.float32),
        lax.psum(accumulators[2].astype(jnp.bfloat16), "dp").astype(jnp.float32),
        lax.psum(accumulators[3].astype(jnp.bfloat16), "dp").astype(jnp.float32),
        lax.psum(accumulators[4].astype(jnp.bfloat16), "dp").astype(jnp.float32),
    )
    mel_f32 = mel.astype(jnp.float32)
    later_four = later_mask.astype(jnp.float32).reshape(micro_count, per_micro, hop_size)
    hop_share = hop_size // section_count
    cond_part = lax.psum_scatter(
        grad_cond.reshape(mel_ch, frames_dev, hop_size).astype(jnp.bfloat16),
        "section",
        scatter_dimension=2,
        tiled=True,
    ).astype(jnp.float32)
    first_offset = section_index * hop_share
    later_part = lax.dynamic_slice_in_dim(later_four, first_offset, hop_share, axis=2)
    up_part = up_grad(cond_part, mel_f32)
    grad_up = lax.dynamic_update_slice_in_dim(
        jnp.zeros(upsample_weight.shape, jnp.float32), up_part, first_offset, axis=0
    )
    grad_table = table_grad(
        cond_part.reshape(mel_ch, micro_count, per_micro, hop_share), later_part, seg_onehot
    )
    grad_up, grad_table, grad_postw, grad_outw, loss_total = lax.psum(
        (grad_up, grad_table, grad_postw, grad_outw, loss_sum), ("section", "dp")
    )
    return (
        loss_total,
        grad_inputs,
        dilated_sum[None],
        conditioning_sum[None],
        bias_sum_total[None],
        residual_sum[None],
        skip_sum_total[None],
        grad_up,
        grad_table,
        grad_postw,
        grad_outw,
    )


def solution(mesh):
    return jax.shard_map(
        local,
        mesh=mesh,
        in_specs=(
            P(None, "dp"),
            P("dp"),
            P(None, "dp"),
            P("dp", None),
            P(),
            P("dp", None),
            P("section"),
            P("section", None, None),
            P("section", None, None),
            P("section", None),
            P("section", None, None),
            P("section", None, None),
            P(),
            P(),
            P(),
            P(),
        ),
        out_specs=(
            P(),
            P("section", "dp"),
            P("section", None, None),
            P("section", None, None),
            P("section", None),
            P("section", None, None),
            P("section", None, None),
            P(),
            P(),
            P(),
            P(),
        ),
        check_vma=False,
    )
```

profile of v0, /device:TPU:0, one launch (start us, length us, event | category | flops | bytes accessed | tf_op | source)
XLA Modules:
  0.0 1105.4 jit_solution(15526140463333276355)
XLA Ops:
  9.0 3.5 conditional.4
  9.1 2.5 fusion.8
  16.7 49.7 %all-reduce.13.cloned.1.call-done = bf16[80,1024]{1,0:T(8,128)(2,1)} async-done(((bf16[80,1024]{1,0:T(8,128)(2,1)}), bf16[80,1024]{1,0:T(8,128)(2,1)}) %all-reduce.13.cloned.1.call-update) | async-done | bytes 163856 | tf_op jit(solution)/shard_map/psum | solution.py:15
  68.2 2.5 broadcast_in_dim.196
  73.8 217.9 %while.61 = (s32[]{:T(128)}, bf16[512,256]{0,1:T(8,128)(2,1)}, f32[512,256]{0,1:T(8,128)S(1)}, bf16[4,512,256]{1,2,0:T(8,128)(2,1)}, f32[4,1024,256]{1,2,0:T(8,1...) while((s32[]{:T(128)}, bf16[512,256]{0,1:T(8,128)(2,1)}, ...), condition=%wide.region_13.14_spmd.clone.clone, body=%wide.region_4.13_spmd.clone.clone.sunk | while | flops 1461586432 | bytes 45463384 | solution.py:244
  73.9 9.8 conditional.14
  88.4 9.8 conditional.14
  98.3 4.0 collective-permute-start.2
  106.3 9.8 conditional.14
  116.1 8.0 collective-permute-start.2
  124.1 4.3 collective-permute-start.1
  130.5 9.8 conditional.14
  140.3 8.0 collective-permute-start.2
  148.3 4.3 collective-permute-start.1
  154.7 2.3 conditional.14
  157.0 15.5 %collective-permute-start.2 = (f32[512,256]{0,1:T(8,128)}, f32[512,256]{0,1:T(8,128)S(1)}, u32[]{:S(2)}, u32[]{:S(2)}) collective-permute-start(f32[512,256]{0,1:T(8,128)} %get-tuple-element.2396), channel_id=1, source_target_pairs={{0,4},{4,8},{8,12},{12,16},{16,20},{20,24},{24,28},{1,5},{5,9},{9,... | collective-permute-start | bytes 1572872 | tf_op jit(solution)/shard_map/while/body/eval_jaxpr/ppermute | solution.py:21
  172.5 4.3 collective-permute-start.1
  181.2 7.9 collective-permute-start.2
  189.1 11.9 %collective-permute-start.1 = (bf16[512,256]{0,1:T(8,128)(2,1)}, bf16[512,256]{0,1:T(8,128)(2,1)S(1)}, u32[]{:S(2)}, u32[]{:S(2)}) collective-permute-start(bf16[512,256]{0,1:T(8,128)(2,1)} %get-tuple-element.2395), channel_id=1, source_target_pairs={{0,4},{4,8},{8,12},{12,16},{16,20},{20,24},{24,28},{1,5},{5,9},{9,... | collective-permute-start | bytes 786440 | tf_op jit(solution)/shard_map/while/body/eval_jaxpr/ppermute | solution.py:21
  205.4 7.9 collective-permute-start.2
  213.3 4.3 collective-permute-start.1
  222.0 7.9 collective-permute-start.2
  229.9 4.3 collective-permute-start.1
  238.6 7.9 collective-permute-start.2
  246.5 6.8 collective-permute-start.1
  257.7 10.1 collective-permute-start.2
  267.8 4.3 collective-permute-start.1
  276.6 8.8 collective-permute-start.2
  285.3 4.3 collective-permute-start.1
  293.0 5.4 copy.83
  300.6 72.7 %all-reduce.15.cloned.1.call-done = bf16[4,512,256]{1,2,0:T(8,128)(2,1)} async-done(((bf16[4,512,256]{1,2,0:T(8,128)(2,1)}), bf16[4,512,256]{1,2,0:T(8,128)(2,1)}) %all-reduce.15.cloned.1.call-update) | async-done | bytes 1048592 | tf_op jit(solution)/shard_map/psum | solution.py:15
  377.4 2.5 broadcast_in_dim.205
  382.8 299.3 %while.60 = (s32[]{:T(128)}, bf16[512,256]{1,0:T(8,128)(2,1)S(1)}, bf16[512,1024]{1,0:T(8,128)(2,1)}, bf16[80,1024]{1,0:T(8,128)(2,1)}, f32[1024,1024]{1,0:T(8,1...) while((s32[]{:T(128)}, bf16[512,256]{1,0:T(8,128)(2,1)S(1)}, ...), condition=%wide.region_20.21_spmd.clone, body=%wide.region_16.20_spmd.clone.sunk | while | flops 1707164416 | bytes 67947272 | solution.py:341
  384.9 2.3 collective-permute-done
  389.2 5.0 collective-permute-done
  396.2 6.6 collective-permute-done
  404.9 6.6 collective-permute-done
  413.5 6.6 collective-permute-done
  422.1 6.6 collective-permute-done
  430.7 135.3 %collective-permute-done = bf16[512,256]{1,0:T(8,128)(2,1)S(1)} collective-permute-done((bf16[512,256]{1,0:T(8,128)(2,1)}, bf16[512,256]{1,0:T(8,128)(2,1)S(1)}, u32[]{:S(2)}, u32[]{:S(2)}) %collective-permute-start) | collective-permute-done | bytes 262176 | tf_op jit(solution)/shard_map/while/body/eval_jaxpr/ppermute | solution.py:21
  566.1 21.5 %conditional.13 = (bf16[512,256]{1,0:T(8,128)(2,1)}, bf16[512,1024]{1,0:T(8,128)(2,1)}, bf16[80,1024]{1,0:T(8,128)(2,1)}, f32[1024,1024]{1,0:T(8,128)}, f32[1024...) conditional(s32[]{:T(128)} %convert_element_type.256, ...), branch_computations={%region_17.17_spmd, %region_18.19_spmd.clone} | conditional | flops 1707164416 | bytes 66894076 | solution.py:334
  576.9 5.1 convolution_add_fusion.3
  588.9 7.5 collective-permute-done
  596.4 21.5 %conditional.13 = (bf16[512,256]{1,0:T(8,128)(2,1)}, bf16[512,1024]{1,0:T(8,128)(2,1)}, bf16[80,1024]{1,0:T(8,128)(2,1)}, f32[1024,1024]{1,0:T(8,128)}, f32[1024...) conditional(s32[]{:T(128)} %convert_element_type.256, ...), branch_computations={%region_17.17_spmd, %region_18.19_spmd.clone} | conditional | flops 1707164416 | bytes 66894076 | solution.py:334
  607.2 5.1 convolution_add_fusion.3
  619.2 7.5 collective-permute-done
  626.7 21.5 %conditional.13 = (bf16[512,256]{1,0:T(8,128)(2,1)}, bf16[512,1024]{1,0:T(8,128)(2,1)}, bf16[80,1024]{1,0:T(8,128)(2,1)}, f32[1024,1024]{1,0:T(8,128)}, f32[1024...) conditional(s32[]{:T(128)} %convert_element_type.256, ...), branch_computations={%region_17.17_spmd, %region_18.19_spmd.clone} | conditional | flops 1707164416 | bytes 66894076 | solution.py:334
  637.6 5.1 convolution_add_fusion.3
  649.5 7.5 collective-permute-done
  657.0 21.5 %conditional.13 = (bf16[512,256]{1,0:T(8,128)(2,1)}, bf16[512,1024]{1,0:T(8,128)(2,1)}, bf16[80,1024]{1,0:T(8,128)(2,1)}, f32[1024,1024]{1,0:T(8,128)}, f32[1024...) conditional(s32[]{:T(128)} %convert_element_type.256, ...), branch_computations={%region_17.17_spmd, %region_18.19_spmd.clone} | conditional | flops 1707164416 | bytes 66894076 | solution.py:334
  667.9 5.1 convolution_add_fusion.3
  679.8 2.3 collective-permute-done
  684.3 3.8 convert_bitcast_fusion
  695.5 41.5 %all-reduce.17.cloned.1.call-done = bf16[80,4,256]{0,1,2:T(4,128)(2,1)} async-done(((bf16[80,4,256]{0,1,2:T(4,128)(2,1)}), bf16[80,4,256]{0,1,2:T(4,128)(2,1)}) %all-reduce.17.cloned.1.call-update) | async-done | bytes 163856
  738.2 2.3 copy.87
  740.5 3.6 broadcast_in_dim.219
  744.1 16.6 %dynamic_update_slice.30 = f32[256,80,80]{0,2,1:T(8,128)} dynamic-update-slice(f32[256,80,80]{0,2,1:T(8,128)} %broadcast_in_dim.219, f32[32,80,80]{0,2,1:T(8,128)} %copy.87, s32[]{:T(128)S(6)} %select_n.174, s32[]{:T(128)} %constant.269.clone.1, s32[]{:T(128)} %constant.269.clone.1) | dynamic-update-slice | bytes 1638404 | tf_op jit(solution)/shard_map/dynamic_update_slice | solution.py:367
  760.9 12.5 %psum.89 = bf16[1,1024]{1,0:T(2,128)(2,1)S(1)} all-reduce(bf16[1,1024]{1,0:T(2,128)(2,1)S(1)} %broadcast_in_dim.213), channel_id=1, replica_groups=mesh['section'=8,'dp'=4] {'dp'}, use_global_device_ids=true, to_apply=%region_24.25 | all-reduce | flops 1024 | bytes 4096 | tf_op jit(solution)/shard_map/psum | solution.py:351
  774.5 46.6 %all-reduce.4 = (f32[]{:T(128)}, f32[80,109]{1,0:T(8,128)}) all-reduce(f32[]{:T(128)} %get-tuple-element.1426, f32[80,109]{1,0:T(8,128)S(1)} %fusion.81), channel_id=1, replica_groups=mesh['section'=8,'dp'=4] {'section','dp'}, use_global_device_ids=true, to_apply=%region_14.15 | all-reduce | flops 8721 | bytes 69768 | tf_op jit(solution)/shard_map/psum | solution.py:373
  821.0 46.7 %all-reduce.21.cloned.1.call-done = (bf16[1,1024,1024]{2,1,0:T(8,128)(2,1)}, bf16[1,1024,80]{1,2,0:T(8,128)(2,1)}, bf16[1,512,512]{2,1,0:T(8,128)(2,1)}, bf16[1,512,512]{2,1,0:T(8,128)(2,1)}) async-done(((bf16[1,1024,1024]{2,1,0:T(8,128)(2,1)}, bf16[1,1024,80]{1,2,0:T(8,128)(2,1)}, bf16[1,512,512]{2,1,0:T(8,128)(2,1)}, bf16[1,512,512]{2,1,0:T(8,128)(2,1)}), (bf16[1,1024,1024]{2,1,0:T(8,128)(2,1)}, ...) | async-done | bytes 3309584 | tf_op jit(solution)/shard_map/psum | solution.py:349
  867.7 4.2 broadcast_in_dim.210
  874.9 32.1 %reduce-scatter.2.cloned.1.call-done = bf16[64,1024]{1,0:T(8,128)(2,1)} async-done(((bf16[512,1024]{1,0:T(8,128)(2,1)}), bf16[64,1024]{1,0:T(8,128)(2,1)}) %reduce-scatter.2.cloned.1.call-update) | async-done | bytes 131088 | tf_op jit(solution)/shard_map/reduce_scatter | solution.py:345
  906.9 183.7 %all-reduce.19.cloned.1.call-done = (f32[256,80,80]{0,2,1:T(8,128)}, f32[512,512]{1,0:T(8,128)}, f32[256,512]{1,0:T(8,128)}) async-done(((f32[256,80,80]{0,2,1:T(8,128)}, f32[512,512]{1,0:T(8,128)}, f32[256,512]{1,0:T(8,128)}), (f32[256,80,80]{0,2,1:T(8,128)}, f32[512,512]{1,0:T(8,128)}, f32[256,512]{1,0:T(8,128)})) %all-reduce.19.cloned.1.call-update) | async-done | bytes 8126480 | tf_op jit(solution)/shard_map/psum | solution.py:373
  1090.6 6.2 copy.213
  (442 shorter events, 205.4 us)
Async XLA Ops:
  7.2 6.1 copy-start.20
  7.2 59.2 %all-reduce.13.cloned.1.call-start = ((), (), s32[]{:S(2)}) async-start(), calls=%async_computation.1 | async-start | bytes 327680 | tf_op jit(solution)/shard_map/psum | solution.py:15
  9.0 6.5 copy-start.28
  9.0 6.5 copy-start.29
  9.0 7.1 copy-start.32
  13.3 360.0 %all-reduce.15.cloned.1.call-start = ((), (), s32[]{:S(2)}) async-start(), calls=%async_computation.2 | async-start | bytes 2097152 | tf_op jit(solution)/shard_map/psum | solution.py:15
  67.1 6.7 copy-start
  67.1 6.7 copy-start.1
  83.7 4.0 collective-permute-start.2
  85.0 2.7 collective-permute-start.1
  98.3 7.2 collective-permute-start.2
  102.2 3.2 collective-permute-start.1
  116.1 13.6 %collective-permute-start.2 = (f32[512,256]{0,1:T(8,128)}, f32[512,256]{0,1:T(8,128)S(1)}, u32[]{:S(2)}, u32[]{:S(2)}) collective-permute-start(f32[512,256]{0,1:T(8,128)} %get-tuple-element.2396), channel_id=1, source_target_pairs={{0,4},{4,8},{8,12},{12,16},{16,20},{20,24},{24,28},{1,5},{5,9},{9,... | collective-permute-start | bytes 1572872 | tf_op jit(solution)/shard_map/while/body/eval_jaxpr/ppermute | solution.py:21
  124.1 5.6 collective-permute-start.1
  140.3 13.6 %collective-permute-start.2 = (f32[512,256]{0,1:T(8,128)}, f32[512,256]{0,1:T(8,128)S(1)}, u32[]{:S(2)}, u32[]{:S(2)}) collective-permute-start(f32[512,256]{0,1:T(8,128)} %get-tuple-element.2396), channel_id=1, source_target_pairs={{0,4},{4,8},{8,12},{12,16},{16,20},{20,24},{24,28},{1,5},{5,9},{9,... | collective-permute-start | bytes 1572872 | tf_op jit(solution)/shard_map/while/body/eval_jaxpr/ppermute | solution.py:21
  148.3 5.6 collective-permute-start.1
  157.0 21.1 %collective-permute-start.2 = (f32[512,256]{0,1:T(8,128)}, f32[512,256]{0,1:T(8,128)S(1)}, u32[]{:S(2)}, u32[]{:S(2)}) collective-permute-start(f32[512,256]{0,1:T(8,128)} %get-tuple-element.2396), channel_id=1, source_target_pairs={{0,4},{4,8},{8,12},{12,16},{16,20},{20,24},{24,28},{1,5},{5,9},{9,... | collective-permute-start | bytes 1572872 | tf_op jit(solution)/shard_map/while/body/eval_jaxpr/ppermute | solution.py:21
  172.5 5.6 collective-permute-start.1
  181.2 21.1 %collective-permute-start.2 = (f32[512,256]{0,1:T(8,128)}, f32[512,256]{0,1:T(8,128)S(1)}, u32[]{:S(2)}, u32[]{:S(2)}) collective-permute-start(f32[512,256]{0,1:T(8,128)} %get-tuple-element.2396), channel_id=1, source_target_pairs={{0,4},{4,8},{8,12},{12,16},{16,20},{20,24},{24,28},{1,5},{5,9},{9,... | collective-permute-start | bytes 1572872 | tf_op jit(solution)/shard_map/while/body/eval_jaxpr/ppermute | solution.py:21
  189.1 13.2 %collective-permute-start.1 = (bf16[512,256]{0,1:T(8,128)(2,1)}, bf16[512,256]{0,1:T(8,128)(2,1)S(1)}, u32[]{:S(2)}, u32[]{:S(2)}) collective-permute-start(bf16[512,256]{0,1:T(8,128)(2,1)} %get-tuple-element.2395), channel_id=1, source_target_pairs={{0,4},{4,8},{8,12},{12,16},{16,20},{20,24},{24,28},{1,5},{5,9},{9,... | collective-permute-start | bytes 786440 | tf_op jit(solution)/shard_map/while/body/eval_jaxpr/ppermute | solution.py:21
  205.4 13.5 %collective-permute-start.2 = (f32[512,256]{0,1:T(8,128)}, f32[512,256]{0,1:T(8,128)S(1)}, u32[]{:S(2)}, u32[]{:S(2)}) collective-permute-start(f32[512,256]{0,1:T(8,128)} %get-tuple-element.2396), channel_id=1, source_target_pairs={{0,4},{4,8},{8,12},{12,16},{16,20},{20,24},{24,28},{1,5},{5,9},{9,... | collective-permute-start | bytes 1572872 | tf_op jit(solution)/shard_map/while/body/eval_jaxpr/ppermute | solution.py:21
  213.3 5.6 collective-permute-start.1
  222.0 13.5 %collective-permute-start.2 = (f32[512,256]{0,1:T(8,128)}, f32[512,256]{0,1:T(8,128)S(1)}, u32[]{:S(2)}, u32[]{:S(2)}) collective-permute-start(f32[512,256]{0,1:T(8,128)} %get-tuple-element.2396), channel_id=1, source_target_pairs={{0,4},{4,8},{8,12},{12,16},{16,20},{20,24},{24,28},{1,5},{5,9},{9,... | collective-permute-start | bytes 1572872 | tf_op jit(solution)/shard_map/while/body/eval_jaxpr/ppermute | solution.py:21
  229.9 5.6 collective-permute-start.1
  238.6 16.0 %collective-permute-start.2 = (f32[512,256]{0,1:T(8,128)}, f32[512,256]{0,1:T(8,128)S(1)}, u32[]{:S(2)}, u32[]{:S(2)}) collective-permute-start(f32[512,256]{0,1:T(8,128)} %get-tuple-element.2396), channel_id=1, source_target_pairs={{0,4},{4,8},{8,12},{12,16},{16,20},{20,24},{24,28},{1,5},{5,9},{9,... | collective-permute-start | bytes 1572872 | tf_op jit(solution)/shard_map/while/body/eval_jaxpr/ppermute | solution.py:21
  246.5 8.1 collective-permute-start.1
  257.7 15.8 %collective-permute-start.2 = (f32[512,256]{0,1:T(8,128)}, f32[512,256]{0,1:T(8,128)S(1)}, u32[]{:S(2)}, u32[]{:S(2)}) collective-permute-start(f32[512,256]{0,1:T(8,128)} %get-tuple-element.2396), channel_id=1, source_target_pairs={{0,4},{4,8},{8,12},{12,16},{16,20},{20,24},{24,28},{1,5},{5,9},{9,... | collective-permute-start | bytes 1572872 | tf_op jit(solution)/shard_map/while/body/eval_jaxpr/ppermute | solution.py:21
  267.8 5.6 collective-permute-start.1
  276.6 14.4 %collective-permute-start.2 = (f32[512,256]{0,1:T(8,128)}, f32[512,256]{0,1:T(8,128)S(1)}, u32[]{:S(2)}, u32[]{:S(2)}) collective-permute-start(f32[512,256]{0,1:T(8,128)} %get-tuple-element.2396), channel_id=1, source_target_pairs={{0,4},{4,8},{8,12},{12,16},{16,20},{20,24},{24,28},{1,5},{5,9},{9,... | collective-permute-start | bytes 1572872 | tf_op jit(solution)/shard_map/while/body/eval_jaxpr/ppermute | solution.py:21
  285.3 5.6 collective-permute-start.1
  292.7 444.3 %all-reduce.17.cloned.1.call-start = ((), (), s32[]{:S(2)}) async-start(), calls=%async_computation.4 | async-start | bytes 524288
  383.6 3.6 collective-permute-start
  387.9 6.3 collective-permute-start
  395.0 7.9 collective-permute-start
  403.6 7.9 collective-permute-start
  412.2 7.9 collective-permute-start
  420.8 7.9 collective-permute-start
  429.4 136.6 %collective-permute-start = (bf16[512,256]{1,0:T(8,128)(2,1)}, bf16[512,256]{1,0:T(8,128)(2,1)S(1)}, u32[]{:S(2)}, u32[]{:S(2)}) collective-permute-start(bf16[512,256]{1,0:T(8,128)(2,1)} %get-tuple-element.2359), channel_id=1, source_target_pairs={{4,0},{8,4},{12,8},{16,12},{20,16},{24,20},{28,24},{5,1},{9,5},{13... | collective-permute-start | bytes 786440 | tf_op jit(solution)/shard_map/while/body/eval_jaxpr/ppermute | solution.py:21
  566.1 6.5 copy-start.5
  576.9 7.5 copy-start.6
  576.9 7.5 copy-start.7
  576.9 7.5 copy-start.14
  587.6 8.8 collective-permute-start
  596.4 6.5 copy-start.5
  607.2 7.5 copy-start.6
  607.2 7.5 copy-start.7
  607.2 7.5 copy-start.14
  617.9 8.8 collective-permute-start
  626.7 6.5 copy-start.5
  637.5 7.5 copy-start.6
  637.5 7.5 copy-start.7
  637.5 7.5 copy-start.14
  648.2 8.8 collective-permute-start
  657.0 6.5 copy-start.5
  667.8 7.5 copy-start.6
  667.8 7.5 copy-start.7
  667.9 7.5 copy-start.14
  678.5 3.6 collective-permute-start
  684.2 183.5 %all-reduce.21.cloned.1.call-start = ((), (), s32[]{:S(2)}) async-start(), calls=%async_computation.6 | async-start | bytes 6619136 | tf_op jit(solution)/shard_map/psum | solution.py:349
  690.7 47.1 %copy-start.30 = (bf16[80,4]{0,1:T(4,128)(2,1)S(1)}, bf16[80,4]{0,1:T(4,128)(2,1)}, u32[]{:S(2)}) copy-start(bf16[80,4]{0,1:T(4,128)(2,1)} %param.30) | copy-start | bytes 1924
  692.9 214.0 %reduce-scatter.2.cloned.1.call-start = ((), (), s32[]{:S(2)}) async-start(), calls=%async_computation.3 | async-start | bytes 1179648 | tf_op jit(solution)/shard_map/reduce_scatter | solution.py:345
  694.2 396.4 %all-reduce.19.cloned.1.call-start = ((), (), s32[]{:S(2)}) async-start(), calls=%async_computation.5 | async-start | bytes 16252928 | tf_op jit(solution)/shard_map/psum | solution.py:373
  1090.6 6.2 copy-start.21
  1090.6 7.2 copy-start.24
  (43 other events, 107.9 us)
Sparse Core Ops, SparseCore 0:
  13.4 52.9 all-reduce.12
  292.9 80.3 all-reduce.14
  684.3 52.6 all-reduce.16
  740.2 127.4 all-reduce.20
  871.9 35.0 reduce-scatter.1
  914.0 176.4 all-reduce.18
where the time goes:
time: 1110 us
  waiting for transfers between devices  634 us (57%)
  starting transfers between devices  153 us (14%)
  local copies, waits for them, and re-layouts  107 us (10%)
  matrix products  78 us (7%)
  blocking collectives  59.1 us (5%)
  other arithmetic  37.7 us (3%)
  loops' own time  19.9 us (2%)
  between operations  15.6 us (1%)
    ppermute x33, waiting for transfers between devices, shifted_2(): lax.ppermute(value, axis, [(source, source + steps) for source in range(l...  208 us
    psum x1, waiting for transfers between devices, local(): lax.psum((grad_up, grad_table, grad_postw, grad_outw, loss_sum), ('sectio...  184 us
    ppermute x33, starting transfers between devices, shifted_2(): lax.ppermute(value, axis, [(source, source + steps) for source in range(l...  153 us
    psum x2, waiting for transfers between devices, broadcast(): return lax.psum(block, axis)  122 us
    psum x1, waiting for transfers between devices, local(): lax.psum(accumulators[0].astype(jnp.bfloat16), 'dp').astype(jnp.float32)  46.7 us
    psum x1, blocking collectives, local(): lax.psum((grad_up, grad_table, grad_postw, grad_outw, loss_sum), ('sectio...  46.6 us
    unnamed x7, waiting for transfers between devices  41.6 us
    dot_general x16, matrix products, outer_product(): lax.dot_general(left, right, (((1,), (1,)), ((), ())), preferred_element_...  37.6 us
  transfers between devices with their start and end apart: 39, of which 28 were waited for; matrix products, arithmetic and copies ran while one was open for 5% of the time, Pallas kernels for 0%

commit v1 on v0

v1 whole, which is shorter than its diff:
```python
import functools
import math

import jax
import jax.numpy as jnp
from jax import lax
from jax.experimental import pallas as pl
from jax.experimental.pallas import tpu as pltpu
from jax.sharding import PartitionSpec as P

HALF_ROOT = 0.7071067811865476
WEIGHT_SCALE = 64.0
MESH = pl.DeviceIdType.MESH
BF16 = jnp.bfloat16
F32 = jnp.float32

PIECE = 128
EXT = 96
WIDE = 1024
BLOCK = 48
LAG = 3
HEAD_AT = 8


def dot(left, right):
    return jnp.dot(left, right, preferred_element_type=F32)


def dot_nt(left, right):
    return lax.dot_general(left, right, (((1,), (1,)), ((), ())), preferred_element_type=F32)


def sigmoid(values):
    return 0.5 * jnp.tanh(0.5 * values) + 0.5


def step_kernel(
    dims,
    dil_ref,
    offs_ref,
    spk_ref,
    cnt_ref,
    inp_ref,
    tgt_ref,
    cond_ref,
    extra_ref,
    wd_ref,
    wc_ref,
    wr_ref,
    ws_ref,
    wp_ref,
    wk_ref,
    o_acc,
    o_g,
    o_gin,
    x_buf,
    sg_buf,
    gx_buf,
    gc_buf,
    hid_buf,
    d1_buf,
    d2_buf,
    x_out,
    k_out,
    gx_out,
    gc_out,
    gate_buf,
    gh_buf,
    gg_buf,
    shift_buf,
    wc_n,
    wd_t,
    wr_t,
    ws_t,
    wp_t,
    wk_t,
    gl_buf,
    a2_buf,
    gp_buf,
    a1_buf,
    acc,
    part_out,
    part_in,
    gin_buf,
    inp_sem,
    loc_sem,
    x_ss,
    x_rs,
    k_ss,
    k_rs,
    gs_ss,
    gs_rs,
    gx_ss,
    gx_rs,
    gc_ss,
    gc_rs,
    zi_ss,
    zo_ss,
    zp_rs,
    zt_rs,
    hd_ss,
    hd_rs,
    g_rs,
    gown_ss,
    gpeer_ss,
    gup_ss,
    gdn_ss,
    gin_ss,
    gin_rs,
):
    sections, groups, micro, res, half, classes, slots, mel_rows = dims
    pieces = 2 * micro
    s = lax.axis_index("section")
    z = lax.axis_index("dp")
    is_first = s == 0
    is_last = s == sections - 1
    head_scale = 1.0 / math.sqrt(sections)
    main_rows = 2 * half + EXT + half
    head_rows = half // 2 + classes // 2
    main_blocks = main_rows // BLOCK
    head_blocks = head_rows // BLOCK
    share = res // sections

    barrier = pltpu.get_barrier_semaphore()

    def greet(cond, dev_s, dev_z):
        @pl.when(cond)
        def _():
            pl.semaphore_signal(barrier, 1, device_id=(dev_s, dev_z), device_id_type=MESH)

    greet(s > 0, s - 1, z)
    greet(s < sections - 1, s + 1, z)
    greet(z > 0, s, z - 1)
    greet(z < groups - 1, s, z + 1)
    greet(s >= 2, 0, z)

    @pl.when(is_first)
    def _():
        @pl.loop(2, sections)
        def _(other):
            pl.semaphore_signal(barrier, 1, device_id=(other, z), device_id_type=MESH)

    @pl.when(s == 2)
    def _():
        for other in range(groups):
            greet((other > z + 1) | (other < z - 1), s, other)

    def flag(cond):
        return jnp.where(cond, 1, 0)

    z_near = flag(z > 0) + flag(z < groups - 1)
    expected = (
        flag(s > 0)
        + flag(s < sections - 1)
        + z_near
        + jnp.where(is_first, sections - 2, flag(s >= 2))
        + jnp.where(s == 2, groups - 1 - z_near, 0)
    )

    def input_copy(c):
        return pltpu.make_async_copy(
            inp_ref.at[:, pl.ds(pl.multiple_of(c * PIECE, PIECE), PIECE)],
            x_buf.at[c],
            inp_sem.at[c],
        )

    @pl.when(is_first)
    def _():
        @pl.loop(0, pieces)
        def _(c):
            input_copy(c).start()

    wc_n[...] = jnp.transpose(wc_ref[...])

    def prepare():
        wd_t[...] = jnp.transpose(wd_ref[...])
        wr_t[...] = jnp.transpose(wr_ref[...])
        ws_t[...] = jnp.transpose(ws_ref[...])
        acc[...] = jnp.zeros_like(acc)

    pl.semaphore_wait(barrier, expected)

    @pl.when(s > 0)
    def _():
        prepare()

    @pl.when(is_last)
    def _():
        wp_t[...] = jnp.transpose(wp_ref[...])
        wk_t[...] = jnp.transpose(wk_ref[...])
        gx_buf[...] = jnp.zeros_like(gx_buf)

    def remote(src, dst, send_sem, recv_sem, dev_s, dev_z):
        return pltpu.make_async_remote_copy(
            src_ref=src,
            dst_ref=dst,
            send_sem=send_sem,
            recv_sem=recv_sem,
            device_id=(dev_s, dev_z),
            device_id_type=MESH,
        )

    def x_copy(c):
        slot = lax.rem(c, slots)
        return remote(x_out.at[slot], x_buf.at[c], x_ss.at[slot], x_rs.at[c], s + 1, z)

    def k_copy(c):
        slot = lax.rem(c, slots)
        return remote(k_out.at[slot], sg_buf.at[c], k_ss.at[slot], k_rs.at[c], s + 1, z)

    def gs_copy(c):
        return remote(sg_buf.at[c], sg_buf.at[c], gs_ss.at[c], gs_rs.at[c], s - 1, z)

    def gx_copy(c):
        slot = lax.rem(c, slots)
        return remote(gx_out.at[slot], gx_buf.at[c], gx_ss.at[slot], gx_rs.at[c], s - 1, z)

    def gc_copy(c):
        slot = lax.rem(c, slots)
        return remote(gc_out.at[slot], gc_buf.at[c], gc_ss.at[slot], gc_rs.at[c], s - 1, z)

    def reuse(copy, c):
        if pieces > slots:

            @pl.when(c >= slots)
            def _():
                copy(c).wait_send()

    def build_shift(m):
        dilation = dil_ref[0]
        middle = offs_ref[m, 0]
        source = lax.broadcasted_iota(jnp.int32, (2 * PIECE, 2 * PIECE), 0)
        target = lax.broadcasted_iota(jnp.int32, (2 * PIECE, 2 * PIECE), 1)
        start = jnp.where(target >= middle, middle, 0)
        hit = (source == target - dilation) & (source >= start)
        shift_buf[...] = jnp.where(hit, 1.0, 0.0).astype(BF16)

    def head(m, h, total):
        c = 2 * m + h
        total = total.astype(BF16).astype(F32) * head_scale
        sig_1 = sigmoid(total)
        act_1 = (total * sig_1).astype(BF16)
        slope_1 = sig_1 * (1.0 + total * (1.0 - sig_1))
        post = dot(wp_ref[...], act_1)
        sig_2 = sigmoid(post)
        act_2 = (post * sig_2).astype(BF16)
        slope_2 = sig_2 * (1.0 + post * (1.0 - sig_2))
        logits = dot(wk_ref[...], act_2)
        top = jnp.max(logits, axis=0, keepdims=True)
        expo = jnp.exp(logits - top)
        denominator = jnp.sum(expo, axis=0, keepdims=True)
        hit = tgt_ref[c] == lax.broadcasted_iota(jnp.int32, (classes, PIECE), 0)
        picked = jnp.sum(jnp.where(hit, logits, 0.0), axis=0, keepdims=True)
        time = lax.broadcasted_iota(jnp.int32, (1, PIECE), 1) + h * PIECE

        def speaker_weight(which):
            count = cnt_ref[spk_ref[m, which]].astype(F32)
            return WEIGHT_SCALE * lax.rsqrt(jnp.full((1, PIECE), count, F32))

        weight = jnp.where(time >= offs_ref[m, 0], speaker_weight(1), speaker_weight(0))
        weight = jnp.where(time < offs_ref[m, 1], weight, 0.0)
        loss_row = weight * (top + jnp.log(denominator) - picked)
        grad_logits = (weight * (expo / denominator - jnp.where(hit, 1.0, 0.0))).astype(BF16)
        grad_post = (dot(wk_t[...], grad_logits) * slope_2).astype(BF16)
        grad_total = dot(wp_t[...], grad_post) * slope_1 * head_scale
        sg_buf[c] = grad_total.astype(BF16)
        gs_copy(c).start()
        gl_buf[h] = grad_logits
        a2_buf[h] = act_2
        gp_buf[h] = grad_post
        a1_buf[h] = act_1
        high = loss_row.astype(BF16)
        rest = loss_row - high.astype(F32)
        middle = rest.astype(BF16)
        low = (rest - middle.astype(F32)).astype(BF16)
        row = lax.broadcasted_iota(jnp.int32, (EXT, PIECE), 0)
        message = jnp.where(row == mel_rows + 2, high.astype(F32), 0.0)
        message = jnp.where(row == mel_rows + 3, middle.astype(F32), message)
        message = jnp.where(row == mel_rows + 4, low.astype(F32), message)
        gc_buf[c] = message.astype(BF16)

    def forward(m, h):
        c = 2 * m + h

        @pl.when(is_first)
        def _():
            input_copy(c).wait()

        @pl.when(s > 0)
        def _():
            x_copy(c).wait_recv()

        x = x_buf[c]
        if h == 0:
            prev = dot(x, shift_buf[0:PIECE, 0:PIECE])
        else:
            both = jnp.concatenate([x_buf[2 * m], x], axis=1)
            prev = dot(both, shift_buf[:, PIECE : 2 * PIECE])
        stack = jnp.concatenate([prev.astype(BF16), x], axis=0)
        gate_buf[...] = dot(wd_ref[...], stack) + dot(wc_n[...], cond_ref[c])
        th = jnp.tanh(gate_buf[0:half])
        sg = sigmoid(gate_buf[half : 2 * half])
        hidden = (th * sg).astype(BF16)
        hid_buf[c] = hidden

        @pl.when(s < sections - 1)
        def _():
            reuse(x_copy, c)
            out = (x_buf[c].astype(F32) + dot(wr_ref[...], hid_buf[c])) * HALF_ROOT
            x_out[lax.rem(c, slots)] = out.astype(BF16)
            x_copy(c).start()

        gh_buf[...] = dot(ws_ref[...], hid_buf[c])
        th = jnp.tanh(gate_buf[0:half])
        sg = sigmoid(gate_buf[half : 2 * half])
        d1_buf[c] = (sg * (1.0 - th * th)).astype(BF16)
        d2_buf[c] = (th * sg * (1.0 - sg)).astype(BF16)

        @pl.when(s > 0)
        def _():
            k_copy(c).wait_recv()
            gh_buf[...] += sg_buf[c].astype(F32)

        @pl.when(s < sections - 1)
        def _():
            reuse(k_copy, c)
            k_out[lax.rem(c, slots)] = gh_buf[...].astype(BF16)
            k_copy(c).start()

        @pl.when(is_last)
        def _():
            head(m, h, gh_buf[...])

    def backward(m, h):
        c = 2 * m + h

        @pl.when(s < sections - 1)
        def _():
            gs_copy(c).wait_recv()

            @pl.when(s > 0)
            def _():
                gs_copy(c).start()

        gh_buf[...] = dot(ws_t[...], sg_buf[c])

        @pl.when(s < sections - 1)
        def _():
            gx_copy(c).wait_recv()
            gh_buf[...] += HALF_ROOT * dot(wr_t[...], gx_buf[c])

        grad_hidden = gh_buf[...]
        grad_gate = jnp.concatenate(
            [grad_hidden * d1_buf[c].astype(F32), grad_hidden * d2_buf[c].astype(F32)], axis=0
        ).astype(BF16)
        gg_buf[h] = grad_gate
        if h == 1:
            back = dot_nt(grad_gate, shift_buf[PIECE:, PIECE:])
        else:
            both = jnp.concatenate([grad_gate, gg_buf[1]], axis=1)
            back = dot_nt(both, shift_buf[0:PIECE, :])
        grad_x = (
            HALF_ROOT * gx_buf[c].astype(F32)
            + dot(wd_t[res : 2 * res], grad_gate)
            + dot(wd_t[0:res], back.astype(BF16))
        ).astype(BF16)

        @pl.when(s > 0)
        def _():
            reuse(gx_copy, c)
            gx_out[lax.rem(c, slots)] = grad_x
            gx_copy(c).start()

        row = lax.broadcasted_iota(jnp.int32, (EXT, PIECE), 0)
        message = jnp.where(row < mel_rows, dot(wc_ref[...], gg_buf[h]), 0.0)

        @pl.when(s < sections - 1)
        def _():
            gc_copy(c).wait_recv()

        message = message + gc_buf[c].astype(F32)

        @pl.when(s > 0)
        def _():
            reuse(gc_copy, c)
            gc_out[lax.rem(c, slots)] = message.astype(BF16)
            gc_copy(c).start()

        @pl.when(is_first)
        def _():
            d1_buf[c] = grad_x
            gc_buf[c] = message.astype(BF16)
            if h == 0:
                gc_buf[c, mel_rows:EXT, :] = (message[mel_rows:EXT] + extra_ref[m].astype(F32)).astype(BF16)

    def add_halves(first_row, value):
        rows = value.shape[0] // 2
        acc[first_row : first_row + rows, 0:half] += value[0:rows]
        acc[first_row : first_row + rows, half : 2 * half] += value[rows : 2 * rows]

    def weight_gradients(m):
        def pair(ref, first):
            return jnp.concatenate([ref[first], ref[first + 1]], axis=1)

        grad_gate = pair(gg_buf, 0)
        x = pair(x_buf, 2 * m)
        prev = dot(x, shift_buf[...]).astype(BF16)
        acc[0 : 2 * half, 0:res] += dot_nt(grad_gate, prev)
        acc[0 : 2 * half, res : 2 * res] += dot_nt(grad_gate, x)
        acc[2 * half : 2 * half + EXT, :] += dot_nt(pair(cond_ref, 2 * m), grad_gate)
        hidden = pair(hid_buf, 2 * m)
        row = 2 * half + EXT

        @pl.when(s < sections - 1)
        def _():
            add_halves(row, HALF_ROOT * dot_nt(pair(gx_buf, 2 * m), hidden))

        add_halves(row + half // 2, dot_nt(pair(sg_buf, 2 * m), hidden))

        @pl.when(is_last)
        def _():
            add_halves(main_rows, dot_nt(pair(gp_buf, 0), pair(a1_buf, 0)))
            add_halves(main_rows + half // 2, dot_nt(pair(gl_buf, 0), pair(a2_buf, 0)))

    @pl.loop(0, 2 * micro)
    def _(step):
        m = jnp.where(is_last, step // 2, lax.rem(step, micro))
        is_forward = jnp.where(is_last, lax.rem(step, 2) == 0, step < micro)
        build_shift(m)

        @pl.when(is_forward)
        def _():
            forward(m, 0)
            forward(m, 1)

        @pl.when(is_first & (step == micro))
        def _():
            prepare()

        @pl.when(jnp.logical_not(is_forward))
        def _():
            backward(m, 1)
            backward(m, 0)
            weight_gradients(m)

    def gin_copy(other):
        return remote(
            d1_buf.at[:, pl.ds(pl.multiple_of(other * share, share), share), :],
            gin_buf,
            gin_ss.at[other],
            gin_rs.at[0],
            other,
            z,
        )

    def own_local():
        return pltpu.make_async_copy(gc_buf, o_g.at[z], loc_sem.at[0])

    def own_first():
        return remote(gc_buf, o_g.at[z], gown_ss.at[0], g_rs.at[z], s + 1, z)

    def part_up(j):
        return remote(o_g.at[j], o_g.at[j], gup_ss.at[j], g_rs.at[j], s + 1, z)

    def part_down(j):
        return remote(o_g.at[j], o_g.at[j], gdn_ss.at[j], g_rs.at[j], s - 1, z)

    def own_peer(other):
        return remote(o_g.at[z], o_g.at[z], gpeer_ss.at[other], g_rs.at[z], s, other)

    @pl.when(is_first)
    def _():
        own_local().start()
        own_first().start()

        @pl.loop(1, sections)
        def _(other):
            gin_copy(other).start()

        gin_buf[...] = d1_buf[:, 0:share, :]

    left = z < groups // 2
    inward = jnp.where(left, z + 1, z - 1)
    outward = jnp.where(left, z - 1, z + 1)
    is_edge = (z == 0) | (z == groups - 1)
    is_mid = (z == groups // 2 - 1) | (z == groups // 2)
    count = jnp.where(is_last, main_blocks + head_blocks, main_blocks)

    def block_of(i):
        return jnp.where(is_last, jnp.where(i < head_blocks, i + main_blocks, i - head_blocks), i)

    def rows_of(b):
        return pl.ds(pl.multiple_of(b * BLOCK, BLOCK), BLOCK)

    def swap_copy(b):
        return remote(part_out.at[rows_of(b)], o_acc.at[rows_of(b)], zi_ss.at[b], zt_rs.at[b], s, inward)

    def part_copy(b):
        return remote(part_out.at[rows_of(b)], part_in.at[rows_of(b)], zi_ss.at[b], zp_rs.at[b], s, inward)

    def total_copy(b):
        return remote(o_acc.at[rows_of(b)], o_acc.at[rows_of(b)], zo_ss.at[b], zt_rs.at[b], s, outward)

    def head_copy(j):
        rows = rows_of(main_blocks + j)
        return remote(o_acc.at[rows], o_acc.at[rows], hd_ss.at[j], hd_rs.at[j], s - 1, z)

    def send_part(b):
        rows = rows_of(b)

        @pl.when(is_edge)
        def _():
            part_out[rows, :] = acc[rows, :].astype(BF16)

        @pl.when(jnp.logical_not(is_edge))
        def _():
            part_copy(b).wait_recv()
            part_out[rows, :] = (acc[rows, :] + part_in[rows, :].astype(F32)).astype(BF16)

        @pl.when(is_mid)
        def _():
            swap_copy(b).start()

        @pl.when(jnp.logical_not(is_mid))
        def _():
            part_copy(b).start()

    def finish_part(b):
        rows = rows_of(b)
        swap_copy(b).wait_recv()

        @pl.when(is_mid)
        def _():
            o_acc[rows, :] = (part_out[rows, :].astype(F32) + o_acc[rows, :].astype(F32)).astype(BF16)

        @pl.when(jnp.logical_not(is_edge))
        def _():
            total_copy(b).start()

    last_step = main_blocks + LAG - 1
    own_at = jnp.minimum(2 + 4 * s, last_step)
    rest_at = jnp.where(s >= 3, 16 + 3 * (s - 2), jnp.where(s == 2, 16, jnp.where(s == 1, 14, last_step)))
    rest_at = jnp.minimum(rest_at, last_step)

    @pl.loop(0, main_blocks + head_blocks + LAG)
    def _(i):
        @pl.when(i < count)
        def _():
            send_part(block_of(i))

        @pl.when((i >= LAG) & (i < count + LAG))
        def _():
            b = block_of(i - LAG)
            finish_part(b)

            @pl.when(b >= main_blocks)
            def _():
                head_copy(b - main_blocks).start()

        @pl.when(jnp.logical_not(is_last) & (i >= HEAD_AT) & (i < HEAD_AT + head_blocks))
        def _():
            j = i - HEAD_AT
            head_copy(j).wait_recv()

            @pl.when(s > 0)
            def _():
                head_copy(j).start()

        @pl.when((s > 0) & (i == own_at))
        def _():
            part_up(z).wait_recv()

            @pl.when(s < sections - 1)
            def _():
                part_up(z).start()

            @pl.when(s == 2)
            def _():
                for other in range(groups):

                    @pl.when(z != other)
                    def _():
                        own_peer(other).start()

        @pl.when(i == rest_at)
        def _():
            for j in range(groups):

                @pl.when(z != j)
                def _():
                    part_up(j).wait_recv()

                    @pl.when((s >= 2) & (s < sections - 1))
                    def _():
                        part_up(j).start()

                    @pl.when((s == 1) | (s == 2))
                    def _():
                        part_down(j).start()

    @pl.when(s > 0)
    def _():
        gin_copy(0).wait_recv()

    for c in range(pieces):
        o_gin[:, c * PIECE : (c + 1) * PIECE] = gin_buf[c]

    @pl.when(is_first)
    def _():
        own_local().wait()
        own_first().wait_send()

        @pl.loop(1, sections)
        def _(other):
            gin_copy(other).wait_send()

    @pl.when((s > 0) & (s < sections - 1))
    def _():
        part_up(z).wait_send()

    @pl.when(s == 2)
    def _():
        for other in range(groups):

            @pl.when(z != other)
            def _():
                own_peer(other).wait_send()

    for j in range(groups):

        @pl.when((z != j) & (s >= 2) & (s < sections - 1))
        def _():
            part_up(j).wait_send()

        @pl.when((z != j) & ((s == 1) | (s == 2)))
        def _():
            part_down(j).wait_send()

    @pl.when(s > 0)
    def _():
        @pl.loop(0, head_blocks)
        def _(j):
            head_copy(j).wait_send()

    @pl.loop(0, count)
    def _(b):
        part_copy(b).wait_send()

        @pl.when(jnp.logical_not(is_edge))
        def _():
            total_copy(b).wait_send()

    @pl.loop(0, slots)
    def _(c):
        @pl.when(s < sections - 1)
        def _():
            x_copy(c).wait_send()
            k_copy(c).wait_send()

        @pl.when(s > 0)
        def _():
            gx_copy(c).wait_send()
            gc_copy(c).wait_send()

    @pl.when(s > 0)
    def _():
        @pl.loop(0, pieces)
        def _(c):
            gs_copy(c).wait_send()


def run_step(dims, dilations, offsets, speakers, counts, inputs, targets, cond, extra, weights):
    sections, groups, micro, res, half, classes, slots, mel_rows = dims
    pieces = 2 * micro
    rows = 2 * half + EXT + half + half // 2 + classes // 2
    blocks = rows // BLOCK
    head_blocks = (half // 2 + classes // 2) // BLOCK
    share = res // sections
    smem = pl.BlockSpec(memory_space=pltpu.SMEM)
    vmem = pl.BlockSpec(memory_space=pltpu.VMEM)
    anywhere = pl.BlockSpec(memory_space=pl.ANY)
    dma = pltpu.SemaphoreType.DMA

    def tile(*shape, dtype=BF16):
        return pltpu.VMEM(shape, dtype)

    scratch = [
        tile(pieces, res, PIECE),
        tile(pieces, half, PIECE),
        tile(pieces, res, PIECE),
        tile(pieces, EXT, PIECE),
        tile(pieces, half, PIECE),
        tile(pieces, half, PIECE),
        tile(pieces, half, PIECE),
        tile(slots, res, PIECE),
        tile(slots, half, PIECE),
        tile(slots, res, PIECE),
        tile(slots, EXT, PIECE),
        tile(2 * half, PIECE, dtype=F32),
        tile(half, PIECE, dtype=F32),
        tile(2, 2 * half, PIECE),
        tile(2 * PIECE, 2 * PIECE),
        tile(2 * half, EXT),
        tile(2 * res, 2 * half),
        tile(half, res),
        tile(half, half),
        tile(half, half),
        tile(half, classes),
        tile(2, classes, PIECE),
        tile(2, half, PIECE),
        tile(2, half, PIECE),
        tile(2, half, PIECE),
        tile(rows, WIDE, dtype=F32),
        tile(rows, WIDE),
        tile(rows, WIDE),
        tile(pieces, share, PIECE),
        dma((pieces,)),
        dma((1,)),
        dma((slots,)),
        dma((pieces,)),
        dma((slots,)),
        dma((pieces,)),
        dma((pieces,)),
        dma((pieces,)),
        dma((slots,)),
        dma((pieces,)),
        dma((slots,)),
        dma((pieces,)),
        dma((blocks,)),
        dma((blocks,)),
        dma((blocks,)),
        dma((blocks,)),
        dma((head_blocks,)),
        dma((head_blocks,)),
        dma((groups,)),
        dma((1,)),
        dma((groups,)),
        dma((groups,)),
        dma((groups,)),
        dma((sections,)),
        dma((1,)),
    ]
    return pl.pallas_call(
        functools.partial(step_kernel, dims),
        out_shape=(
            jax.ShapeDtypeStruct((rows, WIDE), BF16),
            jax.ShapeDtypeStruct((groups, pieces, EXT, PIECE), BF16),
            jax.ShapeDtypeStruct((share, pieces * PIECE), BF16),
        ),
        in_specs=[smem] * 4 + [anywhere] + [vmem] * 9,
        out_specs=(vmem, anywhere, vmem),
        scratch_shapes=scratch,
        compiler_params=pltpu.CompilerParams(
            collective_id=0, has_side_effects=True, vmem_limit_bytes=63 * 2**20
        ),
        cost_estimate=pl.CostEstimate(flops=10**10, bytes_accessed=3 * 10**7, transcendentals=10**6),
        name="train_step",
    )(dilations, offsets, speakers, counts, inputs, targets, cond, extra, *weights)


def local(
    inputs,
    targets,
    mel,
    speakers,
    speaker_sample_counts,
    segment_offsets,
    dilations,
    dilated_kernel,
    conditioning_projection,
    dilated_gate_bias,
    residual_projection,
    skip_projection,
    upsample_weight,
    speaker_table,
    first_output_projection,
    class_projection,
):
    sections = lax.axis_size("section")
    groups = lax.axis_size("dp")
    micro = segment_offsets.shape[0]
    res, tokens = inputs.shape
    length = tokens // micro
    mel_rows = mel.shape[0]
    hop = upsample_weight.shape[0]
    half = residual_projection.shape[2]
    classes = class_projection.shape[0]
    pieces = 2 * micro
    assert length == 2 * PIECE and hop == length and mel_rows + 16 == EXT and 2 * half == WIDE

    speaker_index = jnp.arange(speaker_table.shape[1], dtype=jnp.int32)
    onehot = (speakers[:, :, None] == speaker_index).astype(BF16)
    table_columns = jnp.einsum("cn,mjn->mjc", speaker_table, onehot, preferred_element_type=F32)
    time = jnp.arange(length, dtype=jnp.int32)
    later = time[None, :] >= segment_offsets[:, 0:1]
    spk_part = jnp.where(
        later[:, None, :], table_columns[:, 1, :, None], table_columns[:, 0, :, None]
    )
    upsampled = jnp.einsum("kca,af->fck", upsample_weight, mel, preferred_element_type=F32)
    cond = (upsampled + spk_part).astype(BF16)
    cond = jnp.concatenate(
        [cond, jnp.ones((micro, 1, length), BF16), jnp.zeros((micro, EXT - mel_rows - 1, length), BF16)],
        axis=1,
    )
    cond = cond.reshape(micro, EXT, 2, PIECE).transpose(0, 2, 1, 3).reshape(pieces, EXT, PIECE)
    weight_cond = jnp.concatenate(
        [
            conditioning_projection[0].T,
            dilated_gate_bias,
            jnp.zeros((EXT - mel_rows - 1, 2 * half), BF16),
        ],
        axis=0,
    )
    ids = jnp.concatenate([speakers, segment_offsets], axis=1).astype(BF16)
    extra = jnp.stack(
        [
            jnp.pad(mel.T, ((0, 0), (0, PIECE - mel_rows))),
            jnp.pad(ids, ((0, 0), (0, PIECE - 4))),
        ],
        axis=1,
    )
    extra = jnp.pad(extra, ((0, 0), (0, 14), (0, 0)))

    slots = pieces if pieces <= 8 else 4
    dims = (sections, groups, micro, res, half, classes, slots, mel_rows)
    sums, shared, grad_inputs = run_step(
        dims,
        dilations,
        segment_offsets,
        speakers,
        speaker_sample_counts,
        inputs,
        targets.reshape(pieces, 1, PIECE),
        cond,
        extra,
        (
            dilated_kernel[0],
            weight_cond,
            residual_projection[0],
            skip_projection[0],
            first_output_projection,
            class_projection,
        ),
    )

    def halves(first, rows):
        block = sums[first : first + rows].astype(F32)
        return jnp.concatenate([block[:, :half], block[:, half:]], axis=0)

    row = 2 * half
    grad_dil = sums[:row].astype(F32)
    cond_block = sums[row : row + EXT].astype(F32)
    grad_cond = cond_block[:mel_rows].T
    grad_bias = cond_block[mel_rows]
    row += EXT
    grad_res = halves(row, half // 2)
    grad_skip = halves(row + half // 2, half // 2)
    grad_post = halves(row + half, half // 2)
    grad_out = halves(row + half + half // 2, classes // 2)

    frames = groups * micro
    shared = shared.reshape(frames, 2, EXT, PIECE)
    field = shared[:, :, :mel_rows]
    mel_all = shared[:, 0, mel_rows, :mel_rows]
    ids_all = shared[:, 0, mel_rows + 1, :4].astype(jnp.int32)
    loss = jnp.sum(shared[:, :, mel_rows + 2 : mel_rows + 5].astype(F32))
    field_3 = field.transpose(2, 0, 1, 3).reshape(mel_rows, frames, length)
    grad_up = jnp.einsum("cfk,fa->cak", field_3, mel_all, preferred_element_type=F32)
    grad_up = grad_up.transpose(2, 0, 1)
    later_all = time[None, :] >= ids_all[:, 2:3]
    seg_mask = jnp.stack([jnp.logical_not(later_all), later_all], axis=1).astype(BF16)
    seg_sums = jnp.einsum("cfk,fjk->cfj", field_3, seg_mask, preferred_element_type=F32)
    seg_hot = (ids_all[:, :2, None] == speaker_index).astype(F32)
    grad_table = jnp.einsum("cfj,fjn->cn", seg_sums, seg_hot, precision=lax.Precision.HIGHEST)
    return (
        loss,
        grad_inputs,
        grad_dil[None],
        grad_cond[None],
        grad_bias[None],
        grad_res[None],
        grad_skip[None],
        grad_up,
        grad_table,
        grad_post,
        grad_out,
    )


def solution(mesh):
    return jax.shard_map(
        local,
        mesh=mesh,
        in_specs=(
            P(None, "dp"),
            P("dp"),
            P(None, "dp"),
            P("dp", None),
            P(),
            P("dp", None),
            P("section"),
            P("section", None, None),
            P("section", None, None),
            P("section", None),
            P("section", None, None),
            P("section", None, None),
            P(),
            P(),
            P(),
            P(),
        ),
        out_specs=(
            P(),
            P("section", "dp"),
            P("section", None, None),
            P("section", None, None),
            P("section", None),
            P("section", None, None),
            P("section", None, None),
            P(),
            P(),
            P(),
            P(),
        ),
        check_vma=False,
    )
```

time: 1110 us -> 415 us (0.37)
  waiting for transfers between devices: 634 us -> 0 us
  Pallas kernels: 0 us -> 380 us
  starting transfers between devices: 153 us -> 0 us
  local copies, waits for them, and re-layouts: 107 us -> 11.3 us
  matrix products: 78 us -> 8.37 us
  blocking collectives: 59.1 us -> 0 us
  other arithmetic: 37.7 us -> 13.5 us
  loops' own time: 19.9 us -> 0 us
  between operations: 15.6 us -> 1.49 us
    pallas_call x0 -> x1, Pallas kernels: none -> 380 us  [run_step(): pl.pallas_call(functools.partial(step_kernel, dims), out_shape=(jax.Shape...]
    psum x4 -> x0, waiting for transfers between devices: 353 us -> none  [the longest x1 184 us: local(): lax.psum((grad_up, grad_table, grad_postw, grad_outw, loss_sum), ('sectio...]
    ppermute x33 -> x0, waiting for transfers between devices: 208 us -> none  [shifted_2(): lax.ppermute(value, axis, [(source, source + steps) for source in range(l...]
    ppermute x33 -> x0, starting transfers between devices: 153 us -> none  [shifted_2(): lax.ppermute(value, axis, [(source, source + steps) for source in range(l...]
    dot_general x54 -> x5, matrix products: 78 us -> 8.37 us  [the longest x1 3.83 us: local(): jnp.einsum('cfk,fa->cak', field_3, mel_all, preferred_element_type=F32)]
    psum x2 -> x0, blocking collectives: 59.1 us -> none  [the longest x1 46.6 us: local(): lax.psum((grad_up, grad_table, grad_postw, grad_outw, loss_sum), ('sectio...]
    unnamed x7 -> x0, waiting for transfers between devices: 41.6 us -> none
    reduce_scatter x1 -> x0, waiting for transfers between devices: 32.1 us -> none  [local(): lax.psum_scatter(input_term.astype(jnp.bfloat16), 'section', scatter_dime...]
  transfers between devices with their start and end apart: 39 -> 0, of which waited for: 28 -> 0; matrix products, arithmetic and copies ran while one was open for 5% -> 0% of each run, Pallas kernels for 0% -> 0%
where the time goes in v1:
time: 415 us; the launch traced here: 414 us
  Pallas kernels  380 us (92%)
  other arithmetic  13.5 us (3%)
  local copies, waits for them, and re-layouts  11.3 us (3%)
  matrix products  8.37 us (2%)
    pallas_call x1, Pallas kernels, run_step(): pl.pallas_call(functools.partial(step_kernel, dims), out_shape=(jax.Shape...  380 us

profile of v1, /device:TPU:0, one launch (start us, length us, event | category | flops | bytes accessed | tf_op | source)
XLA Modules:
  0.0 414.4 jit_solution(12307024222186507583)
XLA Ops:
  0.6 0.0 copy-start
  0.7 0.0 copy-start.4
  0.7 0.0 copy-start.2
  1.4 0.7 convert.8
  2.0 0.7 slice_bitcast_fusion.5
  2.7 0.1 iota_compare_fusion.6
  2.8 0.7 convert.9
  3.5 0.1 pad.35.clone
  3.6 0.1 pad.36.clone
  3.6 0.7 pad_bitcast_fusion
  4.3 1.3 copy.44.spk_ref
  5.7 1.3 copy.43.offs_ref
  7.0 0.0 copy-done
  7.0 0.9 fusion.13
  7.9 0.1 copy.42
  8.0 0.6 fusion.15.extra_ref
  8.6 0.1 copy.37
  8.7 0.1 copy.38
  8.8 2.5 fusion.1
  11.3 0.3 maximum_maximum_fusion
  11.6 0.1 fusion.27
  11.7 0.1 pad_maximum_fusion.2
  11.8 0.7 copy.39
  12.5 0.0 copy-done.4
  12.5 0.0 copy-done.2
  12.5 0.8 maximum_maximum_fusion.1.wc_ref
  13.3 379.7 %train_step.1 = (bf16[2016,1024]{1,0:T(8,128)(2,1)}, bf16[4,8,96,128]{3,2,1,0:T(8,128)(2,1)}, bf16[64,1024]{1,0:T(8,128)(2,1)}) custom-call(s32[1]{0:T(128)S(6)} %copy.63.dil_ref, s32[4,2]{1,0:T(4,128)} %copy.43.offs_ref, s32[4,2]{1,0:T(4,128)} %copy.44.spk_ref, s32[109]{0:T(128)} %cnt_ref.1, bf16[512,1024]{1,0:T(8,128)(2,1)} %inp_ref.1, ...), custom_call_target="tpu_custom_call" | custom-call | flops 10000000000 | bytes 30000000 | tf_op jit(solution)/shard_map/train_step/pallas_call | solution.py:743
  393.0 1.5 convert_reduce_fusion
  394.5 0.8 slice.124
  395.3 0.1 copy.53
  395.4 0.8 slice.122
  396.1 1.1 slice_bitcast_fusion
  397.3 0.5 copy.46
  397.8 0.4 reshape.125
  398.2 0.0 copy-start.1
  398.2 0.1 fusion.22
  398.3 0.3 fusion.2
  398.7 0.9 convolution_bitcast_fusion.2
  399.5 1.0 slice_convert_fusion.4
  400.5 0.6 slice.117
  401.1 0.7 slice_bitcast_fusion.1
  401.8 1.0 slice_convert_fusion.3
  402.9 0.8 pad_maximum_fusion.1
  403.7 0.0 copy-done.1
  403.7 0.3 slice_convert_fusion
  404.0 0.2 fusion.23
  404.2 1.0 pad_maximum_fusion
  405.3 2.5 bitcast_convert_fusion
  407.8 1.0 maximum_bitcast_fusion.1
  408.8 0.1 fusion.25
  408.9 1.0 maximum_bitcast_fusion
  409.9 0.0 copy-start.3
  409.9 3.8 convolution_bitcast_fusion
  413.7 0.0 copy-done.3
  413.7 0.7 copy.64
  (8 shorter events, 0.1 us)
Async XLA Ops:
  0.6 6.4 %copy-start = (bf16[80,109]{1,0:T(8,128)(2,1)S(1)}, bf16[80,109]{1,0:T(8,128)(2,1)}, u32[]{:S(2)}) copy-start(bf16[80,109]{1,0:T(8,128)(2,1)} %param.29) | copy-start | bytes 52324
  0.7 11.9 %copy-start.4 = (bf16[1,1024]{1,0:T(2,128)(2,1)S(1)}, bf16[1,1024]{1,0:T(2,128)(2,1)}, u32[]{:S(2)}) copy-start(bf16[1,1024]{1,0:T(2,128)(2,1)} %param.25) | copy-start | bytes 6148
  0.7 11.9 %copy-start.2 = (bf16[1,1024,80]{1,2,0:T(8,128)(2,1)S(1)}, bf16[1,1024,80]{1,2,0:T(8,128)(2,1)}, u32[]{:S(2)}) copy-start(bf16[1,1024,80]{1,2,0:T(8,128)(2,1)} %param.24) | copy-start | bytes 491524
  398.2 5.5 %copy-start.1 = (bf16[2016,1024]{1,0:T(8,128)(2,1)S(1)}, bf16[2016,1024]{1,0:T(8,128)(2,1)}, u32[]{:S(2)}) copy-start(bf16[2016,1024]{1,0:T(8,128)(2,1)} %get-tuple-element.16) | copy-start | bytes 12386308
  409.9 3.8 copy-start.3

commit v2 on v1

v2 whole, which is shorter than its diff:
```python
import functools
import math

import jax
import jax.numpy as jnp
from jax import lax
from jax.experimental import pallas as pl
from jax.experimental.pallas import tpu as pltpu
from jax.sharding import PartitionSpec as P

HALF_ROOT = 0.7071067811865476
WEIGHT_SCALE = 64.0
MESH = pl.DeviceIdType.MESH
BF16 = jnp.bfloat16
F32 = jnp.float32

PIECE = 128
EXT = 96
WIDE = 1024
BLOCK = 48
HUB = 2
LAG = 4


def dot(left, right):
    return jnp.dot(left, right, preferred_element_type=F32)


def dot_nt(left, right):
    return lax.dot_general(left, right, (((1,), (1,)), ((), ())), preferred_element_type=F32)


def sigmoid(values):
    return 0.5 * jnp.tanh(0.5 * values) + 0.5


def step_kernel(
    dims,
    dil_ref,
    offs_ref,
    spk_ref,
    cnt_ref,
    tgt_ref,
    mel_ref,
    tab_ref,
    wc_in,
    bias_in,
    inp_hbm,
    up_hbm,
    wd_hbm,
    wr_hbm,
    ws_hbm,
    wp_hbm,
    wk_hbm,
    o_acc,
    o_g,
    o_gin,
    x_buf,
    sg_buf,
    gx_buf,
    gc_buf,
    hid_buf,
    d1_buf,
    d2_buf,
    x_out,
    k_out,
    gx_out,
    gc_out,
    gate_buf,
    gh_buf,
    gg_buf,
    shift_buf,
    cond_ref,
    wc_ref,
    wd_ref,
    wr_ref,
    ws_ref,
    wp_ref,
    wk_ref,
    wc_n,
    wd_t,
    wr_t,
    ws_t,
    wp_t,
    wk_t,
    gl_buf,
    a2_buf,
    gp_buf,
    a1_buf,
    acc,
    part_out,
    part_in,
    gin_buf,
    up_buf,
    extra_buf,
    inp_sem,
    load_sem,
    loc_sem,
    x_ss,
    x_rs,
    k_ss,
    k_rs,
    gs_ss,
    gs_rs,
    gx_ss,
    gx_rs,
    gc_ss,
    gc_rs,
    zi_ss,
    zo_ss,
    zp_rs,
    zt_rs,
    hd_ss,
    hd_rs,
    g_rs,
    gown_ss,
    gpeer_ss,
    ghub_ss,
    gnext_ss,
    gin_ss,
    gin_rs,
):
    sections, groups, micro, res, half, classes, slots, keep, mel_rows = dims
    pieces = 2 * micro
    s = lax.axis_index("section")
    z = lax.axis_index("dp")
    is_first = s == 0
    is_last = s == sections - 1
    is_hub = s == HUB
    head_scale = 1.0 / math.sqrt(sections)
    main_rows = 2 * half + EXT + half
    head_rows = half // 2 + classes // 2
    main_blocks = main_rows // BLOCK
    head_blocks = head_rows // BLOCK
    share = res // sections

    barrier = pltpu.get_barrier_semaphore()

    def greet(cond, dev_s, dev_z):
        @pl.when(cond)
        def _():
            pl.semaphore_signal(barrier, 1, device_id=(dev_s, dev_z), device_id_type=MESH)

    greet(s > 0, s - 1, z)
    greet(s < sections - 1, s + 1, z)
    greet(z > 0, s, z - 1)
    greet(z < groups - 1, s, z + 1)
    greet(s >= 2, 0, z)
    greet((s > HUB + 1) & (lax.rem(s, 2) == 0), HUB, z)

    @pl.when(is_first)
    def _():
        @pl.loop(2, sections)
        def _(other):
            pl.semaphore_signal(barrier, 1, device_id=(other, z), device_id_type=MESH)

    @pl.when(is_hub)
    def _():
        @pl.loop(HUB // 2 + 1, sections // 2)
        def _(chip):
            pl.semaphore_signal(barrier, 1, device_id=(2 * chip, z), device_id_type=MESH)

        for other in range(groups):
            greet((other > z + 1) | (other < z - 1), s, other)

    def flag(cond):
        return jnp.where(cond, 1, 0)

    z_near = flag(z > 0) + flag(z < groups - 1)
    expected = (
        flag(s > 0)
        + flag(s < sections - 1)
        + z_near
        + jnp.where(is_first, sections - 2, flag(s >= 2))
        + flag((s > HUB + 1) & (lax.rem(s, 2) == 0))
        + jnp.where(is_hub, groups - 1 - z_near + sections // 2 - HUB // 2 - 1, 0)
    )

    def input_copy(c):
        return pltpu.make_async_copy(
            inp_hbm.at[:, pl.ds(pl.multiple_of(c * PIECE, PIECE), PIECE)],
            x_buf.at[c],
            inp_sem.at[c],
        )

    quarter = mel_rows // 4
    loads = [
        pltpu.make_async_copy(
            up_hbm.at[pl.ds(q * quarter * mel_rows, quarter * mel_rows), :],
            part_out.at[pl.ds(0, quarter * mel_rows), pl.ds(q * 2 * PIECE, 2 * PIECE)],
            load_sem.at[q],
        )
        for q in range(4)
    ]
    weight_refs = ((wd_hbm, wd_ref), (wr_hbm, wr_ref), (ws_hbm, ws_ref), (wp_hbm, wp_ref), (wk_hbm, wk_ref))
    for position, (source, target) in enumerate(weight_refs):
        loads.append(pltpu.make_async_copy(source, target, load_sem.at[4 + position]))
    for load in loads[:5]:
        load.start()

    @pl.when(is_first)
    def _():
        @pl.loop(0, pieces)
        def _(c):
            input_copy(c).start()

    for load in loads[5:]:
        load.start()
    wc_ref[0:mel_rows] = wc_in[...]
    spare = lax.broadcasted_iota(jnp.int32, (EXT - mel_rows, 2 * half), 0)
    bias = jnp.broadcast_to(bias_in[...].astype(F32), (EXT - mel_rows, 2 * half))
    wc_ref[mel_rows:EXT] = jnp.where(spare == 0, bias, 0.0).astype(BF16)
    wc_n[...] = jnp.transpose(wc_ref[...])

    for load in loads[:4]:
        load.wait()

    @pl.loop(0, quarter)
    def _(row):
        for q in range(4):
            matrix = part_out[pl.ds(pl.multiple_of(row * mel_rows, 16), mel_rows), q * 2 * PIECE : (q + 1) * 2 * PIECE]
            frames = dot(mel_ref[...], matrix)
            for h in range(2):
                up_buf[h, pl.ds(q * quarter + row, micro, stride=mel_rows), :] = frames[:, h * PIECE : (h + 1) * PIECE]

    speaker_lane = lax.broadcasted_iota(jnp.int32, tab_ref.shape, 1)
    spare = lax.broadcasted_iota(jnp.int32, (EXT - mel_rows, PIECE), 0)
    table = tab_ref[...].astype(F32)

    @pl.loop(0, micro)
    def _(m):
        def column(which):
            return jnp.sum(jnp.where(speaker_lane == spk_ref[which, m], table, 0.0), axis=1, keepdims=True)

        first, second = column(0), column(1)
        for h in range(2):
            time = lax.broadcasted_iota(jnp.int32, (mel_rows, PIECE), 1) + h * PIECE
            speaker = jnp.where(time >= offs_ref[0, m], second, first)
            rows = pl.ds(pl.multiple_of(m * mel_rows, 16), mel_rows)
            cond_ref[2 * m + h, 0:mel_rows, :] = (up_buf[h, rows, :] + speaker).astype(BF16)
            cond_ref[2 * m + h, mel_rows:EXT, :] = jnp.where(spare == 0, 1.0, 0.0).astype(BF16)

    def prepare():
        wd_t[...] = jnp.transpose(wd_ref[...])
        wr_t[...] = jnp.transpose(wr_ref[...])
        ws_t[...] = jnp.transpose(ws_ref[...])
        acc[...] = jnp.zeros_like(acc)

    for load in loads[4:]:
        load.wait()

    pl.semaphore_wait(barrier, expected)

    @pl.when(s > 0)
    def _():
        prepare()

    @pl.when(is_last)
    def _():
        wp_t[...] = jnp.transpose(wp_ref[...])
        wk_t[...] = jnp.transpose(wk_ref[...])
        gx_buf[...] = jnp.zeros_like(gx_buf)

    def remote(src, dst, send_sem, recv_sem, dev_s, dev_z):
        return pltpu.make_async_remote_copy(
            src_ref=src,
            dst_ref=dst,
            send_sem=send_sem,
            recv_sem=recv_sem,
            device_id=(dev_s, dev_z),
            device_id_type=MESH,
        )

    def x_copy(c):
        slot = lax.rem(c, slots)
        return remote(x_out.at[slot], x_buf.at[c], x_ss.at[slot], x_rs.at[c], s + 1, z)

    def k_copy(c):
        slot = lax.rem(c, slots)
        return remote(k_out.at[slot], sg_buf.at[c], k_ss.at[slot], k_rs.at[c], s + 1, z)

    def gs_copy(c):
        return remote(sg_buf.at[c], sg_buf.at[c], gs_ss.at[c], gs_rs.at[c], s - 1, z)

    def gx_copy(c):
        slot = lax.rem(c, slots)
        return remote(gx_out.at[slot], gx_buf.at[c], gx_ss.at[slot], gx_rs.at[c], s - 1, z)

    def gc_copy(c):
        slot = lax.rem(c, slots)
        return remote(gc_out.at[slot], gc_buf.at[c], gc_ss.at[slot], gc_rs.at[c], s - 1, z)

    def reuse(copy, c):
        if pieces > slots:

            @pl.when(c >= slots)
            def _():
                copy(c).wait_send()

    def build_shift(m):
        dilation = dil_ref[0]
        middle = offs_ref[0, m]
        source = lax.broadcasted_iota(jnp.int32, (2 * PIECE, 2 * PIECE), 0)
        target = lax.broadcasted_iota(jnp.int32, (2 * PIECE, 2 * PIECE), 1)
        start = jnp.where(target >= middle, middle, 0)
        hit = (source == target - dilation) & (source >= start)
        shift_buf[...] = jnp.where(hit, 1.0, 0.0).astype(BF16)

    def columns(ref, first, parts):
        return jnp.concatenate([ref[first + h] for h in parts], axis=1)

    def put(ref, first, parts, value):
        for position, h in enumerate(parts):
            ref[first + h] = value[:, position * PIECE : (position + 1) * PIECE]

    def head(m, total):
        parts = (0, 1)
        width = 2 * PIECE
        total = total.astype(BF16).astype(F32) * head_scale
        sig_1 = sigmoid(total)
        act_1 = (total * sig_1).astype(BF16)
        slope_1 = sig_1 * (1.0 + total * (1.0 - sig_1)) * head_scale
        post = dot(wp_ref[...], act_1)
        sig_2 = sigmoid(post)
        act_2 = (post * sig_2).astype(BF16)
        slope_2 = sig_2 * (1.0 + post * (1.0 - sig_2))
        logits = dot(wk_ref[...], act_2)
        top = jnp.max(logits, axis=0, keepdims=True)
        expo = jnp.exp(logits - top)
        denominator = jnp.sum(expo, axis=0, keepdims=True)
        hit = tgt_ref[m] == lax.broadcasted_iota(jnp.int32, (classes, width), 0)
        picked = jnp.sum(jnp.where(hit, logits, 0.0), axis=0, keepdims=True)
        time = lax.broadcasted_iota(jnp.int32, (1, width), 1)

        def speaker_weight(which):
            count = cnt_ref[spk_ref[which, m]].astype(F32)
            return WEIGHT_SCALE * lax.rsqrt(jnp.full((1, width), count, F32))

        weight = jnp.where(time >= offs_ref[0, m], speaker_weight(1), speaker_weight(0))
        weight = jnp.where(time < offs_ref[1, m], weight, 0.0)
        grad_logits = (weight * (expo / denominator - jnp.where(hit, 1.0, 0.0))).astype(BF16)
        grad_post = (dot(wk_t[...], grad_logits) * slope_2).astype(BF16)
        grad_total = (dot(wp_t[...], grad_post) * slope_1).astype(BF16)
        put(sg_buf, 2 * m, parts, grad_total)
        for h in (1, 0):
            gs_copy(2 * m + h).start()
        kept = 2 * lax.rem(m, keep)
        put(gl_buf, kept, parts, grad_logits)
        put(a2_buf, kept, parts, act_2)
        put(gp_buf, kept, parts, grad_post)
        put(a1_buf, kept, parts, act_1)
        loss_row = weight * (top + jnp.log(denominator) - picked)
        high = loss_row.astype(BF16)
        rest = loss_row - high.astype(F32)
        middle = rest.astype(BF16)
        low = (rest - middle.astype(F32)).astype(BF16)
        row = lax.broadcasted_iota(jnp.int32, (EXT, width), 0)
        message = jnp.where(row == mel_rows + 2, high.astype(F32), 0.0)
        message = jnp.where(row == mel_rows + 3, middle.astype(F32), message)
        message = jnp.where(row == mel_rows + 4, low.astype(F32), message)
        put(gc_buf, 2 * m, parts, message.astype(BF16))

    def forward(m, parts):
        wide = pl.ds(0, len(parts) * PIECE)
        for h in parts:
            c = 2 * m + h

            @pl.when(is_first)
            def _():
                input_copy(c).wait()

            @pl.when(s > 0)
            def _():
                x_copy(c).wait_recv()

        x = columns(x_buf, 2 * m, parts)
        if parts == (0,):
            prev = dot(x, shift_buf[0:PIECE, 0:PIECE])
        elif parts == (1,):
            prev = dot(columns(x_buf, 2 * m, (0, 1)), shift_buf[:, PIECE : 2 * PIECE])
        else:
            prev = dot(x, shift_buf[...])
        stack = jnp.concatenate([prev.astype(BF16), x], axis=0)
        gate = dot(wd_ref[...], stack) + dot(wc_n[...], columns(cond_ref, 2 * m, parts))
        th = jnp.tanh(gate[0:half])
        sg = sigmoid(gate[half : 2 * half])
        gate_buf[0:half, wide] = th
        gate_buf[half : 2 * half, wide] = sg
        put(hid_buf, 2 * m, parts, (th * sg).astype(BF16))

    def forward_rest(m, parts):
        wide = pl.ds(0, len(parts) * PIECE)
        th = gate_buf[0:half, wide]
        sg = gate_buf[half : 2 * half, wide]
        put(d1_buf, 2 * m, parts, (sg * (1.0 - th * th)).astype(BF16))
        put(d2_buf, 2 * m, parts, (th * sg * (1.0 - sg)).astype(BF16))

    def forward_piece(m, h):
        c = 2 * m + h
        forward(m, (h,))
        reuse(x_copy, c)
        out = (x_buf[c].astype(F32) + dot(wr_ref[...], hid_buf[c])) * HALF_ROOT
        x_out[lax.rem(c, slots)] = out.astype(BF16)
        x_copy(c).start()
        gh_buf[:, 0:PIECE] = dot(ws_ref[...], hid_buf[c])
        forward_rest(m, (h,))

        @pl.when(s > 0)
        def _():
            k_copy(c).wait_recv()
            gh_buf[:, 0:PIECE] += sg_buf[c].astype(F32)

        reuse(k_copy, c)
        k_out[lax.rem(c, slots)] = gh_buf[:, 0:PIECE].astype(BF16)
        k_copy(c).start()

    def forward_head(m):
        forward(m, (0, 1))
        total = dot(ws_ref[...], columns(hid_buf, 2 * m, (0, 1)))
        for h in (0, 1):
            k_copy(2 * m + h).wait_recv()
        head(m, total + columns(sg_buf, 2 * m, (0, 1)).astype(F32))
        forward_rest(m, (0, 1))

    def grad_field(m, parts, grad_hidden):
        kept = 2 * lax.rem(m, keep)
        grad_gate = jnp.concatenate(
            [
                grad_hidden * columns(d1_buf, 2 * m, parts).astype(F32),
                grad_hidden * columns(d2_buf, 2 * m, parts).astype(F32),
            ],
            axis=0,
        ).astype(BF16)
        put(gg_buf, kept, parts, grad_gate)
        if parts == (1,):
            back = dot_nt(grad_gate, shift_buf[PIECE:, PIECE:])
        elif parts == (0,):
            both = jnp.concatenate([grad_gate, gg_buf[kept + 1]], axis=1)
            back = dot_nt(both, shift_buf[0:PIECE, :])
        else:
            back = dot_nt(grad_gate, shift_buf[...])
        return dot(wd_t[res : 2 * res], grad_gate) + dot(wd_t[0:res], back.astype(BF16))

    def cond_message(m, parts):
        kept = 2 * lax.rem(m, keep)
        row = lax.broadcasted_iota(jnp.int32, (EXT, len(parts) * PIECE), 0)
        own = jnp.where(row < mel_rows, dot(wc_ref[...], columns(gg_buf, kept, parts)), 0.0)
        return own + columns(gc_buf, 2 * m, parts).astype(F32)

    def backward_piece(m, h):
        c = 2 * m + h
        gs_copy(c).wait_recv()

        @pl.when(s > 0)
        def _():
            gs_copy(c).start()

        gh_buf[:, 0:PIECE] = dot(ws_t[...], sg_buf[c])
        gx_copy(c).wait_recv()
        grad_hidden = gh_buf[:, 0:PIECE] + HALF_ROOT * dot(wr_t[...], gx_buf[c])
        grad_x = (HALF_ROOT * gx_buf[c].astype(F32) + grad_field(m, (h,), grad_hidden)).astype(BF16)

        @pl.when(s > 0)
        def _():
            reuse(gx_copy, c)
            gx_out[lax.rem(c, slots)] = grad_x
            gx_copy(c).start()

        gc_copy(c).wait_recv()
        message = cond_message(m, (h,))

        @pl.when(s > 0)
        def _():
            reuse(gc_copy, c)
            gc_out[lax.rem(c, slots)] = message.astype(BF16)
            gc_copy(c).start()

        @pl.when(is_first)
        def _():
            d1_buf[c] = grad_x
            gc_buf[c, 0:mel_rows, :] = message[0:mel_rows].astype(BF16)
            tail = message[mel_rows:EXT]
            if h == 0:
                frame = lax.broadcasted_iota(jnp.int32, mel_ref.shape, 0) == m
                extra_buf[0:1, 0:mel_rows] = jnp.sum(
                    jnp.where(frame, mel_ref[...].astype(F32), 0.0), axis=0, keepdims=True
                )
                lane = lax.broadcasted_iota(jnp.int32, (1, PIECE), 1)
                ids = jnp.where(lane == 0, spk_ref[0, m], 0)
                ids = jnp.where(lane == 1, spk_ref[1, m], ids)
                ids = jnp.where(lane == 2, offs_ref[0, m], ids)
                extra_buf[1:2, :] = ids.astype(F32)
                tail = tail + extra_buf[...]
            gc_buf[c, mel_rows:EXT, :] = tail.astype(BF16)

    def backward_pair(m):
        parts = (0, 1)
        grad_hidden = dot(ws_t[...], columns(sg_buf, 2 * m, parts))
        grad_x = grad_field(m, parts, grad_hidden).astype(BF16)
        for h in (1, 0):
            c = 2 * m + h
            reuse(gx_copy, c)
            gx_out[lax.rem(c, slots)] = grad_x[:, h * PIECE : (h + 1) * PIECE]
            gx_copy(c).start()
        message = cond_message(m, parts).astype(BF16)
        for h in (1, 0):
            c = 2 * m + h
            reuse(gc_copy, c)
            gc_out[lax.rem(c, slots)] = message[:, h * PIECE : (h + 1) * PIECE]
            gc_copy(c).start()

    def add_halves(first_row, value):
        rows = value.shape[0] // 2
        acc[first_row : first_row + rows, 0:half] += value[0:rows]
        acc[first_row : first_row + rows, half : 2 * half] += value[rows : 2 * rows]

    def weight_gradients(m):
        parts = (0, 1)
        kept = 2 * lax.rem(m, keep)
        grad_gate = columns(gg_buf, kept, parts)
        x = columns(x_buf, 2 * m, parts)
        prev = dot(x, shift_buf[...]).astype(BF16)
        acc[0 : 2 * half, 0:res] += dot_nt(grad_gate, prev)
        acc[0 : 2 * half, res : 2 * res] += dot_nt(grad_gate, x)
        acc[2 * half : 2 * half + EXT, :] += dot_nt(columns(cond_ref, 2 * m, parts), grad_gate)
        hidden = columns(hid_buf, 2 * m, parts)
        row = 2 * half + EXT

        @pl.when(s < sections - 1)
        def _():
            add_halves(row, HALF_ROOT * dot_nt(columns(gx_buf, 2 * m, parts), hidden))

        add_halves(row + half // 2, dot_nt(columns(sg_buf, 2 * m, parts), hidden))

        @pl.when(is_last)
        def _():
            add_halves(main_rows, dot_nt(columns(gp_buf, kept, parts), columns(a1_buf, kept, parts)))
            add_halves(main_rows + half // 2, dot_nt(columns(gl_buf, kept, parts), columns(a2_buf, kept, parts)))

    late = keep == micro

    @pl.when(is_last)
    def _():
        @pl.loop(0, micro)
        def _(m):
            build_shift(m)
            forward_head(m)
            backward_pair(m)
            if not late:
                weight_gradients(m)

    @pl.when(jnp.logical_not(is_last))
    def _():
        @pl.loop(0, micro)
        def _(m):
            build_shift(m)
            forward_piece(m, 0)
            forward_piece(m, 1)

        @pl.when(is_first)
        def _():
            prepare()
            extra_buf[...] = jnp.zeros_like(extra_buf)

    @pl.loop(0, micro)
    def _(m):
        build_shift(m)

        @pl.when(jnp.logical_not(is_last))
        def _():
            backward_piece(m, 1)
            backward_piece(m, 0)

        if late:
            weight_gradients(m)
        else:

            @pl.when(jnp.logical_not(is_last))
            def _():
                weight_gradients(m)

    def gin_copy(other):
        return remote(
            d1_buf.at[:, pl.ds(pl.multiple_of(other * share, share), share), :],
            gin_buf,
            gin_ss.at[other],
            gin_rs.at[0],
            other,
            z,
        )

    def own_local():
        return pltpu.make_async_copy(gc_buf, o_g.at[z], loc_sem.at[0])

    def own_hub():
        return remote(gc_buf, o_g.at[z], gown_ss.at[0], g_rs.at[z], HUB, z)

    def own_peer(other):
        return remote(o_g.at[z], o_g.at[z], gpeer_ss.at[other], g_rs.at[z], HUB, other)

    def part_chip(j, chip):
        return remote(o_g.at[j], o_g.at[j], ghub_ss.at[j, chip], g_rs.at[j], 2 * chip, z)

    def part_next(j):
        return remote(o_g.at[j], o_g.at[j], gnext_ss.at[j], g_rs.at[j], s + 1, z)

    def spread(j):
        part_next(j).start()

        @pl.loop(0, sections // 2)
        def _(chip):
            @pl.when((chip != HUB // 2) & ((chip > 0) | (z != j)))
            def _():
                part_chip(j, chip).start()

    @pl.when(is_first)
    def _():
        own_local().start()
        own_hub().start()
        own_local().wait()

        @pl.loop(1, sections)
        def _(other):
            gin_copy(other).start()

        gin_buf[...] = d1_buf[:, 0:share, :]

    left = z < groups // 2
    inward = jnp.where(left, z + 1, z - 1)
    outward = jnp.where(left, z - 1, z + 1)
    is_edge = (z == 0) | (z == groups - 1)
    is_mid = (z == groups // 2 - 1) | (z == groups // 2)
    distance = jnp.where(left, groups // 2 - 1 - z, z - groups // 2)
    lag = LAG * (2 * distance + 1)
    count = jnp.where(is_last, main_blocks + head_blocks, main_blocks)

    def block_of(i):
        return jnp.where(is_last, jnp.where(i < head_blocks, i + main_blocks, i - head_blocks), i)

    def rows_of(b):
        return pl.ds(pl.multiple_of(b * BLOCK, BLOCK), BLOCK)

    def swap_copy(b):
        return remote(part_out.at[rows_of(b)], o_acc.at[rows_of(b)], zi_ss.at[b], zt_rs.at[b], s, inward)

    def part_copy(b):
        return remote(part_out.at[rows_of(b)], part_in.at[rows_of(b)], zi_ss.at[b], zp_rs.at[b], s, inward)

    def total_copy(b):
        return remote(o_acc.at[rows_of(b)], o_acc.at[rows_of(b)], zo_ss.at[b], zt_rs.at[b], s, outward)

    def head_copy(j):
        rows = rows_of(main_blocks + j)
        return remote(o_acc.at[rows], o_acc.at[rows], hd_ss.at[j], hd_rs.at[j], s - 1, z)

    def send_part(b):
        rows = rows_of(b)

        @pl.when(is_edge)
        def _():
            part_out[rows, :] = acc[rows, :].astype(BF16)

        @pl.when(jnp.logical_not(is_edge))
        def _():
            part_copy(b).wait_recv()
            part_out[rows, :] = (acc[rows, :] + part_in[rows, :].astype(F32)).astype(BF16)

        @pl.when(is_mid)
        def _():
            swap_copy(b).start()

        @pl.when(jnp.logical_not(is_mid))
        def _():
            part_copy(b).start()

    def finish_part(b):
        rows = rows_of(b)
        swap_copy(b).wait_recv()

        @pl.when(is_mid)
        def _():
            o_acc[rows, :] = (part_out[rows, :].astype(F32) + o_acc[rows, :].astype(F32)).astype(BF16)

        @pl.when(jnp.logical_not(is_edge))
        def _():
            total_copy(b).start()

    last_step = main_blocks + lag - 1
    head_at = lag + 2
    own_at = jnp.minimum(9 + 6 * distance, last_step)
    rest_at = jnp.where(is_first, 20, jnp.where(is_hub, 17, jnp.where(s < sections // 2 + 2, 28, 31)))
    rest_at = jnp.minimum(rest_at + 6 * distance, last_step)

    @pl.loop(0, count + lag)
    def _(i):
        @pl.when(i < count)
        def _():
            send_part(block_of(i))

        @pl.when(i >= lag)
        def _():
            b = block_of(i - lag)
            finish_part(b)

            @pl.when(b >= main_blocks)
            def _():
                head_copy(b - main_blocks).start()

        @pl.when(jnp.logical_not(is_last) & (i >= head_at) & (i < head_at + head_blocks))
        def _():
            j = i - head_at
            head_copy(j).wait_recv()

            @pl.when(s > 0)
            def _():
                head_copy(j).start()

        @pl.when(is_hub & (i == own_at))
        def _():
            own_hub().wait_recv()
            for other in range(groups):

                @pl.when(z != other)
                def _():
                    own_peer(other).start()

            spread(z)

        @pl.when((lax.rem(s, 2) == 0) & (i == rest_at))
        def _():
            for j in range(groups):

                @pl.when((z != j) | (s > HUB))
                def _():
                    part_next(j).wait_recv()

                @pl.when(is_hub & (z != j))
                def _():
                    spread(j)

                @pl.when(jnp.logical_not(is_hub))
                def _():
                    part_next(j).start()

    @pl.when(s > 0)
    def _():
        gin_copy(0).wait_recv()

    for c in range(pieces):
        o_gin[:, c * PIECE : (c + 1) * PIECE] = gin_buf[c]

    @pl.when(is_first)
    def _():
        own_hub().wait_send()

        @pl.loop(1, sections)
        def _(other):
            gin_copy(other).wait_send()

    @pl.when(is_hub)
    def _():
        for j in range(groups):

            @pl.when(z != j)
            def _():
                own_peer(j).wait_send()

            @pl.loop(0, sections // 2)
            def _(chip):
                @pl.when((chip != HUB // 2) & ((chip > 0) | (z != j)))
                def _():
                    part_chip(j, chip).wait_send()

    for j in range(groups):

        @pl.when(lax.rem(s, 2) == 0)
        def _():
            part_next(j).wait_send()

        @pl.when(lax.rem(s, 2) == 1)
        def _():
            part_next(j).wait_recv()

    @pl.when(s > 0)
    def _():
        @pl.loop(0, head_blocks)
        def _(j):
            head_copy(j).wait_send()

    @pl.loop(0, count)
    def _(b):
        part_copy(b).wait_send()

        @pl.when(jnp.logical_not(is_edge))
        def _():
            total_copy(b).wait_send()

    @pl.loop(0, slots)
    def _(c):
        @pl.when(s < sections - 1)
        def _():
            x_copy(c).wait_send()
            k_copy(c).wait_send()

        @pl.when(s > 0)
        def _():
            gx_copy(c).wait_send()
            gc_copy(c).wait_send()

    @pl.when(s > 0)
    def _():
        @pl.loop(0, pieces)
        def _(c):
            gs_copy(c).wait_send()


def run_step(dims, tables, arrays, weights):
    sections, groups, micro, res, half, classes, slots, keep, mel_rows = dims
    pieces = 2 * micro
    rows = 2 * half + EXT + half + half // 2 + classes // 2
    blocks = rows // BLOCK
    head_blocks = (half // 2 + classes // 2) // BLOCK
    share = res // sections
    smem = pl.BlockSpec(memory_space=pltpu.SMEM)
    vmem = pl.BlockSpec(memory_space=pltpu.VMEM)
    anywhere = pl.BlockSpec(memory_space=pl.ANY)
    dma = pltpu.SemaphoreType.DMA

    def tile(*shape, dtype=BF16):
        return pltpu.VMEM(shape, dtype)

    scratch = [
        tile(pieces, res, PIECE),
        tile(pieces, half, PIECE),
        tile(pieces, res, PIECE),
        tile(pieces, EXT, PIECE),
        tile(pieces, half, PIECE),
        tile(pieces, half, PIECE),
        tile(pieces, half, PIECE),
        tile(slots, res, PIECE),
        tile(slots, half, PIECE),
        tile(slots, res, PIECE),
        tile(slots, EXT, PIECE),
        tile(2 * half, 2 * PIECE, dtype=F32),
        tile(half, PIECE, dtype=F32),
        tile(2 * keep, 2 * half, PIECE),
        tile(2 * PIECE, 2 * PIECE),
        tile(pieces, EXT, PIECE),
        tile(EXT, 2 * half),
        tile(2 * half, 2 * res),
        tile(res, half),
        tile(half, half),
        tile(half, half),
        tile(classes, half),
        tile(2 * half, EXT),
        tile(2 * res, 2 * half),
        tile(half, res),
        tile(half, half),
        tile(half, half),
        tile(half, classes),
        tile(2 * keep, classes, PIECE),
        tile(2 * keep, half, PIECE),
        tile(2 * keep, half, PIECE),
        tile(2 * keep, half, PIECE),
        tile(rows, WIDE, dtype=F32),
        tile(rows, WIDE),
        tile(rows, WIDE),
        tile(pieces, share, PIECE),
        tile(2, micro * mel_rows, PIECE, dtype=F32),
        tile(EXT - mel_rows, PIECE, dtype=F32),
        dma((pieces,)),
        dma((9,)),
        dma((1,)),
        dma((slots,)),
        dma((pieces,)),
        dma((slots,)),
        dma((pieces,)),
        dma((pieces,)),
        dma((pieces,)),
        dma((slots,)),
        dma((pieces,)),
        dma((slots,)),
        dma((pieces,)),
        dma((blocks,)),
        dma((blocks,)),
        dma((blocks,)),
        dma((blocks,)),
        dma((head_blocks,)),
        dma((head_blocks,)),
        dma((groups,)),
        dma((1,)),
        dma((groups,)),
        dma((groups, sections // 2)),
        dma((groups,)),
        dma((sections,)),
        dma((1,)),
    ]
    return pl.pallas_call(
        functools.partial(step_kernel, dims),
        out_shape=(
            jax.ShapeDtypeStruct((rows, WIDE), BF16),
            jax.ShapeDtypeStruct((groups, pieces, EXT, PIECE), BF16),
            jax.ShapeDtypeStruct((share, pieces * PIECE), BF16),
        ),
        in_specs=[smem] * 4 + [vmem] * 5 + [anywhere] * 7,
        out_specs=(vmem, anywhere, vmem),
        scratch_shapes=scratch,
        compiler_params=pltpu.CompilerParams(
            collective_id=0, has_side_effects=True, vmem_limit_bytes=63 * 2**20
        ),
        cost_estimate=pl.CostEstimate(flops=10**10, bytes_accessed=3 * 10**7, transcendentals=10**6),
        name="train_step",
    )(*tables, *arrays, *weights)


def finish_kernel(
    dims, steps, dil, cond, res, skip, post, out, shared, o_dil, o_cond, o_bias, o_res, o_skip, o_post, o_out,
    o_up, o_table, o_loss, field, mel_rows_buf, mel_columns, table,
):
    mel_rows, half = dims
    i = pl.program_id(0)
    frames = shared.shape[0]

    @pl.when(i == 0)
    def _():
        table[...] = jnp.zeros_like(table)
        lane = lax.broadcasted_iota(jnp.int32, (mel_rows, PIECE), 1)
        number = lane.astype(F32)

        def one(f, loss):
            extra = shared[f, 0, mel_rows:EXT, :].astype(F32)
            loss = loss + extra + shared[f, 1, mel_rows:EXT, :].astype(F32)
            mel_rows_buf[pl.ds(f, 1), :] = extra[0:1]
            ids = extra[1:2]
            first = jnp.zeros((mel_rows, 1), F32)
            second = jnp.zeros((mel_rows, 1), F32)
            for h in range(2):
                part = shared[f, h, 0:mel_rows, :].astype(F32)
                field[h, pl.ds(pl.multiple_of(f * mel_rows, 16), mel_rows), :] = part
                later = number + float(h * PIECE) >= ids[:, 2:3]
                first = first + jnp.sum(jnp.where(later, 0.0, part), axis=1, keepdims=True)
                second = second + jnp.sum(jnp.where(later, part, 0.0), axis=1, keepdims=True)
            table[...] += jnp.where(number == ids[:, 0:1], first, 0.0)
            table[...] += jnp.where(number == ids[:, 1:2], second, 0.0)
            return loss

        loss = lax.fori_loop(0, frames, one, jnp.zeros((EXT - mel_rows, PIECE), F32))
        row = lax.broadcasted_iota(jnp.int32, loss.shape, 0)
        loss = jnp.where((row >= 2) & (row < 5), loss, 0.0)
        o_loss[...] = jnp.sum(jnp.sum(loss, axis=1, keepdims=True), axis=0, keepdims=True)
        o_table[...] = table[:, 0 : o_table.shape[1]]
        mel_columns[...] = jnp.transpose(mel_rows_buf[...])[0:mel_rows].astype(BF16)

    o_dil[0] = dil[...].astype(F32)
    for source, target in ((res, o_res), (skip, o_skip), (post, o_post), (out, o_out)):
        target[0] = source[:, 0:half].astype(F32)
        target[1] = source[:, half : 2 * half].astype(F32)

    @pl.when(i < mel_rows // 16)
    def _():
        o_cond[...] = cond[...].astype(F32)

    @pl.when(i == mel_rows // 16)
    def _():
        o_bias[...] = cond[...].astype(F32)[0:1]

    channels = mel_rows // steps
    for j in range(channels):
        rows = pl.ds(i * channels + j, frames, stride=mel_rows)
        matrix = jnp.concatenate([field[0, rows, :], field[1, rows, :]], axis=1)
        o_up[j] = dot(mel_columns[...], matrix.astype(BF16))


def finish(sums, shared, half, classes, mel_rows, speakers):
    steps = 8
    frames = shared.shape[0]
    first = 2 * half
    small = half // 2 // steps
    last = classes // 2 // steps
    res_at = (first + EXT) // small
    per = half // 2 // small
    rows = mel_rows // 16

    def strip(height, index):
        return pl.BlockSpec((height, WIDE), index)

    def two(height):
        return pl.BlockSpec((2, height, half), lambda i: (0, i, 0))

    def fixed(*shape):
        return pl.BlockSpec(shape, lambda i: (0,) * len(shape))

    def f32(*shape):
        return jax.ShapeDtypeStruct(shape, F32)

    return pl.pallas_call(
        functools.partial(finish_kernel, (mel_rows, half), steps),
        grid=(steps,),
        out_shape=(
            f32(1, first, WIDE),
            f32(mel_rows, WIDE),
            f32(1, WIDE),
            f32(2, half // 2, half),
            f32(2, half // 2, half),
            f32(2, half // 2, half),
            f32(2, classes // 2, half),
            f32(mel_rows, mel_rows, 2 * PIECE),
            f32(mel_rows, speakers),
            f32(1, 1),
        ),
        in_specs=[
            strip(first // steps, lambda i: (i, 0)),
            strip(16, lambda i: (first // 16 + jnp.minimum(i, rows), 0)),
            strip(small, lambda i: (res_at + i, 0)),
            strip(small, lambda i: (res_at + per + i, 0)),
            strip(small, lambda i: (res_at + 2 * per + i, 0)),
            strip(last, lambda i: ((first + EXT + half + half // 2) // last + i, 0)),
            pl.BlockSpec(memory_space=pltpu.VMEM),
        ],
        out_specs=(
            pl.BlockSpec((1, first // steps, WIDE), lambda i: (0, i, 0)),
            strip(16, lambda i: (jnp.minimum(i, rows - 1), 0)),
            fixed(1, WIDE),
            two(small),
            two(small),
            two(small),
            two(last),
            pl.BlockSpec((mel_rows // steps, mel_rows, 2 * PIECE), lambda i: (i, 0, 0)),
            fixed(mel_rows, speakers),
            fixed(1, 1),
        ),
        scratch_shapes=[
            pltpu.VMEM((2, frames * mel_rows, PIECE), F32),
            pltpu.VMEM((frames, PIECE), F32),
            pltpu.VMEM((mel_rows, frames), BF16),
            pltpu.VMEM((mel_rows, PIECE), F32),
        ],
        compiler_params=pltpu.CompilerParams(
            vmem_limit_bytes=48 * 2**20, dimension_semantics=("arbitrary",)
        ),
        name="finish",
    )(sums, sums, sums, sums, sums, sums, shared)


def local(
    inputs,
    targets,
    mel,
    speakers,
    speaker_sample_counts,
    segment_offsets,
    dilations,
    dilated_kernel,
    conditioning_projection,
    dilated_gate_bias,
    residual_projection,
    skip_projection,
    upsample_weight,
    speaker_table,
    first_output_projection,
    class_projection,
):
    sections = lax.axis_size("section")
    groups = lax.axis_size("dp")
    micro = segment_offsets.shape[0]
    res, tokens = inputs.shape
    length = tokens // micro
    mel_rows = mel.shape[0]
    hop = upsample_weight.shape[0]
    half = residual_projection.shape[2]
    classes = class_projection.shape[0]
    pieces = 2 * micro
    assert length == 2 * PIECE and hop == length and mel_rows + 16 == EXT and 2 * half == WIDE

    slots, keep = (pieces, micro) if pieces <= 8 else (2, 1)
    dims = (sections, groups, micro, res, half, classes, slots, keep, mel_rows)
    sums, shared, grad_inputs = run_step(
        dims,
        (dilations, segment_offsets.T, speakers.T, speaker_sample_counts),
        (
            targets.reshape(micro, 1, length),
            mel.T,
            speaker_table,
            conditioning_projection[0].T,
            dilated_gate_bias,
        ),
        (
            inputs,
            upsample_weight.transpose(1, 2, 0).reshape(mel_rows * mel_rows, hop),
            dilated_kernel[0],
            residual_projection[0],
            skip_projection[0],
            first_output_projection,
            class_projection,
        ),
    )
    shared = shared.reshape(groups * micro, 2, EXT, PIECE)
    dil, cond, bias, grad_res, grad_skip, post, out, up, table, loss = finish(
        sums, shared, half, classes, mel_rows, speaker_table.shape[1]
    )
    return (
        loss.reshape(()),
        grad_inputs,
        dil,
        cond.T[None],
        bias,
        grad_res.reshape(1, half, half),
        grad_skip.reshape(1, half, half),
        up.transpose(2, 0, 1),
        table,
        post.reshape(half, half),
        out.reshape(classes, half),
    )


def solution(mesh):
    return jax.shard_map(
        local,
        mesh=mesh,
        in_specs=(
            P(None, "dp"),
            P("dp"),
            P(None, "dp"),
            P("dp", None),
            P(),
            P("dp", None),
            P("section"),
            P("section", None, None),
            P("section", None, None),
            P("section", None),
            P("section", None, None),
            P("section", None, None),
            P(),
            P(),
            P(),
            P(),
        ),
        out_specs=(
            P(),
            P("section", "dp"),
            P("section", None, None),
            P("section", None, None),
            P("section", None),
            P("section", None, None),
            P("section", None, None),
            P(),
            P(),
            P(),
            P(),
        ),
        check_vma=False,
    )
```

time: 415 us -> 209 us (0.50)
  Pallas kernels: 380 us -> 204 us
  other arithmetic: 13.5 us -> 0 us
  matrix products: 8.37 us -> 0 us
  local copies, waits for them, and re-layouts: 11.3 us -> 3.95 us
    pallas_call x1, Pallas kernels: 380 us -> 194 us  [run_step(): pl.pallas_call(functools.partial(step_kernel, dims), out_shape=(jax.Shape...]
    pallas_call x0 -> x1, Pallas kernels: none -> 9.81 us  [finish(): pl.pallas_call(functools.partial(finish_kernel, (mel_rows, half), steps),...]
    dot_general x5 -> x0, matrix products: 8.37 us -> none  [the longest x1 3.83 us: local(): jnp.einsum('cfk,fa->cak', field_3, mel_all, preferred_element_type=F32)]
    broadcast_in_dim x3 -> x0, other arithmetic: 4.56 us -> none  [the longest x1 2.48 us: local(): grad_dil[None]]
where the time goes in v2:
time: 209 us
  Pallas kernels  204 us (98%)
  local copies, waits for them, and re-layouts  3.95 us (2%)
    pallas_call x1, Pallas kernels, run_step(): pl.pallas_call(functools.partial(step_kernel, dims), out_shape=(jax.Shape...  194 us
    pallas_call x1, Pallas kernels, finish(): pl.pallas_call(functools.partial(finish_kernel, (mel_rows, half), steps),...  9.81 us

profile of v2, /device:TPU:0, one launch (start us, length us, event | category | flops | bytes accessed | tf_op | source)
XLA Modules:
  0.0 209.2 jit_solution(2424046231358457585)
XLA Ops:
  1.3 194.1 %train_step.1 = (bf16[2016,1024]{1,0:T(8,128)(2,1)}, bf16[4,8,96,128]{3,2,1,0:T(8,128)(2,1)}, bf16[64,1024]{1,0:T(8,128)(2,1)}) custom-call(s32[1]{0:T(128)S(6)} %copy.28.dil_ref, s32[2,4]{1,0:T(2,128)} %bitcast.36, s32[2,4]{1,0:T(2,128)} %bitcast.37, s32[109]{0:T(128)} %cnt_ref.1, s32[4,1,256]{2,1,0:T(1,128)} %bitcast.35, bf16[4,80]{1,0:T(4,128)(2,1)} %bitcast.38, ...), custom_call_target="tpu_custom_call" | custom-call | flops 10000000000 | bytes 30000000 | tf_op jit(solution)/shard_map/train_step/pallas_call | solution.py:898
  195.4 0.0 copy-start
  195.4 2.2 %copy-done = bf16[2016,1024]{1,0:T(8,128)(2,1)S(1)} copy-done((bf16[2016,1024]{1,0:T(8,128)(2,1)S(1)}, bf16[2016,1024]{1,0:T(8,128)(2,1)}, u32[]{:S(2)}) %copy-start) | copy-done | bytes 4128792
  197.6 0.0 copy-start.1
  197.6 1.1 copy-done.1
  198.7 0.0 copy-start.2
  198.7 9.8 %finish.1 = (f32[1,1024,1024]{2,1,0:T(8,128)}, f32[80,1024]{1,0:T(8,128)}, f32[1,1024]{1,0:T(1,128)}, f32[2,256,512]{2,1,0:T(8,128)}, f32[2,256,512]{2,1,0:T(8,1...) custom-call(bf16[2016,1024]{1,0:T(8,128)(2,1)S(1)} %copy-done, ...), custom_call_target="tpu_custom_call" | custom-call | tf_op jit(solution)/shard_map/finish/pallas_call | solution.py:996
  208.6 0.0 copy-done.2
  208.6 0.7 copy.29
Async XLA Ops:
  195.4 2.2 %copy-start = (bf16[2016,1024]{1,0:T(8,128)(2,1)S(1)}, bf16[2016,1024]{1,0:T(8,128)(2,1)}, u32[]{:S(2)}) copy-start(bf16[2016,1024]{1,0:T(8,128)(2,1)} %get-tuple-element.24.dil.cond.res.skip.post.out) | copy-start | bytes 12386308
  197.6 1.1 copy-start.1
  198.7 9.8 %copy-start.2 = (bf16[64,1024]{1,0:T(8,128)(2,1)S(1)}, bf16[64,1024]{1,0:T(8,128)(2,1)}, u32[]{:S(2)}) copy-start(bf16[64,1024]{1,0:T(8,128)(2,1)} %get-tuple-element.49) | copy-start | bytes 393220

commit v3 on v2

--- a/solution.py
+++ b/solution.py
@@ -17,9 +17,9 @@
 PIECE = 128
 EXT = 96
 WIDE = 1024
-BLOCK = 48
+BLOCK = 32
 HUB = 2
-LAG = 4
+LAG = 3
 
 
 def dot(left, right):
@@ -28,6 +28,10 @@
 
 def dot_nt(left, right):
     return lax.dot_general(left, right, (((1,), (1,)), ((), ())), preferred_element_type=F32)
+
+
+def dot_tn(left, right):
+    return lax.dot_general(left, right, (((0,), (0,)), ((), ())), preferred_element_type=F32)
 
 
 def sigmoid(values):
@@ -43,10 +47,10 @@
     tgt_ref,
     mel_ref,
     tab_ref,
-    wc_in,
     bias_in,
     inp_hbm,
     up_hbm,
+    wc_hbm,
     wd_hbm,
     wr_hbm,
     ws_hbm,
@@ -69,15 +73,17 @@
     gate_buf,
     gh_buf,
     gg_buf,
+    inp_buf,
     shift_buf,
+    shift_back,
     cond_ref,
+    cond_t,
     wc_ref,
     wd_ref,
     wr_ref,
     ws_ref,
     wp_ref,
     wk_ref,
-    wc_n,
     wd_t,
     wr_t,
     ws_t,
@@ -133,6 +139,7 @@
     main_blocks = main_rows // BLOCK
     head_blocks = head_rows // BLOCK
     share = res // sections
+    feeder = sections - 3 if sections > 4 else sections - 1
 
     barrier = pltpu.get_barrier_semaphore()
 
@@ -162,6 +169,18 @@
 
         for other in range(groups):
             greet((other > z + 1) | (other < z - 1), s, other)
+
+    far = (lax.rem(s, 2) == 1) & (s > 1) & (s < sections - 1)
+    greet(far, sections - 1, z)
+
+    @pl.when(is_last)
+    def _():
+        @pl.loop(1, sections // 2 - 1)
+        def _(chip):
+            pl.semaphore_signal(barrier, 1, device_id=(2 * chip + 1, z), device_id_type=MESH)
+
+    greet(s == 1, feeder, z)
+    greet(s == feeder, 1, z)
 
     def flag(cond):
         return jnp.where(cond, 1, 0)
@@ -173,18 +192,35 @@
         + z_near
         + jnp.where(is_first, sections - 2, flag(s >= 2))
         + flag((s > HUB + 1) & (lax.rem(s, 2) == 0))
+        + flag(far)
+        + flag(s == 1)
+        + flag(s == feeder)
+        + jnp.where(is_last, sections // 2 - 2, 0)
         + jnp.where(is_hub, groups - 1 - z_near + sections // 2 - HUB // 2 - 1, 0)
     )
 
     def input_copy(c):
+        slot = lax.rem(c, slots)
         return pltpu.make_async_copy(
             inp_hbm.at[:, pl.ds(pl.multiple_of(c * PIECE, PIECE), PIECE)],
-            x_buf.at[c],
-            inp_sem.at[c],
+            inp_buf.at[slot],
+            inp_sem.at[slot],
         )
 
     quarter = mel_rows // 4
+    weight_refs = (
+        (wd_hbm, wd_ref),
+        (wr_hbm, wr_ref),
+        (ws_hbm, ws_ref),
+        (wc_hbm, wc_ref.at[0:mel_rows]),
+        (wp_hbm, wp_ref),
+        (wk_hbm, wk_ref),
+    )
     loads = [
+        pltpu.make_async_copy(source, target, load_sem.at[4 + position])
+        for position, (source, target) in enumerate(weight_refs)
+    ]
+    frame_loads = [
         pltpu.make_async_copy(
             up_hbm.at[pl.ds(q * quarter * mel_rows, quarter * mel_rows), :],
             part_out.at[pl.ds(0, quarter * mel_rows), pl.ds(q * 2 * PIECE, 2 * PIECE)],
@@ -192,36 +228,41 @@
         )
         for q in range(4)
     ]
-    weight_refs = ((wd_hbm, wd_ref), (wr_hbm, wr_ref), (ws_hbm, ws_ref), (wp_hbm, wp_ref), (wk_hbm, wk_ref))
-    for position, (source, target) in enumerate(weight_refs):
-        loads.append(pltpu.make_async_copy(source, target, load_sem.at[4 + position]))
-    for load in loads[:5]:
+    for load in loads[:4] + frame_loads:
         load.start()
 
     @pl.when(is_first)
     def _():
-        @pl.loop(0, pieces)
+        @pl.loop(0, slots)
         def _(c):
             input_copy(c).start()
 
-    for load in loads[5:]:
+    for load in loads[4:]:
         load.start()
-    wc_ref[0:mel_rows] = wc_in[...]
     spare = lax.broadcasted_iota(jnp.int32, (EXT - mel_rows, 2 * half), 0)
     bias = jnp.broadcast_to(bias_in[...].astype(F32), (EXT - mel_rows, 2 * half))
     wc_ref[mel_rows:EXT] = jnp.where(spare == 0, bias, 0.0).astype(BF16)
-    wc_n[...] = jnp.transpose(wc_ref[...])
-
-    for load in loads[:4]:
+    loads[0].wait()
+    wd_t[...] = jnp.transpose(wd_ref[...])
+    for load in loads[1:]:
         load.wait()
-
-    @pl.loop(0, quarter)
-    def _(row):
+    wr_t[...] = jnp.transpose(wr_ref[...])
+    ws_t[...] = jnp.transpose(ws_ref[...])
+
+    for load in frame_loads:
+        load.wait()
+
+    @pl.loop(0, quarter // 4)
+    def _(group):
         for q in range(4):
-            matrix = part_out[pl.ds(pl.multiple_of(row * mel_rows, 16), mel_rows), q * 2 * PIECE : (q + 1) * 2 * PIECE]
-            frames = dot(mel_ref[...], matrix)
-            for h in range(2):
-                up_buf[h, pl.ds(q * quarter + row, micro, stride=mel_rows), :] = frames[:, h * PIECE : (h + 1) * PIECE]
+            for part in range(4):
+                row = group * 4 + part
+                lanes = slice(q * 2 * PIECE, (q + 1) * 2 * PIECE)
+                matrix = part_out[pl.ds(pl.multiple_of(row * mel_rows, 16), mel_rows), lanes]
+                frames = dot(mel_ref[...], matrix)
+                rows = pl.ds(q * quarter + row, micro, stride=mel_rows)
+                for h in range(2):
+                    up_buf[h, rows, :] = frames[:, h * PIECE : (h + 1) * PIECE]
 
     speaker_lane = lax.broadcasted_iota(jnp.int32, tab_ref.shape, 1)
     spare = lax.broadcasted_iota(jnp.int32, (EXT - mel_rows, PIECE), 0)
@@ -239,27 +280,19 @@
             rows = pl.ds(pl.multiple_of(m * mel_rows, 16), mel_rows)
             cond_ref[2 * m + h, 0:mel_rows, :] = (up_buf[h, rows, :] + speaker).astype(BF16)
             cond_ref[2 * m + h, mel_rows:EXT, :] = jnp.where(spare == 0, 1.0, 0.0).astype(BF16)
-
-    def prepare():
-        wd_t[...] = jnp.transpose(wd_ref[...])
-        wr_t[...] = jnp.transpose(wr_ref[...])
-        ws_t[...] = jnp.transpose(ws_ref[...])
+            cond_t[2 * m + h] = jnp.transpose(cond_ref[2 * m + h])
+
+    @pl.when(s > 0)
+    def _():
         acc[...] = jnp.zeros_like(acc)
-
-    for load in loads[4:]:
-        load.wait()
-
-    pl.semaphore_wait(barrier, expected)
-
-    @pl.when(s > 0)
-    def _():
-        prepare()
 
     @pl.when(is_last)
     def _():
         wp_t[...] = jnp.transpose(wp_ref[...])
         wk_t[...] = jnp.transpose(wk_ref[...])
         gx_buf[...] = jnp.zeros_like(gx_buf)
+
+    pl.semaphore_wait(barrier, expected)
 
     def remote(src, dst, send_sem, recv_sem, dev_s, dev_z):
         return pltpu.make_async_remote_copy(
@@ -271,52 +304,91 @@
             device_id_type=MESH,
         )
 
+    ring = pieces > slots
+
+    def send_of(semaphores, slot):
+        return semaphores.at[slot if ring else 0]
+
     def x_copy(c):
         slot = lax.rem(c, slots)
-        return remote(x_out.at[slot], x_buf.at[c], x_ss.at[slot], x_rs.at[c], s + 1, z)
+        return remote(x_out.at[slot], x_buf.at[c], send_of(x_ss, slot), x_rs.at[c], s + 1, z)
 
     def k_copy(c):
         slot = lax.rem(c, slots)
-        return remote(k_out.at[slot], sg_buf.at[c], k_ss.at[slot], k_rs.at[c], s + 1, z)
-
-    def gs_copy(c):
-        return remote(sg_buf.at[c], sg_buf.at[c], gs_ss.at[c], gs_rs.at[c], s - 1, z)
+        return remote(k_out.at[slot], sg_buf.at[c], send_of(k_ss, slot), k_rs.at[c], s + 1, z)
 
     def gx_copy(c):
         slot = lax.rem(c, slots)
-        return remote(gx_out.at[slot], gx_buf.at[c], gx_ss.at[slot], gx_rs.at[c], s - 1, z)
+        return remote(gx_out.at[slot], gx_buf.at[c], send_of(gx_ss, slot), gx_rs.at[c], s - 1, z)
 
     def gc_copy(c):
         slot = lax.rem(c, slots)
-        return remote(gc_out.at[slot], gc_buf.at[c], gc_ss.at[slot], gc_rs.at[c], s - 1, z)
+        return remote(gc_out.at[slot], gc_buf.at[c], send_of(gc_ss, slot), gc_rs.at[c], s - 1, z)
 
     def reuse(copy, c):
-        if pieces > slots:
+        if ring:
 
             @pl.when(c >= slots)
             def _():
                 copy(c).wait_send()
 
+    def drain(copy, whole):
+        if ring:
+
+            @pl.loop(0, slots)
+            def _(c):
+                copy(c).wait_send()
+
+        else:
+            whole().wait_send()
+
+    chips = sections // 2
+    far_chips = range(chips - 2, 0, -1)
+
+    def gs_copy(c):
+        return remote(sg_buf.at[c], sg_buf.at[c], gs_ss.at[0], gs_rs.at[c], s - 1, z)
+
+    def gs_first(c):
+        return remote(sg_buf.at[c], sg_buf.at[c], gs_ss.at[1], gs_rs.at[c], 1, z)
+
+    def gs_chip(c, chip):
+        return remote(sg_buf.at[c], sg_buf.at[c], gs_ss.at[1 + chip], gs_rs.at[c], 2 * chip + 1, z)
+
+    def gs_whole(position):
+        return remote(sg_buf, sg_buf, gs_ss.at[position], gs_rs.at[0], s - 1, z)
+
     def build_shift(m):
         dilation = dil_ref[0]
         middle = offs_ref[0, m]
-        source = lax.broadcasted_iota(jnp.int32, (2 * PIECE, 2 * PIECE), 0)
-        target = lax.broadcasted_iota(jnp.int32, (2 * PIECE, 2 * PIECE), 1)
-        start = jnp.where(target >= middle, middle, 0)
-        hit = (source == target - dilation) & (source >= start)
-        shift_buf[...] = jnp.where(hit, 1.0, 0.0).astype(BF16)
-
-    def columns(ref, first, parts):
-        return jnp.concatenate([ref[first + h] for h in parts], axis=1)
+        shape = (2 * PIECE, 2 * PIECE)
+
+        def matrix(source, target):
+            start = jnp.where(target >= middle, middle, 0)
+            hit = (source == target - dilation) & (source >= start)
+            return jnp.where(hit, 1.0, 0.0).astype(BF16)
+
+        rows = lax.broadcasted_iota(jnp.int32, shape, 0)
+        lanes = lax.broadcasted_iota(jnp.int32, shape, 1)
+        shift_buf[...] = matrix(lanes, rows)
+        shift_back[...] = matrix(rows, lanes)
+
+    def pair(ref, first):
+        return jnp.concatenate([ref[first], ref[first + 1]], axis=1)
+
+    def put_pair(ref, first, value):
+        for h in range(2):
+            ref[first + h] = value[:, h * PIECE : (h + 1) * PIECE]
+
+    def both(ref, first, parts):
+        return jnp.concatenate([ref[first + h] for h in parts], axis=0)
 
     def put(ref, first, parts, value):
         for position, h in enumerate(parts):
-            ref[first + h] = value[:, position * PIECE : (position + 1) * PIECE]
+            ref[first + h] = value[position * PIECE : (position + 1) * PIECE]
 
     def head(m, total):
-        parts = (0, 1)
         width = 2 * PIECE
-        total = total.astype(BF16).astype(F32) * head_scale
+        total = jnp.transpose(total.astype(BF16)).astype(F32) * head_scale
         sig_1 = sigmoid(total)
         act_1 = (total * sig_1).astype(BF16)
         slope_1 = sig_1 * (1.0 + total * (1.0 - sig_1)) * head_scale
@@ -341,14 +413,19 @@
         grad_logits = (weight * (expo / denominator - jnp.where(hit, 1.0, 0.0))).astype(BF16)
         grad_post = (dot(wk_t[...], grad_logits) * slope_2).astype(BF16)
         grad_total = (dot(wp_t[...], grad_post) * slope_1).astype(BF16)
-        put(sg_buf, 2 * m, parts, grad_total)
+        put(sg_buf, 2 * m, (0, 1), jnp.transpose(grad_total))
         for h in (1, 0):
-            gs_copy(2 * m + h).start()
+            c = 2 * m + h
+            for chip in far_chips:
+                gs_chip(c, chip).start()
+            gs_copy(c).start()
+            if feeder == sections - 1:
+                gs_first(c).start()
         kept = 2 * lax.rem(m, keep)
-        put(gl_buf, kept, parts, grad_logits)
-        put(a2_buf, kept, parts, act_2)
-        put(gp_buf, kept, parts, grad_post)
-        put(a1_buf, kept, parts, act_1)
+        put_pair(gl_buf, kept, grad_logits)
+        put_pair(a2_buf, kept, act_2)
+        put_pair(gp_buf, kept, grad_post)
+        put_pair(a1_buf, kept, act_1)
         loss_row = weight * (top + jnp.log(denominator) - picked)
         high = loss_row.astype(BF16)
         rest = loss_row - high.astype(F32)
@@ -358,40 +435,49 @@
         message = jnp.where(row == mel_rows + 2, high.astype(F32), 0.0)
         message = jnp.where(row == mel_rows + 3, middle.astype(F32), message)
         message = jnp.where(row == mel_rows + 4, low.astype(F32), message)
-        put(gc_buf, 2 * m, parts, message.astype(BF16))
+        put_pair(gc_buf, 2 * m, message.astype(BF16))
 
     def forward(m, parts):
-        wide = pl.ds(0, len(parts) * PIECE)
+        high = len(parts) * PIECE
         for h in parts:
             c = 2 * m + h
 
             @pl.when(is_first)
             def _():
                 input_copy(c).wait()
+                x_buf[c] = jnp.transpose(inp_buf[lax.rem(c, slots)])
+                if ring:
+
+                    @pl.when(c + slots < pieces)
+                    def _():
+                        input_copy(c + slots).start()
 
             @pl.when(s > 0)
             def _():
                 x_copy(c).wait_recv()
 
-        x = columns(x_buf, 2 * m, parts)
+        x = both(x_buf, 2 * m, parts)
         if parts == (0,):
-            prev = dot(x, shift_buf[0:PIECE, 0:PIECE])
+            prev = dot(shift_buf[0:PIECE, 0:PIECE], x)
         elif parts == (1,):
-            prev = dot(columns(x_buf, 2 * m, (0, 1)), shift_buf[:, PIECE : 2 * PIECE])
+            prev = dot(shift_buf[PIECE : 2 * PIECE, :], both(x_buf, 2 * m, (0, 1)))
         else:
-            prev = dot(x, shift_buf[...])
-        stack = jnp.concatenate([prev.astype(BF16), x], axis=0)
-        gate = dot(wd_ref[...], stack) + dot(wc_n[...], columns(cond_ref, 2 * m, parts))
-        th = jnp.tanh(gate[0:half])
-        sg = sigmoid(gate[half : 2 * half])
-        gate_buf[0:half, wide] = th
-        gate_buf[half : 2 * half, wide] = sg
+            prev = dot(shift_buf[...], x)
+        gate = (
+            dot(x, wd_t[res : 2 * res])
+            + dot(both(cond_t, 2 * m, parts), wc_ref[...])
+            + dot(prev.astype(BF16), wd_t[0:res])
+        )
+        th = jnp.tanh(gate[:, 0:half])
+        sg = sigmoid(gate[:, half : 2 * half])
+        gate_buf[0:high, 0:half] = th
+        gate_buf[0:high, half : 2 * half] = sg
         put(hid_buf, 2 * m, parts, (th * sg).astype(BF16))
 
     def forward_rest(m, parts):
-        wide = pl.ds(0, len(parts) * PIECE)
-        th = gate_buf[0:half, wide]
-        sg = gate_buf[half : 2 * half, wide]
+        high = len(parts) * PIECE
+        th = gate_buf[0:high, 0:half]
+        sg = gate_buf[0:high, half : 2 * half]
         put(d1_buf, 2 * m, parts, (sg * (1.0 - th * th)).astype(BF16))
         put(d2_buf, 2 * m, parts, (th * sg * (1.0 - sg)).astype(BF16))
 
@@ -399,65 +485,70 @@
         c = 2 * m + h
         forward(m, (h,))
         reuse(x_copy, c)
-        out = (x_buf[c].astype(F32) + dot(wr_ref[...], hid_buf[c])) * HALF_ROOT
+        out = (x_buf[c].astype(F32) + dot(hid_buf[c], wr_t[...])) * HALF_ROOT
         x_out[lax.rem(c, slots)] = out.astype(BF16)
         x_copy(c).start()
-        gh_buf[:, 0:PIECE] = dot(ws_ref[...], hid_buf[c])
+        gh_buf[...] = dot(hid_buf[c], ws_t[...])
         forward_rest(m, (h,))
 
         @pl.when(s > 0)
         def _():
             k_copy(c).wait_recv()
-            gh_buf[:, 0:PIECE] += sg_buf[c].astype(F32)
+            gh_buf[...] += sg_buf[c].astype(F32)
 
         reuse(k_copy, c)
-        k_out[lax.rem(c, slots)] = gh_buf[:, 0:PIECE].astype(BF16)
+        k_out[lax.rem(c, slots)] = gh_buf[...].astype(BF16)
         k_copy(c).start()
 
     def forward_head(m):
         forward(m, (0, 1))
-        total = dot(ws_ref[...], columns(hid_buf, 2 * m, (0, 1)))
+        total = dot(both(hid_buf, 2 * m, (0, 1)), ws_t[...])
         for h in (0, 1):
             k_copy(2 * m + h).wait_recv()
-        head(m, total + columns(sg_buf, 2 * m, (0, 1)).astype(F32))
+        head(m, total + both(sg_buf, 2 * m, (0, 1)).astype(F32))
         forward_rest(m, (0, 1))
 
     def grad_field(m, parts, grad_hidden):
         kept = 2 * lax.rem(m, keep)
         grad_gate = jnp.concatenate(
             [
-                grad_hidden * columns(d1_buf, 2 * m, parts).astype(F32),
-                grad_hidden * columns(d2_buf, 2 * m, parts).astype(F32),
+                grad_hidden * both(d1_buf, 2 * m, parts).astype(F32),
+                grad_hidden * both(d2_buf, 2 * m, parts).astype(F32),
             ],
-            axis=0,
+            axis=1,
         ).astype(BF16)
         put(gg_buf, kept, parts, grad_gate)
         if parts == (1,):
-            back = dot_nt(grad_gate, shift_buf[PIECE:, PIECE:])
+            back = dot(shift_back[PIECE:, PIECE:], grad_gate)
         elif parts == (0,):
-            both = jnp.concatenate([grad_gate, gg_buf[kept + 1]], axis=1)
-            back = dot_nt(both, shift_buf[0:PIECE, :])
+            back = dot(shift_back[0:PIECE, :], jnp.concatenate([grad_gate, gg_buf[kept + 1]], axis=0))
         else:
-            back = dot_nt(grad_gate, shift_buf[...])
-        return dot(wd_t[res : 2 * res], grad_gate) + dot(wd_t[0:res], back.astype(BF16))
-
-    def cond_message(m, parts):
+            back = dot(shift_back[...], grad_gate)
+        return dot(grad_gate, wd_ref[:, res : 2 * res]) + dot(back.astype(BF16), wd_ref[:, 0:res])
+
+    def cond_message(m, h):
         kept = 2 * lax.rem(m, keep)
-        row = lax.broadcasted_iota(jnp.int32, (EXT, len(parts) * PIECE), 0)
-        own = jnp.where(row < mel_rows, dot(wc_ref[...], columns(gg_buf, kept, parts)), 0.0)
-        return own + columns(gc_buf, 2 * m, parts).astype(F32)
+        row = lax.broadcasted_iota(jnp.int32, (EXT, PIECE), 0)
+        own = jnp.where(row < mel_rows, dot_nt(wc_ref[...], gg_buf[kept + h]), 0.0)
+        return own + gc_buf[2 * m + h].astype(F32)
 
     def backward_piece(m, h):
         c = 2 * m + h
         gs_copy(c).wait_recv()
 
-        @pl.when(s > 0)
+        @pl.when(lax.rem(s, 2) == 1)
         def _():
             gs_copy(c).start()
 
-        gh_buf[:, 0:PIECE] = dot(ws_t[...], sg_buf[c])
+        if feeder < sections - 1:
+
+            @pl.when(s == feeder)
+            def _():
+                gs_first(c).start()
+
+        gh_buf[...] = dot(sg_buf[c], ws_ref[...])
         gx_copy(c).wait_recv()
-        grad_hidden = gh_buf[:, 0:PIECE] + HALF_ROOT * dot(wr_t[...], gx_buf[c])
+        grad_hidden = gh_buf[...] + HALF_ROOT * dot(gx_buf[c], wr_ref[...])
         grad_x = (HALF_ROOT * gx_buf[c].astype(F32) + grad_field(m, (h,), grad_hidden)).astype(BF16)
 
         @pl.when(s > 0)
@@ -466,8 +557,12 @@
             gx_out[lax.rem(c, slots)] = grad_x
             gx_copy(c).start()
 
+        @pl.when(is_first)
+        def _():
+            inp_buf[lax.rem(c, slots)] = jnp.transpose(grad_x)
+
         gc_copy(c).wait_recv()
-        message = cond_message(m, (h,))
+        message = cond_message(m, h)
 
         @pl.when(s > 0)
         def _():
@@ -477,7 +572,6 @@
 
         @pl.when(is_first)
         def _():
-            d1_buf[c] = grad_x
             gc_buf[c, 0:mel_rows, :] = message[0:mel_rows].astype(BF16)
             tail = message[mel_rows:EXT]
             if h == 0:
@@ -494,19 +588,17 @@
             gc_buf[c, mel_rows:EXT, :] = tail.astype(BF16)
 
     def backward_pair(m):
-        parts = (0, 1)
-        grad_hidden = dot(ws_t[...], columns(sg_buf, 2 * m, parts))
-        grad_x = grad_field(m, parts, grad_hidden).astype(BF16)
+        grad_hidden = dot(both(sg_buf, 2 * m, (0, 1)), ws_ref[...])
+        grad_x = grad_field(m, (0, 1), grad_hidden).astype(BF16)
         for h in (1, 0):
             c = 2 * m + h
             reuse(gx_copy, c)
-            gx_out[lax.rem(c, slots)] = grad_x[:, h * PIECE : (h + 1) * PIECE]
+            gx_out[lax.rem(c, slots)] = grad_x[h * PIECE : (h + 1) * PIECE]
             gx_copy(c).start()
-        message = cond_message(m, parts).astype(BF16)
         for h in (1, 0):
             c = 2 * m + h
             reuse(gc_copy, c)
-            gc_out[lax.rem(c, slots)] = message[:, h * PIECE : (h + 1) * PIECE]
+            gc_out[lax.rem(c, slots)] = cond_message(m, h).astype(BF16)
             gc_copy(c).start()
 
     def add_halves(first_row, value):
@@ -517,27 +609,49 @@
     def weight_gradients(m):
         parts = (0, 1)
         kept = 2 * lax.rem(m, keep)
-        grad_gate = columns(gg_buf, kept, parts)
-        x = columns(x_buf, 2 * m, parts)
-        prev = dot(x, shift_buf[...]).astype(BF16)
-        acc[0 : 2 * half, 0:res] += dot_nt(grad_gate, prev)
-        acc[0 : 2 * half, res : 2 * res] += dot_nt(grad_gate, x)
-        acc[2 * half : 2 * half + EXT, :] += dot_nt(columns(cond_ref, 2 * m, parts), grad_gate)
-        hidden = columns(hid_buf, 2 * m, parts)
+        grad_gate = both(gg_buf, kept, parts)
+        x = both(x_buf, 2 * m, parts)
+        prev = dot(shift_buf[...], x).astype(BF16)
+        acc[0 : 2 * half, :] += dot_tn(grad_gate, jnp.concatenate([prev, x], axis=1))
+        acc[2 * half : 2 * half + EXT, :] += dot(pair(cond_ref, 2 * m), grad_gate)
+        hidden = both(hid_buf, 2 * m, parts)
         row = 2 * half + EXT
 
         @pl.when(s < sections - 1)
         def _():
-            add_halves(row, HALF_ROOT * dot_nt(columns(gx_buf, 2 * m, parts), hidden))
-
-        add_halves(row + half // 2, dot_nt(columns(sg_buf, 2 * m, parts), hidden))
+            add_halves(row, HALF_ROOT * dot_tn(both(gx_buf, 2 * m, parts), hidden))
+
+        add_halves(row + half // 2, dot_tn(both(sg_buf, 2 * m, parts), hidden))
 
         @pl.when(is_last)
         def _():
-            add_halves(main_rows, dot_nt(columns(gp_buf, kept, parts), columns(a1_buf, kept, parts)))
-            add_halves(main_rows + half // 2, dot_nt(columns(gl_buf, kept, parts), columns(a2_buf, kept, parts)))
-
-    late = keep == micro
+            add_halves(main_rows, dot_nt(pair(gp_buf, kept), pair(a1_buf, kept)))
+            add_halves(main_rows + half // 2, dot_nt(pair(gl_buf, kept), pair(a2_buf, kept)))
+
+    def gin_rows(other, group):
+        return remote(
+            inp_buf.at[:, pl.ds(pl.multiple_of(other * share, share), share), :],
+            gin_buf.at[pl.ds(pl.multiple_of(group * slots, slots), slots)],
+            gin_ss.at[0],
+            gin_rs.at[0],
+            other,
+            z,
+        )
+
+    def gin_sent():
+        return remote(
+            inp_buf.at[:, share:res, :], inp_buf.at[:, share:res, :], gin_ss.at[0], gin_rs.at[0], 1, z
+        )
+
+    def gin_arrived():
+        return remote(gin_buf, gin_buf, gin_ss.at[0], gin_rs.at[0], 1, z)
+
+    def hand_out(group):
+        @pl.loop(1, sections)
+        def _(other):
+            gin_rows(other, group).start()
+
+        gin_buf[pl.ds(pl.multiple_of(group * slots, slots), slots)] = inp_buf[:, 0:share, :]
 
     @pl.when(is_last)
     def _():
@@ -546,7 +660,7 @@
             build_shift(m)
             forward_head(m)
             backward_pair(m)
-            if not late:
+            if keep < micro:
                 weight_gradients(m)
 
     @pl.when(jnp.logical_not(is_last))
@@ -559,35 +673,35 @@
 
         @pl.when(is_first)
         def _():
-            prepare()
+            acc[...] = jnp.zeros_like(acc)
             extra_buf[...] = jnp.zeros_like(extra_buf)
 
-    @pl.loop(0, micro)
-    def _(m):
+    late = (s >= sections // 2) if keep == micro else is_last
+
+    @pl.loop(0, 2 * micro)
+    def _(step):
+        m = jnp.where(late, lax.rem(step, micro), step // 2)
+        is_back = jnp.where(late, step < micro, lax.rem(step, 2) == 0)
         build_shift(m)
 
-        @pl.when(jnp.logical_not(is_last))
-        def _():
+        @pl.when(is_back & jnp.logical_not(is_last))
+        def _():
+            if ring:
+
+                @pl.when(is_first & (m > 0))
+                def _():
+                    gin_sent().wait_send()
+
             backward_piece(m, 1)
             backward_piece(m, 0)
 
-        if late:
+            @pl.when(is_first & (lax.rem(2 * m + 2, slots) == 0))
+            def _():
+                hand_out((2 * m + 2) // slots - 1)
+
+        @pl.when(jnp.logical_not(is_back) & ((keep == micro) | jnp.logical_not(is_last)))
+        def _():
             weight_gradients(m)
-        else:
-
-            @pl.when(jnp.logical_not(is_last))
-            def _():
-                weight_gradients(m)
-
-    def gin_copy(other):
-        return remote(
-            d1_buf.at[:, pl.ds(pl.multiple_of(other * share, share), share), :],
-            gin_buf,
-            gin_ss.at[other],
-            gin_rs.at[0],
-            other,
-            z,
-        )
 
     def own_local():
         return pltpu.make_async_copy(gc_buf, o_g.at[z], loc_sem.at[0])
@@ -618,12 +732,6 @@
         own_local().start()
         own_hub().start()
         own_local().wait()
-
-        @pl.loop(1, sections)
-        def _(other):
-            gin_copy(other).start()
-
-        gin_buf[...] = d1_buf[:, 0:share, :]
 
     left = z < groups // 2
     inward = jnp.where(left, z + 1, z - 1)
@@ -631,7 +739,7 @@
     is_edge = (z == 0) | (z == groups - 1)
     is_mid = (z == groups // 2 - 1) | (z == groups // 2)
     distance = jnp.where(left, groups // 2 - 1 - z, z - groups // 2)
-    lag = LAG * (2 * distance + 1)
+    lag = LAG * (2 * distance + 1) + 4 * distance
     count = jnp.where(is_last, main_blocks + head_blocks, main_blocks)
 
     def block_of(i):
@@ -640,21 +748,26 @@
     def rows_of(b):
         return pl.ds(pl.multiple_of(b * BLOCK, BLOCK), BLOCK)
 
-    def swap_copy(b):
-        return remote(part_out.at[rows_of(b)], o_acc.at[rows_of(b)], zi_ss.at[b], zt_rs.at[b], s, inward)
-
-    def part_copy(b):
-        return remote(part_out.at[rows_of(b)], part_in.at[rows_of(b)], zi_ss.at[b], zp_rs.at[b], s, inward)
-
-    def total_copy(b):
-        return remote(o_acc.at[rows_of(b)], o_acc.at[rows_of(b)], zo_ss.at[b], zt_rs.at[b], s, outward)
+    cycle = zp_rs.shape[0]
+
+    def swap_copy(i):
+        rows = rows_of(block_of(i))
+        return remote(part_out.at[rows], o_acc.at[rows], zi_ss.at[0], zt_rs.at[lax.rem(i, cycle)], s, inward)
+
+    def part_copy(i):
+        rows = rows_of(block_of(i))
+        return remote(part_out.at[rows], part_in.at[rows], zi_ss.at[0], zp_rs.at[lax.rem(i, cycle)], s, inward)
+
+    def total_copy(i):
+        rows = rows_of(block_of(i))
+        return remote(o_acc.at[rows], o_acc.at[rows], zo_ss.at[0], zt_rs.at[lax.rem(i, cycle)], s, outward)
 
     def head_copy(j):
         rows = rows_of(main_blocks + j)
-        return remote(o_acc.at[rows], o_acc.at[rows], hd_ss.at[j], hd_rs.at[j], s - 1, z)
-
-    def send_part(b):
-        rows = rows_of(b)
+        return remote(o_acc.at[rows], o_acc.at[rows], hd_ss.at[0], hd_rs.at[j], s - 1, z)
+
+    def send_part(i):
+        rows = rows_of(block_of(i))
 
         @pl.when(is_edge)
         def _():
@@ -662,20 +775,20 @@
 
         @pl.when(jnp.logical_not(is_edge))
         def _():
-            part_copy(b).wait_recv()
+            part_copy(i).wait_recv()
             part_out[rows, :] = (acc[rows, :] + part_in[rows, :].astype(F32)).astype(BF16)
 
         @pl.when(is_mid)
         def _():
-            swap_copy(b).start()
+            swap_copy(i).start()
 
         @pl.when(jnp.logical_not(is_mid))
         def _():
-            part_copy(b).start()
-
-    def finish_part(b):
-        rows = rows_of(b)
-        swap_copy(b).wait_recv()
+            part_copy(i).start()
+
+    def finish_part(i):
+        rows = rows_of(block_of(i))
+        swap_copy(i).wait_recv()
 
         @pl.when(is_mid)
         def _():
@@ -683,24 +796,24 @@
 
         @pl.when(jnp.logical_not(is_edge))
         def _():
-            total_copy(b).start()
+            total_copy(i).start()
 
     last_step = main_blocks + lag - 1
     head_at = lag + 2
-    own_at = jnp.minimum(9 + 6 * distance, last_step)
-    rest_at = jnp.where(is_first, 20, jnp.where(is_hub, 17, jnp.where(s < sections // 2 + 2, 28, 31)))
-    rest_at = jnp.minimum(rest_at + 6 * distance, last_step)
+    own_at = jnp.minimum(12 + 9 * distance, last_step)
+    rest_at = jnp.where(is_first, 32, jnp.where(is_hub, 27, jnp.where(s < sections // 2 + 2, 46, 51)))
+    rest_at = jnp.minimum(rest_at + 9 * distance, last_step)
 
     @pl.loop(0, count + lag)
     def _(i):
         @pl.when(i < count)
         def _():
-            send_part(block_of(i))
+            send_part(i)
 
         @pl.when(i >= lag)
         def _():
+            finish_part(i - lag)
             b = block_of(i - lag)
-            finish_part(b)
 
             @pl.when(b >= main_blocks)
             def _():
@@ -744,7 +857,7 @@
 
     @pl.when(s > 0)
     def _():
-        gin_copy(0).wait_recv()
+        gin_arrived().wait_recv()
 
     for c in range(pieces):
         o_gin[:, c * PIECE : (c + 1) * PIECE] = gin_buf[c]
@@ -752,10 +865,7 @@
     @pl.when(is_first)
     def _():
         own_hub().wait_send()
-
-        @pl.loop(1, sections)
-        def _(other):
-            gin_copy(other).wait_send()
+        gin_sent().wait_send()
 
     @pl.when(is_hub)
     def _():
@@ -781,44 +891,48 @@
         def _():
             part_next(j).wait_recv()
 
+    def sum_sent(rows):
+        remote(part_out.at[rows], part_out.at[rows], zi_ss.at[0], zp_rs.at[0], s, inward).wait_send()
+
+        @pl.when(jnp.logical_not(is_edge))
+        def _():
+            remote(o_acc.at[rows], o_acc.at[rows], zo_ss.at[0], zt_rs.at[0], s, outward).wait_send()
+
+    @pl.when(is_last)
+    def _():
+        sum_sent(pl.ds(0, main_rows + head_rows))
+
+    @pl.when(jnp.logical_not(is_last))
+    def _():
+        sum_sent(pl.ds(0, main_rows))
+        drain(x_copy, lambda: remote(x_out, x_out, x_ss.at[0], x_rs.at[0], s + 1, z))
+        drain(k_copy, lambda: remote(k_out, k_out, k_ss.at[0], k_rs.at[0], s + 1, z))
+
     @pl.when(s > 0)
     def _():
-        @pl.loop(0, head_blocks)
-        def _(j):
-            head_copy(j).wait_send()
-
-    @pl.loop(0, count)
-    def _(b):
-        part_copy(b).wait_send()
-
-        @pl.when(jnp.logical_not(is_edge))
-        def _():
-            total_copy(b).wait_send()
-
-    @pl.loop(0, slots)
-    def _(c):
-        @pl.when(s < sections - 1)
-        def _():
-            x_copy(c).wait_send()
-            k_copy(c).wait_send()
-
-        @pl.when(s > 0)
-        def _():
-            gx_copy(c).wait_send()
-            gc_copy(c).wait_send()
-
-    @pl.when(s > 0)
-    def _():
-        @pl.loop(0, pieces)
-        def _(c):
-            gs_copy(c).wait_send()
+        rows = pl.ds(main_rows, head_rows)
+        remote(o_acc.at[rows], o_acc.at[rows], hd_ss.at[0], hd_rs.at[0], s - 1, z).wait_send()
+        drain(gx_copy, lambda: remote(gx_out, gx_out, gx_ss.at[0], gx_rs.at[0], s - 1, z))
+        drain(gc_copy, lambda: remote(gc_out, gc_out, gc_ss.at[0], gc_rs.at[0], s - 1, z))
+
+    @pl.when(lax.rem(s, 2) == 1)
+    def _():
+        gs_whole(0).wait_send()
+
+    @pl.when(is_last)
+    def _():
+        for chip in far_chips:
+            gs_whole(1 + chip).wait_send()
+
+    @pl.when(s == feeder)
+    def _():
+        gs_whole(1).wait_send()
 
 
 def run_step(dims, tables, arrays, weights):
     sections, groups, micro, res, half, classes, slots, keep, mel_rows = dims
     pieces = 2 * micro
     rows = 2 * half + EXT + half + half // 2 + classes // 2
-    blocks = rows // BLOCK
     head_blocks = (half // 2 + classes // 2) // BLOCK
     share = res // sections
     smem = pl.BlockSpec(memory_space=pltpu.SMEM)
@@ -829,30 +943,36 @@
     def tile(*shape, dtype=BF16):
         return pltpu.VMEM(shape, dtype)
 
+    distance = groups // 2 - 1
+    cycle = max(LAG * (2 * distance + 1) + 4 * distance + 4, 2 * LAG + 4)
+    sends = slots if pieces > slots else 1
+
     scratch = [
-        tile(pieces, res, PIECE),
-        tile(pieces, half, PIECE),
-        tile(pieces, res, PIECE),
+        tile(pieces, PIECE, res),
+        tile(pieces, PIECE, half),
+        tile(pieces, PIECE, res),
         tile(pieces, EXT, PIECE),
-        tile(pieces, half, PIECE),
-        tile(pieces, half, PIECE),
-        tile(pieces, half, PIECE),
+        tile(pieces, PIECE, half),
+        tile(pieces, PIECE, half),
+        tile(pieces, PIECE, half),
+        tile(slots, PIECE, res),
+        tile(slots, PIECE, half),
+        tile(slots, PIECE, res),
+        tile(slots, EXT, PIECE),
+        tile(2 * PIECE, 2 * half, dtype=F32),
+        tile(PIECE, half, dtype=F32),
+        tile(2 * keep, PIECE, 2 * half),
         tile(slots, res, PIECE),
-        tile(slots, half, PIECE),
-        tile(slots, res, PIECE),
-        tile(slots, EXT, PIECE),
-        tile(2 * half, 2 * PIECE, dtype=F32),
-        tile(half, PIECE, dtype=F32),
-        tile(2 * keep, 2 * half, PIECE),
+        tile(2 * PIECE, 2 * PIECE),
         tile(2 * PIECE, 2 * PIECE),
         tile(pieces, EXT, PIECE),
+        tile(pieces, PIECE, EXT),
         tile(EXT, 2 * half),
         tile(2 * half, 2 * res),
         tile(res, half),
         tile(half, half),
         tile(half, half),
         tile(classes, half),
-        tile(2 * half, EXT),
         tile(2 * res, 2 * half),
         tile(half, res),
         tile(half, half),
@@ -868,31 +988,31 @@
         tile(pieces, share, PIECE),
         tile(2, micro * mel_rows, PIECE, dtype=F32),
         tile(EXT - mel_rows, PIECE, dtype=F32),
+        dma((slots,)),
+        dma((10,)),
+        dma((1,)),
+        dma((sends,)),
         dma((pieces,)),
-        dma((9,)),
+        dma((sends,)),
+        dma((pieces,)),
+        dma((max(2, sections // 2),)),
+        dma((pieces,)),
+        dma((sends,)),
+        dma((pieces,)),
+        dma((sends,)),
+        dma((pieces,)),
         dma((1,)),
-        dma((slots,)),
-        dma((pieces,)),
-        dma((slots,)),
-        dma((pieces,)),
-        dma((pieces,)),
-        dma((pieces,)),
-        dma((slots,)),
-        dma((pieces,)),
-        dma((slots,)),
-        dma((pieces,)),
-        dma((blocks,)),
-        dma((blocks,)),
-        dma((blocks,)),
-        dma((blocks,)),
-        dma((head_blocks,)),
+        dma((1,)),
+        dma((cycle,)),
+        dma((cycle,)),
+        dma((1,)),
         dma((head_blocks,)),
         dma((groups,)),
         dma((1,)),
         dma((groups,)),
         dma((groups, sections // 2)),
         dma((groups,)),
-        dma((sections,)),
+        dma((1,)),
         dma((1,)),
     ]
     return pl.pallas_call(
@@ -902,7 +1022,7 @@
             jax.ShapeDtypeStruct((groups, pieces, EXT, PIECE), BF16),
             jax.ShapeDtypeStruct((share, pieces * PIECE), BF16),
         ),
-        in_specs=[smem] * 4 + [vmem] * 5 + [anywhere] * 7,
+        in_specs=[smem] * 4 + [vmem] * 4 + [anywhere] * 8,
         out_specs=(vmem, anywhere, vmem),
         scratch_shapes=scratch,
         compiler_params=pltpu.CompilerParams(
@@ -914,7 +1034,7 @@
 
 
 def finish_kernel(
-    dims, steps, dil, cond, res, skip, post, out, shared, o_dil, o_cond, o_bias, o_res, o_skip, o_post, o_out,
+    dims, steps, dil, cond, res, skip, post, out, gin, shared, o_gin, o_dil, o_cond, o_bias, o_res, o_skip, o_post, o_out,
     o_up, o_table, o_loss, field, mel_rows_buf, mel_columns, table,
 ):
     mel_rows, half = dims
@@ -951,6 +1071,7 @@
         o_table[...] = table[:, 0 : o_table.shape[1]]
         mel_columns[...] = jnp.transpose(mel_rows_buf[...])[0:mel_rows].astype(BF16)
 
+    o_gin[...] = gin[...]
     o_dil[0] = dil[...].astype(F32)
     for source, target in ((res, o_res), (skip, o_skip), (post, o_post), (out, o_out)):
         target[0] = source[:, 0:half].astype(F32)
@@ -971,7 +1092,7 @@
         o_up[j] = dot(mel_columns[...], matrix.astype(BF16))
 
 
-def finish(sums, shared, half, classes, mel_rows, speakers):
+def finish(sums, shared, grad_inputs, half, classes, mel_rows, speakers):
     steps = 8
     frames = shared.shape[0]
     first = 2 * half
@@ -997,6 +1118,7 @@
         functools.partial(finish_kernel, (mel_rows, half), steps),
         grid=(steps,),
         out_shape=(
+            jax.ShapeDtypeStruct(grad_inputs.shape, grad_inputs.dtype),
             f32(1, first, WIDE),
             f32(mel_rows, WIDE),
             f32(1, WIDE),
@@ -1015,9 +1137,11 @@
             strip(small, lambda i: (res_at + per + i, 0)),
             strip(small, lambda i: (res_at + 2 * per + i, 0)),
             strip(last, lambda i: ((first + EXT + half + half // 2) // last + i, 0)),
+            pl.BlockSpec((grad_inputs.shape[0], grad_inputs.shape[1] // steps), lambda i: (0, i)),
             pl.BlockSpec(memory_space=pltpu.VMEM),
         ],
         out_specs=(
+            pl.BlockSpec((grad_inputs.shape[0], grad_inputs.shape[1] // steps), lambda i: (0, i)),
             pl.BlockSpec((1, first // steps, WIDE), lambda i: (0, i, 0)),
             strip(16, lambda i: (jnp.minimum(i, rows - 1), 0)),
             fixed(1, WIDE),
@@ -1036,10 +1160,10 @@
             pltpu.VMEM((mel_rows, PIECE), F32),
         ],
         compiler_params=pltpu.CompilerParams(
-            vmem_limit_bytes=48 * 2**20, dimension_semantics=("arbitrary",)
+            vmem_limit_bytes=62 * 2**20, dimension_semantics=("arbitrary",)
         ),
         name="finish",
-    )(sums, sums, sums, sums, sums, sums, shared)
+    )(sums, sums, sums, sums, sums, sums, grad_inputs, shared)
 
 
 def local(
@@ -1081,12 +1205,12 @@
             targets.reshape(micro, 1, length),
             mel.T,
             speaker_table,
-            conditioning_projection[0].T,
             dilated_gate_bias,
         ),
         (
             inputs,
             upsample_weight.transpose(1, 2, 0).reshape(mel_rows * mel_rows, hop),
+            conditioning_projection[0].T,
             dilated_kernel[0],
             residual_projection[0],
             skip_projection[0],
@@ -1095,8 +1219,8 @@
         ),
     )
     shared = shared.reshape(groups * micro, 2, EXT, PIECE)
-    dil, cond, bias, grad_res, grad_skip, post, out, up, table, loss = finish(
-        sums, shared, half, classes, mel_rows, speaker_table.shape[1]
+    grad_inputs, dil, cond, bias, grad_res, grad_skip, post, out, up, table, loss = finish(
+        sums, shared, grad_inputs, half, classes, mel_rows, speaker_table.shape[1]
     )
     return (
         loss.reshape(()),

time: 209 us -> 193 us (0.923)
  Pallas kernels: 204 us -> 191 us
  local copies, waits for them, and re-layouts: 3.95 us -> 0 us
    pallas_call x1, Pallas kernels: 194 us -> 178 us  [run_step(): pl.pallas_call(functools.partial(step_kernel, dims), out_shape=(jax.Shape...]
    unnamed x7 -> x0, local copies, waits for them, and re-layouts: 3.95 us -> none
    pallas_call x1, Pallas kernels: 9.81 us -> 13 us  [finish(): pl.pallas_call(functools.partial(finish_kernel, (mel_rows, half), steps),...]
where the time goes in v3:
time: 193 us
  Pallas kernels  191 us (99%)
    pallas_call x1, Pallas kernels, run_step(): pl.pallas_call(functools.partial(step_kernel, dims), out_shape=(jax.Shape...  178 us
    pallas_call x1, Pallas kernels, finish(): pl.pallas_call(functools.partial(finish_kernel, (mel_rows, half), steps),...  13 us

profile of v3, /device:TPU:0, one launch (start us, length us, event | category | flops | bytes accessed | tf_op | source)
XLA Modules:
  0.0 192.6 jit_solution(7564035970562119819)
XLA Ops:
  1.3 178.3 %train_step.1 = (bf16[2016,1024]{1,0:T(8,128)(2,1)}, bf16[4,8,96,128]{3,2,1,0:T(8,128)(2,1)}, bf16[64,1024]{1,0:T(8,128)(2,1)}) custom-call(s32[1]{0:T(128)S(6)} %copy.27.dil_ref, s32[2,4]{1,0:T(2,128)} %bitcast.36, s32[2,4]{1,0:T(2,128)} %bitcast.37, s32[109]{0:T(128)} %cnt_ref.1, s32[4,1,256]{2,1,0:T(1,128)} %bitcast.35, bf16[4,80]{1,0:T(4,128)(2,1)} %bitcast.38, ...), custom_call_target="tpu_custom_call" | custom-call | flops 10000000000 | bytes 30000000 | tf_op jit(solution)/shard_map/train_step/pallas_call | solution.py:1018
  179.6 13.0 %finish.1 = (bf16[64,1024]{1,0:T(8,128)(2,1)}, f32[1,1024,1024]{2,1,0:T(8,128)}, f32[80,1024]{1,0:T(8,128)}, f32[1,1024]{1,0:T(1,128)}, f32[2,256,512]{2,1,0:T(8...) custom-call(bf16[2016,1024]{1,0:T(8,128)(2,1)} %get-tuple-element.25, ...), custom_call_target="tpu_custom_call" | custom-call | tf_op jit(solution)/shard_map/finish/pallas_call | solution.py:1117

commit v4 on v3

--- a/solution.py
+++ b/solution.py
@@ -18,8 +18,7 @@
 EXT = 96
 WIDE = 1024
 BLOCK = 32
-HUB = 2
-LAG = 3
+LAG = 4
 
 
 def dot(left, right):
@@ -132,7 +131,8 @@
     z = lax.axis_index("dp")
     is_first = s == 0
     is_last = s == sections - 1
-    is_hub = s == HUB
+    hub = sections - 2
+    is_hub = s == hub
     head_scale = 1.0 / math.sqrt(sections)
     main_rows = 2 * half + EXT + half
     head_rows = half // 2 + classes // 2
@@ -153,7 +153,8 @@
     greet(z > 0, s, z - 1)
     greet(z < groups - 1, s, z + 1)
     greet(s >= 2, 0, z)
-    greet((s > HUB + 1) & (lax.rem(s, 2) == 0), HUB, z)
+    told = (lax.rem(s, 2) == 0) & (s > 0) & (s < hub)
+    greet(told, hub, z)
 
     @pl.when(is_first)
     def _():
@@ -163,7 +164,7 @@
 
     @pl.when(is_hub)
     def _():
-        @pl.loop(HUB // 2 + 1, sections // 2)
+        @pl.loop(1, sections // 2 - 1)
         def _(chip):
             pl.semaphore_signal(barrier, 1, device_id=(2 * chip, z), device_id_type=MESH)
 
@@ -191,12 +192,12 @@
         + flag(s < sections - 1)
         + z_near
         + jnp.where(is_first, sections - 2, flag(s >= 2))
-        + flag((s > HUB + 1) & (lax.rem(s, 2) == 0))
+        + flag(told)
         + flag(far)
         + flag(s == 1)
         + flag(s == feeder)
         + jnp.where(is_last, sections // 2 - 2, 0)
-        + jnp.where(is_hub, groups - 1 - z_near + sections // 2 - HUB // 2 - 1, 0)
+        + jnp.where(is_hub, groups - 1 - z_near + sections // 2 - 2, 0)
     )
 
     def input_copy(c):
@@ -653,6 +654,30 @@
 
         gin_buf[pl.ds(pl.multiple_of(group * slots, slots), slots)] = inp_buf[:, 0:share, :]
 
+    def own_local():
+        return pltpu.make_async_copy(gc_buf, o_g.at[z], loc_sem.at[0])
+
+    def own_hub():
+        return remote(gc_buf, o_g.at[z], gown_ss.at[0], g_rs.at[z], hub, z)
+
+    def own_peer(other):
+        return remote(o_g.at[z], o_g.at[z], gpeer_ss.at[other], g_rs.at[z], hub, other)
+
+    def part_chip(j, chip):
+        return remote(o_g.at[j], o_g.at[j], ghub_ss.at[j, chip], g_rs.at[j], 2 * chip, z)
+
+    def part_next(j):
+        return remote(o_g.at[j], o_g.at[j], gnext_ss.at[j], g_rs.at[j], s + 1, z)
+
+    def spread(j):
+        part_next(j).start()
+
+        @pl.loop(0, sections // 2 - 1)
+        def _(chip):
+            @pl.when((chip > 0) | (z != j))
+            def _():
+                part_chip(j, chip).start()
+
     @pl.when(is_last)
     def _():
         @pl.loop(0, micro)
@@ -663,28 +688,38 @@
             if keep < micro:
                 weight_gradients(m)
 
-    @pl.when(jnp.logical_not(is_last))
-    def _():
-        @pl.loop(0, micro)
-        def _(m):
-            build_shift(m)
+    roomy = keep == micro
+    swings = (s == sections - 2) if roomy else False
+    late = (s >= sections // 2) if roomy else is_last
+
+    @pl.loop(0, 3 * micro)
+    def _(step):
+        after = step - micro
+        odd = lax.rem(step, 2) == 1
+        forth = step < micro
+        back = jnp.where(late, (after >= 0) & (after < micro), (after >= 0) & (lax.rem(after, 2) == 0))
+        m = jnp.where(forth, step, jnp.where(late, lax.rem(step, micro), after // 2))
+        if roomy:
+            turning = swings & (step < 2 * micro)
+            end = step == 2 * micro - 1
+            swing_forth = (step == 0) | (odd & jnp.logical_not(end))
+            forth = jnp.where(turning, swing_forth, forth)
+            back = jnp.where(turning, jnp.logical_not(swing_forth), back)
+            swing_m = jnp.where(swing_forth, (step + 1) // 2, jnp.where(end, micro - 1, step // 2 - 1))
+            m = jnp.where(turning, swing_m, m)
+        build_shift(m)
+
+        @pl.when(forth & jnp.logical_not(is_last))
+        def _():
             forward_piece(m, 0)
             forward_piece(m, 1)
 
-        @pl.when(is_first)
+        @pl.when(is_first & (step == micro))
         def _():
             acc[...] = jnp.zeros_like(acc)
             extra_buf[...] = jnp.zeros_like(extra_buf)
 
-    late = (s >= sections // 2) if keep == micro else is_last
-
-    @pl.loop(0, 2 * micro)
-    def _(step):
-        m = jnp.where(late, lax.rem(step, micro), step // 2)
-        is_back = jnp.where(late, step < micro, lax.rem(step, 2) == 0)
-        build_shift(m)
-
-        @pl.when(is_back & jnp.logical_not(is_last))
+        @pl.when(back & jnp.logical_not(is_last))
         def _():
             if ring:
 
@@ -699,38 +734,17 @@
             def _():
                 hand_out((2 * m + 2) // slots - 1)
 
-        @pl.when(jnp.logical_not(is_back) & ((keep == micro) | jnp.logical_not(is_last)))
+            @pl.when(is_first & (m == micro - 1))
+            def _():
+                own_hub().start()
+                own_local().start()
+
+        @pl.when(jnp.logical_not(forth | back) & (roomy | jnp.logical_not(is_last)))
         def _():
             weight_gradients(m)
 
-    def own_local():
-        return pltpu.make_async_copy(gc_buf, o_g.at[z], loc_sem.at[0])
-
-    def own_hub():
-        return remote(gc_buf, o_g.at[z], gown_ss.at[0], g_rs.at[z], HUB, z)
-
-    def own_peer(other):
-        return remote(o_g.at[z], o_g.at[z], gpeer_ss.at[other], g_rs.at[z], HUB, other)
-
-    def part_chip(j, chip):
-        return remote(o_g.at[j], o_g.at[j], ghub_ss.at[j, chip], g_rs.at[j], 2 * chip, z)
-
-    def part_next(j):
-        return remote(o_g.at[j], o_g.at[j], gnext_ss.at[j], g_rs.at[j], s + 1, z)
-
-    def spread(j):
-        part_next(j).start()
-
-        @pl.loop(0, sections // 2)
-        def _(chip):
-            @pl.when((chip != HUB // 2) & ((chip > 0) | (z != j)))
-            def _():
-                part_chip(j, chip).start()
-
     @pl.when(is_first)
     def _():
-        own_local().start()
-        own_hub().start()
         own_local().wait()
 
     left = z < groups // 2
@@ -800,8 +814,8 @@
 
     last_step = main_blocks + lag - 1
     head_at = lag + 2
-    own_at = jnp.minimum(12 + 9 * distance, last_step)
-    rest_at = jnp.where(is_first, 32, jnp.where(is_hub, 27, jnp.where(s < sections // 2 + 2, 46, 51)))
+    own_at = jnp.minimum(23 + 9 * distance, last_step)
+    rest_at = jnp.where(is_hub, 36, jnp.where(is_first, 34, jnp.where(s < sections // 2, 37, 45)))
     rest_at = jnp.minimum(rest_at + 9 * distance, last_step)
 
     @pl.loop(0, count + lag)
@@ -843,7 +857,7 @@
         def _():
             for j in range(groups):
 
-                @pl.when((z != j) | (s > HUB))
+                @pl.when((z != j) | ((s > 0) & (s < hub)))
                 def _():
                     part_next(j).wait_recv()
 
@@ -875,9 +889,9 @@
             def _():
                 own_peer(j).wait_send()
 
-            @pl.loop(0, sections // 2)
+            @pl.loop(0, sections // 2 - 1)
             def _(chip):
-                @pl.when((chip != HUB // 2) & ((chip > 0) | (z != j)))
+                @pl.when((chip > 0) | (z != j))
                 def _():
                     part_chip(j, chip).wait_send()
 
@@ -1034,136 +1048,167 @@
 
 
 def finish_kernel(
-    dims, steps, dil, cond, res, skip, post, out, gin, shared, o_gin, o_dil, o_cond, o_bias, o_res, o_skip, o_post, o_out,
-    o_up, o_table, o_loss, field, mel_rows_buf, mel_columns, table,
+    dims,
+    sums,
+    gin,
+    shared_hbm,
+    o_gin,
+    o_dil,
+    o_cond,
+    o_res,
+    o_skip,
+    o_post,
+    o_out,
+    o_up,
+    o_bias,
+    o_table,
+    o_loss,
+    sums_buf,
+    shared,
+    dil_buf,
+    cond_buf,
+    res_buf,
+    skip_buf,
+    post_buf,
+    out_buf,
+    up_buf,
+    field,
+    mel_rows_buf,
+    mel_columns,
+    table,
+    load_sem,
+    store_sem,
 ):
     mel_rows, half = dims
-    i = pl.program_id(0)
-    frames = shared.shape[0]
-
-    @pl.when(i == 0)
-    def _():
-        table[...] = jnp.zeros_like(table)
-        lane = lax.broadcasted_iota(jnp.int32, (mel_rows, PIECE), 1)
-        number = lane.astype(F32)
-
-        def one(f, loss):
-            extra = shared[f, 0, mel_rows:EXT, :].astype(F32)
-            loss = loss + extra + shared[f, 1, mel_rows:EXT, :].astype(F32)
-            mel_rows_buf[pl.ds(f, 1), :] = extra[0:1]
-            ids = extra[1:2]
-            first = jnp.zeros((mel_rows, 1), F32)
-            second = jnp.zeros((mel_rows, 1), F32)
-            for h in range(2):
-                part = shared[f, h, 0:mel_rows, :].astype(F32)
-                field[h, pl.ds(pl.multiple_of(f * mel_rows, 16), mel_rows), :] = part
-                later = number + float(h * PIECE) >= ids[:, 2:3]
-                first = first + jnp.sum(jnp.where(later, 0.0, part), axis=1, keepdims=True)
-                second = second + jnp.sum(jnp.where(later, part, 0.0), axis=1, keepdims=True)
-            table[...] += jnp.where(number == ids[:, 0:1], first, 0.0)
-            table[...] += jnp.where(number == ids[:, 1:2], second, 0.0)
-            return loss
-
-        loss = lax.fori_loop(0, frames, one, jnp.zeros((EXT - mel_rows, PIECE), F32))
-        row = lax.broadcasted_iota(jnp.int32, loss.shape, 0)
-        loss = jnp.where((row >= 2) & (row < 5), loss, 0.0)
-        o_loss[...] = jnp.sum(jnp.sum(loss, axis=1, keepdims=True), axis=0, keepdims=True)
-        o_table[...] = table[:, 0 : o_table.shape[1]]
-        mel_columns[...] = jnp.transpose(mel_rows_buf[...])[0:mel_rows].astype(BF16)
-
-    o_gin[...] = gin[...]
-    o_dil[0] = dil[...].astype(F32)
-    for source, target in ((res, o_res), (skip, o_skip), (post, o_post), (out, o_out)):
-        target[0] = source[:, 0:half].astype(F32)
-        target[1] = source[:, half : 2 * half].astype(F32)
-
-    @pl.when(i < mel_rows // 16)
-    def _():
-        o_cond[...] = cond[...].astype(F32)
-
-    @pl.when(i == mel_rows // 16)
-    def _():
-        o_bias[...] = cond[...].astype(F32)[0:1]
-
-    channels = mel_rows // steps
-    for j in range(channels):
-        rows = pl.ds(i * channels + j, frames, stride=mel_rows)
-        matrix = jnp.concatenate([field[0, rows, :], field[1, rows, :]], axis=1)
-        o_up[j] = dot(mel_columns[...], matrix.astype(BF16))
-
-
-def finish(sums, shared, grad_inputs, half, classes, mel_rows, speakers):
-    steps = 8
     frames = shared.shape[0]
     first = 2 * half
-    small = half // 2 // steps
-    last = classes // 2 // steps
-    res_at = (first + EXT) // small
-    per = half // 2 // small
-    rows = mel_rows // 16
-
-    def strip(height, index):
-        return pl.BlockSpec((height, WIDE), index)
-
-    def two(height):
-        return pl.BlockSpec((2, height, half), lambda i: (0, i, 0))
-
-    def fixed(*shape):
-        return pl.BlockSpec(shape, lambda i: (0,) * len(shape))
+    total_rows = sums_buf.shape[0]
+    strips = ((0, half), (half, half), (first, total_rows - first))
+    loads = [
+        pltpu.make_async_copy(sums.at[pl.ds(row, rows), :], sums_buf.at[pl.ds(row, rows), :], load_sem.at[k])
+        for k, (row, rows) in enumerate(strips)
+    ]
+    loads.append(pltpu.make_async_copy(shared_hbm, shared, load_sem.at[3]))
+    for load in loads:
+        load.start()
+    stores = []
+
+    def store(source, target):
+        copy = pltpu.make_async_copy(source, target, store_sem.at[len(stores)])
+        copy.start()
+        stores.append(copy)
+
+    store(gin, o_gin)
+
+    for k in range(2):
+        loads[k].wait()
+        rows = pl.ds(k * half, half)
+        dil_buf[rows, :] = sums_buf[rows, :].astype(F32)
+        store(dil_buf.at[rows, :], o_dil.at[0, rows, :])
+    loads[2].wait()
+    cond_buf[...] = sums_buf[first : first + mel_rows, :].astype(F32)
+    o_bias[...] = sums_buf[first + mel_rows : first + EXT, :].astype(F32)[0:1]
+    store(cond_buf, o_cond)
+    row = first + EXT
+    for buffer, target in ((res_buf, o_res), (skip_buf, o_skip), (post_buf, o_post), (out_buf, o_out)):
+        rows = buffer.shape[1]
+        buffer[0] = sums_buf[row : row + rows, 0:half].astype(F32)
+        buffer[1] = sums_buf[row : row + rows, half : 2 * half].astype(F32)
+        store(buffer, target)
+        row += rows
+
+    loads[3].wait()
+
+    def by_channel(f, loss):
+        extra = shared[f, 0, mel_rows:EXT, :].astype(F32)
+        mel_rows_buf[pl.ds(f, 1), :] = extra[0:1]
+        for h in range(2):
+            rows = pl.ds(pl.multiple_of(f * mel_rows, 16), mel_rows)
+            field[h, rows, :] = shared[f, h, 0:mel_rows, :].astype(F32)
+        return loss + extra + shared[f, 1, mel_rows:EXT, :].astype(F32)
+
+    loss = lax.fori_loop(0, frames, by_channel, jnp.zeros((EXT - mel_rows, PIECE), F32))
+    row = lax.broadcasted_iota(jnp.int32, loss.shape, 0)
+    loss = jnp.where((row >= 2) & (row < 5), loss, 0.0)
+    o_loss[...] = jnp.sum(jnp.sum(loss, axis=1, keepdims=True), axis=0, keepdims=True)
+    mel_columns[...] = jnp.transpose(mel_rows_buf[...])[0:mel_rows].astype(BF16)
+
+    parts = 4
+    channels = mel_rows // parts
+    for part in range(parts):
+
+        @pl.loop(0, channels // 10)
+        def _(group):
+            for j in range(10):
+                c = part * channels + group * 10 + j
+                rows = pl.ds(c, frames, stride=mel_rows)
+                matrix = jnp.concatenate([field[0, rows, :], field[1, rows, :]], axis=1)
+                up_buf[c] = dot(mel_columns[...], matrix.astype(BF16))
+
+        rows = pl.ds(part * channels, channels)
+        store(up_buf.at[rows], o_up.at[rows])
+
+    table[...] = jnp.zeros_like(table)
+
+    @pl.loop(0, frames)
+    def _(f):
+        ids = shared[f, 0, mel_rows:EXT, :].astype(F32)[1:2]
+        time = lax.broadcasted_iota(jnp.int32, (PIECE, PIECE), 0).astype(F32)
+        number = lax.broadcasted_iota(jnp.int32, (PIECE, PIECE), 1).astype(F32)
+        for h in range(2):
+            speaker = jnp.where(time + float(h * PIECE) >= ids[:, 2:3], ids[:, 1:2], ids[:, 0:1])
+            hot = jnp.where(number == speaker, 1.0, 0.0).astype(BF16)
+            table[...] += dot(shared[f, h, 0:mel_rows, :], hot)
+
+    o_table[...] = table[:, 0 : o_table.shape[1]]
+    for copy in stores:
+        copy.wait()
+
+
+def finish(sums, shared, grad_inputs, half, classes, mel_rows, speakers):
+    frames = shared.shape[0]
+    first = 2 * half
+    vmem = pl.BlockSpec(memory_space=pltpu.VMEM)
+    anywhere = pl.BlockSpec(memory_space=pl.ANY)
+    large = (
+        (first, WIDE),
+        (mel_rows, WIDE),
+        (2, half // 2, half),
+        (2, half // 2, half),
+        (2, half // 2, half),
+        (2, classes // 2, half),
+        (mel_rows, mel_rows, 2 * PIECE),
+    )
 
     def f32(*shape):
         return jax.ShapeDtypeStruct(shape, F32)
 
     return pl.pallas_call(
-        functools.partial(finish_kernel, (mel_rows, half), steps),
-        grid=(steps,),
+        functools.partial(finish_kernel, (mel_rows, half)),
         out_shape=(
             jax.ShapeDtypeStruct(grad_inputs.shape, grad_inputs.dtype),
-            f32(1, first, WIDE),
-            f32(mel_rows, WIDE),
+            f32(1, *large[0]),
+            *[f32(*shape) for shape in large[1:]],
             f32(1, WIDE),
-            f32(2, half // 2, half),
-            f32(2, half // 2, half),
-            f32(2, half // 2, half),
-            f32(2, classes // 2, half),
-            f32(mel_rows, mel_rows, 2 * PIECE),
             f32(mel_rows, speakers),
             f32(1, 1),
         ),
-        in_specs=[
-            strip(first // steps, lambda i: (i, 0)),
-            strip(16, lambda i: (first // 16 + jnp.minimum(i, rows), 0)),
-            strip(small, lambda i: (res_at + i, 0)),
-            strip(small, lambda i: (res_at + per + i, 0)),
-            strip(small, lambda i: (res_at + 2 * per + i, 0)),
-            strip(last, lambda i: ((first + EXT + half + half // 2) // last + i, 0)),
-            pl.BlockSpec((grad_inputs.shape[0], grad_inputs.shape[1] // steps), lambda i: (0, i)),
-            pl.BlockSpec(memory_space=pltpu.VMEM),
-        ],
-        out_specs=(
-            pl.BlockSpec((grad_inputs.shape[0], grad_inputs.shape[1] // steps), lambda i: (0, i)),
-            pl.BlockSpec((1, first // steps, WIDE), lambda i: (0, i, 0)),
-            strip(16, lambda i: (jnp.minimum(i, rows - 1), 0)),
-            fixed(1, WIDE),
-            two(small),
-            two(small),
-            two(small),
-            two(last),
-            pl.BlockSpec((mel_rows // steps, mel_rows, 2 * PIECE), lambda i: (i, 0, 0)),
-            fixed(mel_rows, speakers),
-            fixed(1, 1),
-        ),
+        in_specs=[anywhere] * 3,
+        out_specs=(anywhere,) * 8 + (vmem,) * 3,
         scratch_shapes=[
+            pltpu.VMEM(sums.shape, BF16),
+            pltpu.VMEM(shared.shape, BF16),
+            *[pltpu.VMEM(shape, F32) for shape in large],
             pltpu.VMEM((2, frames * mel_rows, PIECE), F32),
             pltpu.VMEM((frames, PIECE), F32),
             pltpu.VMEM((mel_rows, frames), BF16),
             pltpu.VMEM((mel_rows, PIECE), F32),
+            pltpu.SemaphoreType.DMA((4,)),
+            pltpu.SemaphoreType.DMA((12,)),
         ],
-        compiler_params=pltpu.CompilerParams(
-            vmem_limit_bytes=62 * 2**20, dimension_semantics=("arbitrary",)
-        ),
+        compiler_params=pltpu.CompilerParams(vmem_limit_bytes=62 * 2**20),
         name="finish",
-    )(sums, sums, sums, sums, sums, sums, grad_inputs, shared)
+    )(sums, grad_inputs, shared)
 
 
 def local(
@@ -1219,7 +1264,7 @@
         ),
     )
     shared = shared.reshape(groups * micro, 2, EXT, PIECE)
-    grad_inputs, dil, cond, bias, grad_res, grad_skip, post, out, up, table, loss = finish(
+    grad_inputs, dil, cond, grad_res, grad_skip, post, out, up, bias, table, loss = finish(
         sums, shared, grad_inputs, half, classes, mel_rows, speaker_table.shape[1]
     )
     return (

time: 193 us -> 181 us (0.938)
  Pallas kernels: 191 us -> 180 us
    pallas_call x1, Pallas kernels: 178 us -> 170 us  [run_step(): pl.pallas_call(functools.partial(step_kernel, dims), out_shape=(jax.Shape...]
    pallas_call x1, Pallas kernels: 13 us -> 9.95 us  [finish(): pl.pallas_call(functools.partial(finish_kernel, (mel_rows, half)), out_sh...]
where the time goes in v4:
time: 181 us
  Pallas kernels  180 us (99%)
    pallas_call x1, Pallas kernels, run_step(): pl.pallas_call(functools.partial(step_kernel, dims), out_shape=(jax.Shape...  170 us
    pallas_call x1, Pallas kernels, finish(): pl.pallas_call(functools.partial(finish_kernel, (mel_rows, half)), out_sh...  9.95 us

profile of v4, /device:TPU:0, one launch (start us, length us, event | category | flops | bytes accessed | tf_op | source)
XLA Modules:
  0.0 181.1 jit_solution(5090152402654059700)
XLA Ops:
  1.3 169.8 %train_step.1 = (bf16[2016,1024]{1,0:T(8,128)(2,1)}, bf16[4,8,96,128]{3,2,1,0:T(8,128)(2,1)}, bf16[64,1024]{1,0:T(8,128)(2,1)}) custom-call(s32[1]{0:T(128)S(6)} %copy.27.dil_ref, s32[2,4]{1,0:T(2,128)} %bitcast.36, s32[2,4]{1,0:T(2,128)} %bitcast.37, s32[109]{0:T(128)} %cnt_ref.1, s32[4,1,256]{2,1,0:T(1,128)} %bitcast.35, bf16[4,80]{1,0:T(4,128)(2,1)} %bitcast.38, ...), custom_call_target="tpu_custom_call" | custom-call | flops 10000000000 | bytes 30000000 | tf_op jit(solution)/shard_map/train_step/pallas_call | solution.py:1032
  171.1 9.9 %finish.1 = (bf16[64,1024]{1,0:T(8,128)(2,1)}, f32[1,1024,1024]{2,1,0:T(8,128)}, f32[80,1024]{1,0:T(8,128)}, f32[2,256,512]{2,1,0:T(8,128)}, f32[2,256,512]{2,1,...) custom-call(bf16[2016,1024]{1,0:T(8,128)(2,1)} %get-tuple-element.25, ...), custom_call_target="tpu_custom_call" | custom-call | tf_op jit(solution)/shard_map/finish/pallas_call | solution.py:1186

commit v5 on v4

--- a/solution.py
+++ b/solution.py
@@ -18,6 +18,7 @@
 EXT = 96
 WIDE = 1024
 BLOCK = 32
+EXPORT = 4
 LAG = 4
 
 
@@ -35,6 +36,12 @@
 
 def sigmoid(values):
     return 0.5 * jnp.tanh(0.5 * values) + 0.5
+
+
+def exported_blocks(dims):
+    sections, groups, micro, keep = dims[0], dims[1], dims[2], dims[7]
+    feeder = sections - 3 if sections > 4 else sections - 1
+    return EXPORT if keep == micro and feeder == sections // 2 + 1 else 0
 
 
 def step_kernel(
@@ -55,7 +62,7 @@
     ws_hbm,
     wp_hbm,
     wk_hbm,
-    o_acc,
+    o_sum,
     o_g,
     o_gin,
     x_buf,
@@ -95,11 +102,14 @@
     acc,
     part_out,
     part_in,
+    o_acc,
+    taken_buf,
     gin_buf,
     up_buf,
     extra_buf,
     inp_sem,
     load_sem,
+    out_sem,
     loc_sem,
     x_ss,
     x_rs,
@@ -124,6 +134,8 @@
     gnext_ss,
     gin_ss,
     gin_rs,
+    give_ss,
+    give_rs,
 ):
     sections, groups, micro, res, half, classes, slots, keep, mel_rows = dims
     pieces = 2 * micro
@@ -140,6 +152,8 @@
     head_blocks = head_rows // BLOCK
     share = res // sections
     feeder = sections - 3 if sections > 4 else sections - 1
+    exports = exported_blocks(dims)
+    helper = sections // 2
 
     barrier = pltpu.get_barrier_semaphore()
 
@@ -238,14 +252,17 @@
         def _(c):
             input_copy(c).start()
 
-    for load in loads[4:]:
-        load.start()
+    @pl.when(is_last)
+    def _():
+        for load in loads[4:]:
+            load.start()
+
     spare = lax.broadcasted_iota(jnp.int32, (EXT - mel_rows, 2 * half), 0)
     bias = jnp.broadcast_to(bias_in[...].astype(F32), (EXT - mel_rows, 2 * half))
     wc_ref[mel_rows:EXT] = jnp.where(spare == 0, bias, 0.0).astype(BF16)
     loads[0].wait()
     wd_t[...] = jnp.transpose(wd_ref[...])
-    for load in loads[1:]:
+    for load in loads[1:4]:
         load.wait()
     wr_t[...] = jnp.transpose(wr_ref[...])
     ws_t[...] = jnp.transpose(ws_ref[...])
@@ -265,30 +282,38 @@
                 for h in range(2):
                     up_buf[h, rows, :] = frames[:, h * PIECE : (h + 1) * PIECE]
 
-    speaker_lane = lax.broadcasted_iota(jnp.int32, tab_ref.shape, 1)
-    spare = lax.broadcasted_iota(jnp.int32, (EXT - mel_rows, PIECE), 0)
-    table = tab_ref[...].astype(F32)
-
-    @pl.loop(0, micro)
-    def _(m):
-        def column(which):
-            return jnp.sum(jnp.where(speaker_lane == spk_ref[which, m], table, 0.0), axis=1, keepdims=True)
-
-        first, second = column(0), column(1)
+    def condition(m):
+        shape = (tab_ref.shape[1], 2 * PIECE)
+        time = lax.broadcasted_iota(jnp.int32, shape, 1)
+        speaker = jnp.where(time >= offs_ref[0, m], spk_ref[1, m], spk_ref[0, m])
+        hot = jnp.where(lax.broadcasted_iota(jnp.int32, shape, 0) == speaker, 1.0, 0.0).astype(BF16)
+        columns = dot(tab_ref[...], hot)
+        ones = jnp.where(lax.broadcasted_iota(jnp.int32, (EXT - mel_rows, PIECE), 0) == 0, 1.0, 0.0)
+        rows = pl.ds(pl.multiple_of(m * mel_rows, 16), mel_rows)
         for h in range(2):
-            time = lax.broadcasted_iota(jnp.int32, (mel_rows, PIECE), 1) + h * PIECE
-            speaker = jnp.where(time >= offs_ref[0, m], second, first)
-            rows = pl.ds(pl.multiple_of(m * mel_rows, 16), mel_rows)
-            cond_ref[2 * m + h, 0:mel_rows, :] = (up_buf[h, rows, :] + speaker).astype(BF16)
-            cond_ref[2 * m + h, mel_rows:EXT, :] = jnp.where(spare == 0, 1.0, 0.0).astype(BF16)
-            cond_t[2 * m + h] = jnp.transpose(cond_ref[2 * m + h])
+            c = 2 * m + h
+            value = up_buf[h, rows, :] + columns[:, h * PIECE : (h + 1) * PIECE]
+            cond_ref[c] = jnp.concatenate([value, ones], axis=0).astype(BF16)
+            cond_t[c] = jnp.transpose(cond_ref[c])
+
+    @pl.when(is_first)
+    def _():
+        condition(0)
 
     @pl.when(s > 0)
     def _():
+        @pl.loop(0, micro)
+        def _(m):
+            condition(m)
+
+    @pl.when(s > 0)
+    def _():
         acc[...] = jnp.zeros_like(acc)
 
     @pl.when(is_last)
     def _():
+        for load in loads[4:]:
+            load.wait()
         wp_t[...] = jnp.transpose(wp_ref[...])
         wk_t[...] = jnp.transpose(wk_ref[...])
         gx_buf[...] = jnp.zeros_like(gx_buf)
@@ -709,6 +734,10 @@
             m = jnp.where(turning, swing_m, m)
         build_shift(m)
 
+        @pl.when(forth & is_first & (m > 0))
+        def _():
+            condition(m)
+
         @pl.when(forth & jnp.logical_not(is_last))
         def _():
             forward_piece(m, 0)
@@ -754,10 +783,18 @@
     is_mid = (z == groups // 2 - 1) | (z == groups // 2)
     distance = jnp.where(left, groups // 2 - 1 - z, z - groups // 2)
     lag = LAG * (2 * distance + 1) + 4 * distance
-    count = jnp.where(is_last, main_blocks + head_blocks, main_blocks)
+    base = jnp.where(is_last, main_blocks + head_blocks, main_blocks)
+    gives = (s < 2) if exports else False
+    takes = ((s == helper) | (s == helper + 1)) if exports else False
+    count = base - jnp.where(gives, exports, 0) + jnp.where(takes, exports, 0)
+
+    all_blocks = main_blocks + head_blocks
+    taken_at = base - 2 * exports
 
     def block_of(i):
-        return jnp.where(is_last, jnp.where(i < head_blocks, i + main_blocks, i - head_blocks), i)
+        j = jnp.where(takes & (i >= taken_at + exports), i - exports, i)
+        own = jnp.where(is_last, jnp.where(j < head_blocks, j + main_blocks, j - head_blocks), j)
+        return jnp.where(takes & (j == i) & (i >= taken_at), i - taken_at + all_blocks, own)
 
     def rows_of(b):
         return pl.ds(pl.multiple_of(b * BLOCK, BLOCK), BLOCK)
@@ -800,6 +837,9 @@
         def _():
             part_copy(i).start()
 
+    def keep_rows(rows):
+        return pltpu.make_async_copy(o_acc.at[rows], o_sum.at[rows], out_sem.at[0])
+
     def finish_part(i):
         rows = rows_of(block_of(i))
         swap_copy(i).wait_recv()
@@ -812,14 +852,41 @@
         def _():
             total_copy(i).start()
 
-    last_step = main_blocks + lag - 1
+        @pl.when(block_of(i) < all_blocks)
+        def _():
+            keep_rows(rows).start()
+
+    given_rows = pl.ds(main_rows - exports * BLOCK, exports * BLOCK)
+    taken_rows = pl.ds(main_rows + head_rows, exports * BLOCK)
+
+    def give_copy():
+        return remote(part_out.at[given_rows], taken_buf, give_ss.at[0], give_rs.at[0], s + helper, z)
+
+    def return_copy():
+        return remote(o_acc.at[taken_rows], o_acc.at[given_rows], give_ss.at[1], give_rs.at[1], s - helper, z)
+
+    if exports:
+
+        @pl.when(gives)
+        def _():
+            part_out[given_rows, :] = acc[given_rows, :].astype(BF16)
+            give_copy().start()
+
+    last_step = main_blocks - exports + lag - 1
     head_at = lag + 2
-    own_at = jnp.minimum(23 + 9 * distance, last_step)
-    rest_at = jnp.where(is_hub, 36, jnp.where(is_first, 34, jnp.where(s < sections // 2, 37, 45)))
+    own_at = jnp.minimum(17 + 9 * distance, last_step)
+    rest_at = jnp.where(is_hub, 33, jnp.where(s < sections // 2, 40, 45))
     rest_at = jnp.minimum(rest_at + 9 * distance, last_step)
 
     @pl.loop(0, count + lag)
     def _(i):
+        if exports:
+
+            @pl.when(takes & (i == taken_at))
+            def _():
+                give_copy().wait_recv()
+                acc[taken_rows, :] = taken_buf[...].astype(F32)
+
         @pl.when(i < count)
         def _():
             send_part(i)
@@ -829,14 +896,21 @@
             finish_part(i - lag)
             b = block_of(i - lag)
 
-            @pl.when(b >= main_blocks)
+            @pl.when((b >= main_blocks) & (b < all_blocks))
             def _():
                 head_copy(b - main_blocks).start()
 
+            if exports:
+
+                @pl.when(b == all_blocks + exports - 1)
+                def _():
+                    return_copy().start()
+
         @pl.when(jnp.logical_not(is_last) & (i >= head_at) & (i < head_at + head_blocks))
         def _():
             j = i - head_at
             head_copy(j).wait_recv()
+            keep_rows(rows_of(main_blocks + j)).start()
 
             @pl.when(s > 0)
             def _():
@@ -905,6 +979,20 @@
         def _():
             part_next(j).wait_recv()
 
+    if exports:
+
+        @pl.when(gives)
+        def _():
+            return_copy().wait_recv()
+            keep_rows(given_rows).start()
+            give_copy().wait_send()
+
+        @pl.when(takes)
+        def _():
+            return_copy().wait_send()
+
+    keep_rows(pl.ds(0, main_rows + head_rows)).wait()
+
     def sum_sent(rows):
         remote(part_out.at[rows], part_out.at[rows], zi_ss.at[0], zp_rs.at[0], s, inward).wait_send()
 
@@ -914,11 +1002,24 @@
 
     @pl.when(is_last)
     def _():
-        sum_sent(pl.ds(0, main_rows + head_rows))
+        sum_sent(pl.ds(0, main_rows + head_rows + (exports * BLOCK if helper + 1 == sections - 1 else 0)))
+
+    if exports:
+
+        @pl.when(takes & jnp.logical_not(is_last))
+        def _():
+            sum_sent(pl.ds(0, main_rows + exports * BLOCK))
+
+        @pl.when(gives)
+        def _():
+            sum_sent(pl.ds(0, main_rows - exports * BLOCK))
+
+    @pl.when(jnp.logical_not(is_last | gives | takes))
+    def _():
+        sum_sent(pl.ds(0, main_rows))
 
     @pl.when(jnp.logical_not(is_last))
     def _():
-        sum_sent(pl.ds(0, main_rows))
         drain(x_copy, lambda: remote(x_out, x_out, x_ss.at[0], x_rs.at[0], s + 1, z))
         drain(k_copy, lambda: remote(k_out, k_out, k_ss.at[0], k_rs.at[0], s + 1, z))
 
@@ -960,6 +1061,7 @@
     distance = groups // 2 - 1
     cycle = max(LAG * (2 * distance + 1) + 4 * distance + 4, 2 * LAG + 4)
     sends = slots if pieces > slots else 1
+    taken = exported_blocks(dims) * BLOCK
 
     scratch = [
         tile(pieces, PIECE, res),
@@ -996,14 +1098,17 @@
         tile(2 * keep, half, PIECE),
         tile(2 * keep, half, PIECE),
         tile(2 * keep, half, PIECE),
-        tile(rows, WIDE, dtype=F32),
-        tile(rows, WIDE),
-        tile(rows, WIDE),
+        tile(rows + taken, WIDE, dtype=F32),
+        tile(rows + taken, WIDE),
+        tile(rows + taken, WIDE),
+        tile(rows + taken, WIDE),
+        tile(max(taken, 16), WIDE),
         tile(pieces, share, PIECE),
         tile(2, micro * mel_rows, PIECE, dtype=F32),
         tile(EXT - mel_rows, PIECE, dtype=F32),
         dma((slots,)),
         dma((10,)),
+        dma((1,)),
         dma((1,)),
         dma((sends,)),
         dma((pieces,)),
@@ -1028,6 +1133,8 @@
         dma((groups,)),
         dma((1,)),
         dma((1,)),
+        dma((2,)),
+        dma((2,)),
     ]
     return pl.pallas_call(
         functools.partial(step_kernel, dims),
@@ -1037,7 +1144,7 @@
             jax.ShapeDtypeStruct((share, pieces * PIECE), BF16),
         ),
         in_specs=[smem] * 4 + [vmem] * 4 + [anywhere] * 8,
-        out_specs=(vmem, anywhere, vmem),
+        out_specs=(anywhere, anywhere, vmem),
         scratch_shapes=scratch,
         compiler_params=pltpu.CompilerParams(
             collective_id=0, has_side_effects=True, vmem_limit_bytes=63 * 2**20
@@ -1135,8 +1242,8 @@
 
     parts = 4
     channels = mel_rows // parts
-    for part in range(parts):
-
+
+    def upsampling(part):
         @pl.loop(0, channels // 10)
         def _(group):
             for j in range(10):
@@ -1148,19 +1255,28 @@
         rows = pl.ds(part * channels, channels)
         store(up_buf.at[rows], o_up.at[rows])
 
+    for part in range(parts - 2):
+        upsampling(part)
+
     table[...] = jnp.zeros_like(table)
-
-    @pl.loop(0, frames)
-    def _(f):
-        ids = shared[f, 0, mel_rows:EXT, :].astype(F32)[1:2]
-        time = lax.broadcasted_iota(jnp.int32, (PIECE, PIECE), 0).astype(F32)
-        number = lax.broadcasted_iota(jnp.int32, (PIECE, PIECE), 1).astype(F32)
-        for h in range(2):
-            speaker = jnp.where(time + float(h * PIECE) >= ids[:, 2:3], ids[:, 1:2], ids[:, 0:1])
-            hot = jnp.where(number == speaker, 1.0, 0.0).astype(BF16)
-            table[...] += dot(shared[f, h, 0:mel_rows, :], hot)
+    time = lax.broadcasted_iota(jnp.int32, (2 * PIECE, PIECE), 0).astype(F32)
+    number = lax.broadcasted_iota(jnp.int32, (2 * PIECE, PIECE), 1).astype(F32)
+
+    @pl.loop(0, frames // 4)
+    def _(group):
+        grads, hots = [], []
+        for k in range(4):
+            f = group * 4 + k
+            ids = shared[f, 0, mel_rows:EXT, :].astype(F32)[1:2]
+            speaker = jnp.where(time >= ids[:, 2:3], ids[:, 1:2], ids[:, 0:1])
+            hots.append(jnp.where(number == speaker, 1.0, 0.0).astype(BF16))
+            grads += [shared[f, 0, 0:mel_rows, :], shared[f, 1, 0:mel_rows, :]]
+        table[...] += dot(jnp.concatenate(grads, axis=1), jnp.concatenate(hots, axis=0))
 
     o_table[...] = table[:, 0 : o_table.shape[1]]
+    for part in range(parts - 2, parts):
+        upsampling(part)
+
     for copy in stores:
         copy.wait()
 

time: 181 us -> 170 us (0.939); the launches traced: 181 us -> 168 us
  Pallas kernels: 180 us -> 167 us
    pallas_call x1, Pallas kernels: 170 us -> 159 us  [run_step(): pl.pallas_call(functools.partial(step_kernel, dims), out_shape=(jax.Shape...]
    pallas_call x1, Pallas kernels: 9.95 us -> 8.08 us  [finish(): pl.pallas_call(functools.partial(finish_kernel, (mel_rows, half)), out_sh...]
where the time goes in v5:
time: 170 us; the launch traced here: 168 us
  Pallas kernels  167 us (98%)
    pallas_call x1, Pallas kernels, run_step(): pl.pallas_call(functools.partial(step_kernel, dims), out_shape=(jax.Shape...  159 us
    pallas_call x1, Pallas kernels, finish(): pl.pallas_call(functools.partial(finish_kernel, (mel_rows, half)), out_sh...  8.08 us

profile of v5, /device:TPU:0, one launch (start us, length us, event | category | flops | bytes accessed | tf_op | source)
XLA Modules:
  0.0 168.0 jit_solution(10997368900753940118)
XLA Ops:
  1.3 158.6 %train_step.1 = (bf16[2016,1024]{1,0:T(8,128)(2,1)}, bf16[4,8,96,128]{3,2,1,0:T(8,128)(2,1)}, bf16[64,1024]{1,0:T(8,128)(2,1)}) custom-call(s32[1]{0:T(128)S(6)} %copy.27.dil_ref, s32[2,4]{1,0:T(2,128)} %bitcast.36, s32[2,4]{1,0:T(2,128)} %bitcast.37, s32[109]{0:T(128)} %cnt_ref.1, s32[4,1,256]{2,1,0:T(1,128)} %bitcast.35, bf16[4,80]{1,0:T(4,128)(2,1)} %bitcast.38, ...), custom_call_target="tpu_custom_call" | custom-call | flops 10000000000 | bytes 30000000 | tf_op jit(solution)/shard_map/train_step/pallas_call | solution.py:1139
  159.9 8.1 %finish.1 = (bf16[64,1024]{1,0:T(8,128)(2,1)}, f32[1,1024,1024]{2,1,0:T(8,128)}, f32[80,1024]{1,0:T(8,128)}, f32[2,256,512]{2,1,0:T(8,128)}, f32[2,256,512]{2,1,...) custom-call(bf16[2016,1024]{1,0:T(8,128)(2,1)} %get-tuple-element.25, ...), custom_call_target="tpu_custom_call" | custom-call | tf_op jit(solution)/shard_map/finish/pallas_call | solution.py:1302

commit v6 on v5

--- a/solution.py
+++ b/solution.py
@@ -18,7 +18,8 @@
 EXT = 96
 WIDE = 1024
 BLOCK = 32
-EXPORT = 4
+EXPORTS = (6,)
+LARGE_AT = 3
 LAG = 4
 
 
@@ -40,8 +41,8 @@
 
 def exported_blocks(dims):
     sections, groups, micro, keep = dims[0], dims[1], dims[2], dims[7]
-    feeder = sections - 3 if sections > 4 else sections - 1
-    return EXPORT if keep == micro and feeder == sections // 2 + 1 else 0
+    helped = sections // 4
+    return EXPORTS[:helped] if keep == micro and sections <= 8 else ()
 
 
 def step_kernel(
@@ -182,9 +183,6 @@
         def _(chip):
             pl.semaphore_signal(barrier, 1, device_id=(2 * chip, z), device_id_type=MESH)
 
-        for other in range(groups):
-            greet((other > z + 1) | (other < z - 1), s, other)
-
     far = (lax.rem(s, 2) == 1) & (s > 1) & (s < sections - 1)
     greet(far, sections - 1, z)
 
@@ -211,7 +209,7 @@
         + flag(s == 1)
         + flag(s == feeder)
         + jnp.where(is_last, sections // 2 - 2, 0)
-        + jnp.where(is_hub, groups - 1 - z_near + sections // 2 - 2, 0)
+        + jnp.where(is_hub, sections // 2 - 2, 0)
     )
 
     def input_copy(c):
@@ -632,27 +630,66 @@
         acc[first_row : first_row + rows, 0:half] += value[0:rows]
         acc[first_row : first_row + rows, half : 2 * half] += value[rows : 2 * rows]
 
-    def weight_gradients(m):
+    small_row = 2 * half + EXT
+
+    def small_gradients(m):
         parts = (0, 1)
-        kept = 2 * lax.rem(m, keep)
-        grad_gate = both(gg_buf, kept, parts)
+        hidden = both(hid_buf, 2 * m, parts)
+
+        @pl.when(s < sections - 1)
+        def _():
+            add_halves(small_row, HALF_ROOT * dot_tn(both(gx_buf, 2 * m, parts), hidden))
+
+        add_halves(small_row + half // 2, dot_tn(both(sg_buf, 2 * m, parts), hidden))
+
+        @pl.when(is_last)
+        def _():
+            kept = 2 * lax.rem(m, keep)
+            add_halves(main_rows, dot_nt(pair(gp_buf, kept), pair(a1_buf, kept)))
+            add_halves(main_rows + half // 2, dot_nt(pair(gl_buf, kept), pair(a2_buf, kept)))
+
+    def large_gradients(m):
+        parts = (0, 1)
+        grad_gate = both(gg_buf, 2 * lax.rem(m, keep), parts)
         x = both(x_buf, 2 * m, parts)
         prev = dot(shift_buf[...], x).astype(BF16)
         acc[0 : 2 * half, :] += dot_tn(grad_gate, jnp.concatenate([prev, x], axis=1))
-        acc[2 * half : 2 * half + EXT, :] += dot(pair(cond_ref, 2 * m), grad_gate)
-        hidden = both(hid_buf, 2 * m, parts)
-        row = 2 * half + EXT
+        acc[2 * half : small_row, :] += dot(pair(cond_ref, 2 * m), grad_gate)
+
+    def samples(ref):
+        return ref[...].reshape(pieces * PIECE, ref.shape[2])
+
+    def by_channel(ref):
+        return jnp.concatenate([ref[c] for c in range(pieces)], axis=1)
+
+    def set_halves(first_row, value):
+        rows = value.shape[0] // 2
+        acc[first_row : first_row + rows, 0:half] = value[0:rows]
+        acc[first_row : first_row + rows, half : 2 * half] = value[rows : 2 * rows]
+
+    def all_small_gradients():
+        @pl.when(is_last)
+        def _():
+            set_halves(main_rows, dot_nt(by_channel(gp_buf), by_channel(a1_buf)))
+            set_halves(main_rows + half // 2, dot_nt(by_channel(gl_buf), by_channel(a2_buf)))
+
+        hidden = samples(hid_buf)
+        set_halves(small_row + half // 2, dot_tn(samples(sg_buf), hidden))
 
         @pl.when(s < sections - 1)
         def _():
-            add_halves(row, HALF_ROOT * dot_tn(both(gx_buf, 2 * m, parts), hidden))
-
-        add_halves(row + half // 2, dot_tn(both(sg_buf, 2 * m, parts), hidden))
-
-        @pl.when(is_last)
-        def _():
-            add_halves(main_rows, dot_nt(pair(gp_buf, kept), pair(a1_buf, kept)))
-            add_halves(main_rows + half // 2, dot_nt(pair(gl_buf, kept), pair(a2_buf, kept)))
+            set_halves(small_row, HALF_ROOT * dot_tn(samples(gx_buf), hidden))
+
+    def all_large_gradients():
+        @pl.loop(0, micro)
+        def _(m):
+            build_shift(m)
+            put(d1_buf, 2 * m, (0, 1), dot(shift_buf[...], both(x_buf, 2 * m, (0, 1))).astype(BF16))
+
+        grad_gate = samples(gg_buf)
+        acc[0 : 2 * half, 0:res] = dot_tn(grad_gate, samples(d1_buf))
+        acc[0 : 2 * half, res : 2 * res] = dot_tn(grad_gate, samples(x_buf))
+        acc[2 * half : small_row, :] = dot(by_channel(cond_ref), grad_gate)
 
     def gin_rows(other, group):
         return remote(
@@ -685,8 +722,9 @@
     def own_hub():
         return remote(gc_buf, o_g.at[z], gown_ss.at[0], g_rs.at[z], hub, z)
 
-    def own_peer(other):
-        return remote(o_g.at[z], o_g.at[z], gpeer_ss.at[other], g_rs.at[z], hub, other)
+    def part_along(j, step):
+        sem = gpeer_ss.at[j if step > 0 else groups + j]
+        return remote(o_g.at[j], o_g.at[j], sem, g_rs.at[j], s, z + step)
 
     def part_chip(j, chip):
         return remote(o_g.at[j], o_g.at[j], ghub_ss.at[j, chip], g_rs.at[j], 2 * chip, z)
@@ -711,11 +749,12 @@
             forward_head(m)
             backward_pair(m)
             if keep < micro:
-                weight_gradients(m)
+                small_gradients(m)
+                large_gradients(m)
 
     roomy = keep == micro
     swings = (s == sections - 2) if roomy else False
-    late = (s >= sections // 2) if roomy else is_last
+    late = (s >= sections - 2) if roomy else is_last
 
     @pl.loop(0, 3 * micro)
     def _(step):
@@ -768,9 +807,19 @@
                 own_hub().start()
                 own_local().start()
 
-        @pl.when(jnp.logical_not(forth | back) & (roomy | jnp.logical_not(is_last)))
-        def _():
-            weight_gradients(m)
+        @pl.when(jnp.logical_not(forth | back | late))
+        def _():
+            small_gradients(m)
+
+            @pl.when(m < micro - 1)
+            def _():
+                large_gradients(m)
+
+    if roomy:
+
+        @pl.when(late)
+        def _():
+            all_small_gradients()
 
     @pl.when(is_first)
     def _():
@@ -784,16 +833,21 @@
     distance = jnp.where(left, groups // 2 - 1 - z, z - groups // 2)
     lag = LAG * (2 * distance + 1) + 4 * distance
     base = jnp.where(is_last, main_blocks + head_blocks, main_blocks)
-    gives = (s < 2) if exports else False
-    takes = ((s == helper) | (s == helper + 1)) if exports else False
-    count = base - jnp.where(gives, exports, 0) + jnp.where(takes, exports, 0)
+    helped = 2 * len(exports)
+    gives = (s < helped) if exports else False
+    takes = ((s >= helper) & (s < helper + helped)) if exports else False
+    moved = 0
+    for chip, amount in enumerate(exports):
+        moved = jnp.where(lax.rem(s, helper) // 2 == chip, amount, moved)
+    count = base - jnp.where(gives, moved, 0) + jnp.where(takes, moved, 0)
 
     all_blocks = main_blocks + head_blocks
-    taken_at = base - 2 * exports
+    taken_at = base - 12
 
     def block_of(i):
-        j = jnp.where(takes & (i >= taken_at + exports), i - exports, i)
-        own = jnp.where(is_last, jnp.where(j < head_blocks, j + main_blocks, j - head_blocks), j)
+        j = jnp.where(takes & (i >= taken_at + moved), i - moved, i)
+        heads = jnp.where(is_last, head_blocks, 0)
+        own = jnp.where(j < heads, j + main_blocks, lax.rem(j - heads + small_row // BLOCK, main_blocks))
         return jnp.where(takes & (j == i) & (i >= taken_at), i - taken_at + all_blocks, own)
 
     def rows_of(b):
@@ -856,36 +910,64 @@
         def _():
             keep_rows(rows).start()
 
-    given_rows = pl.ds(main_rows - exports * BLOCK, exports * BLOCK)
-    taken_rows = pl.ds(main_rows + head_rows, exports * BLOCK)
-
-    def give_copy():
-        return remote(part_out.at[given_rows], taken_buf, give_ss.at[0], give_rs.at[0], s + helper, z)
-
-    def return_copy():
-        return remote(o_acc.at[taken_rows], o_acc.at[given_rows], give_ss.at[1], give_rs.at[1], s - helper, z)
-
-    if exports:
-
-        @pl.when(gives)
-        def _():
-            part_out[given_rows, :] = acc[given_rows, :].astype(BF16)
-            give_copy().start()
-
-    last_step = main_blocks - exports + lag - 1
+    def given_rows(amount):
+        return pl.ds(small_row - amount * BLOCK, amount * BLOCK)
+
+    def taken_rows(amount):
+        return pl.ds(main_rows + head_rows, amount * BLOCK)
+
+    def give_copy(amount):
+        target = taken_buf.at[0 : amount * BLOCK]
+        return remote(part_out.at[given_rows(amount)], target, give_ss.at[0], give_rs.at[0], s + helper, z)
+
+    def return_copy(amount):
+        source, target = o_acc.at[taken_rows(amount)], o_acc.at[given_rows(amount)]
+        return remote(source, target, give_ss.at[1], give_rs.at[1], s - helper, z)
+
+    def each_export(cond, act):
+        for chip, amount in enumerate(exports):
+
+            @pl.when(cond & (lax.rem(s, helper) // 2 == chip))
+            def _():
+                act(amount)
+
+    def give(amount):
+        part_out[given_rows(amount), :] = acc[given_rows(amount), :].astype(BF16)
+        give_copy(amount).start()
+
+    def take(amount):
+        give_copy(amount).wait_recv()
+        acc[taken_rows(amount), :] = taken_buf[0 : amount * BLOCK].astype(F32)
+
+    def rest_of_gradients():
+        @pl.when(jnp.logical_not(late))
+        def _():
+            build_shift(micro - 1)
+            large_gradients(micro - 1)
+
+        if roomy:
+
+            @pl.when(late)
+            def _():
+                all_large_gradients()
+
+        each_export(gives, give)
+
+    last_step = main_blocks - max(exports, default=0) + lag - 1
     head_at = lag + 2
-    own_at = jnp.minimum(17 + 9 * distance, last_step)
-    rest_at = jnp.where(is_hub, 33, jnp.where(s < sections // 2, 40, 45))
+    own_at = jnp.minimum(22 + 9 * distance, last_step)
+    rest_at = 50
     rest_at = jnp.minimum(rest_at + 9 * distance, last_step)
 
     @pl.loop(0, count + lag)
     def _(i):
+        @pl.when(i == LARGE_AT)
+        def _():
+            rest_of_gradients()
+
         if exports:
 
-            @pl.when(takes & (i == taken_at))
-            def _():
-                give_copy().wait_recv()
-                acc[taken_rows, :] = taken_buf[...].astype(F32)
+            each_export(takes & (i == taken_at), take)
 
         @pl.when(i < count)
         def _():
@@ -902,9 +984,7 @@
 
             if exports:
 
-                @pl.when(b == all_blocks + exports - 1)
-                def _():
-                    return_copy().start()
+                each_export(b == all_blocks + moved - 1, lambda amount: return_copy(amount).start())
 
         @pl.when(jnp.logical_not(is_last) & (i >= head_at) & (i < head_at + head_blocks))
         def _():
@@ -916,32 +996,36 @@
             def _():
                 head_copy(j).start()
 
-        @pl.when(is_hub & (i == own_at))
-        def _():
-            own_hub().wait_recv()
-            for other in range(groups):
-
-                @pl.when(z != other)
-                def _():
-                    own_peer(other).start()
-
-            spread(z)
-
-        @pl.when((lax.rem(s, 2) == 0) & (i == rest_at))
+        for hop in range(groups):
+
+            @pl.when(is_hub & (i == jnp.minimum(own_at + 8 * hop, last_step)))
+            def _():
+                def pass_on(j, step, known, far):
+                    @pl.when(known)
+                    def _():
+                        if hop:
+                            part_along(j, 1).wait_recv()
+                            spread(j)
+
+                        @pl.when(far)
+                        def _():
+                            part_along(j, step).start()
+
+                if hop == 0:
+                    own_hub().wait_recv()
+                    spread(z)
+                pass_on(z - hop, 1, z >= hop, z < groups - 1)
+                pass_on(z + hop, -1, z + hop < groups, z > 0)
+
+        @pl.when((lax.rem(s, 2) == 0) & jnp.logical_not(is_hub) & (i == rest_at))
         def _():
             for j in range(groups):
 
-                @pl.when((z != j) | ((s > 0) & (s < hub)))
+                @pl.when((z != j) | (s > 0))
                 def _():
                     part_next(j).wait_recv()
 
-                @pl.when(is_hub & (z != j))
-                def _():
-                    spread(j)
-
-                @pl.when(jnp.logical_not(is_hub))
-                def _():
-                    part_next(j).start()
+                part_next(j).start()
 
     @pl.when(s > 0)
     def _():
@@ -959,9 +1043,13 @@
     def _():
         for j in range(groups):
 
-            @pl.when(z != j)
+            @pl.when((j <= z) & (z < groups - 1))
             def _():
-                own_peer(j).wait_send()
+                part_along(j, 1).wait_send()
+
+            @pl.when((j >= z) & (z > 0))
+            def _():
+                part_along(j, -1).wait_send()
 
             @pl.loop(0, sections // 2 - 1)
             def _(chip):
@@ -981,15 +1069,13 @@
 
     if exports:
 
-        @pl.when(gives)
-        def _():
-            return_copy().wait_recv()
-            keep_rows(given_rows).start()
-            give_copy().wait_send()
-
-        @pl.when(takes)
-        def _():
-            return_copy().wait_send()
+        def returned(amount):
+            return_copy(amount).wait_recv()
+            keep_rows(given_rows(amount)).start()
+            give_copy(amount).wait_send()
+
+        each_export(gives, returned)
+        each_export(takes, lambda amount: return_copy(amount).wait_send())
 
     keep_rows(pl.ds(0, main_rows + head_rows)).wait()
 
@@ -1000,19 +1086,14 @@
         def _():
             remote(o_acc.at[rows], o_acc.at[rows], zo_ss.at[0], zt_rs.at[0], s, outward).wait_send()
 
+    if exports:
+        each_export(gives, lambda amount: sum_sent(pl.ds(0, main_rows - amount * BLOCK)))
+        each_export(takes & jnp.logical_not(is_last), lambda amount: sum_sent(pl.ds(0, main_rows + amount * BLOCK)))
+
     @pl.when(is_last)
     def _():
-        sum_sent(pl.ds(0, main_rows + head_rows + (exports * BLOCK if helper + 1 == sections - 1 else 0)))
-
-    if exports:
-
-        @pl.when(takes & jnp.logical_not(is_last))
-        def _():
-            sum_sent(pl.ds(0, main_rows + exports * BLOCK))
-
-        @pl.when(gives)
-        def _():
-            sum_sent(pl.ds(0, main_rows - exports * BLOCK))
+        last_takes = exports[-1] if helper + helped == sections and exports else 0
+        sum_sent(pl.ds(0, main_rows + head_rows + last_takes * BLOCK))
 
     @pl.when(jnp.logical_not(is_last | gives | takes))
     def _():
@@ -1061,7 +1142,7 @@
     distance = groups // 2 - 1
     cycle = max(LAG * (2 * distance + 1) + 4 * distance + 4, 2 * LAG + 4)
     sends = slots if pieces > slots else 1
-    taken = exported_blocks(dims) * BLOCK
+    taken = max(exported_blocks(dims), default=0) * BLOCK
 
     scratch = [
         tile(pieces, PIECE, res),
@@ -1128,7 +1209,7 @@
         dma((head_blocks,)),
         dma((groups,)),
         dma((1,)),
-        dma((groups,)),
+        dma((2 * groups,)),
         dma((groups, sections // 2)),
         dma((groups,)),
         dma((1,)),

time: 170 us -> 166 us (0.976)
  Pallas kernels: 167 us -> 164 us
    pallas_call x1, Pallas kernels: 159 us -> 156 us  [run_step(): pl.pallas_call(functools.partial(step_kernel, dims), out_shape=(jax.Shape...]
where the time goes in v6:
time: 166 us; the launch traced here: 165 us
  Pallas kernels  164 us (99%)
    pallas_call x1, Pallas kernels, run_step(): pl.pallas_call(functools.partial(step_kernel, dims), out_shape=(jax.Shape...  156 us
    pallas_call x1, Pallas kernels, finish(): pl.pallas_call(functools.partial(finish_kernel, (mel_rows, half)), out_sh...  8.09 us

profile of v6, /device:TPU:0, one launch (start us, length us, event | category | flops | bytes accessed | tf_op | source)
XLA Modules:
  0.0 165.5 jit_solution(16781678713414821118)
XLA Ops:
  1.3 155.9 %train_step.1 = (bf16[2016,1024]{1,0:T(8,128)(2,1)}, bf16[4,8,96,128]{3,2,1,0:T(8,128)(2,1)}, bf16[64,1024]{1,0:T(8,128)(2,1)}) custom-call(s32[1]{0:T(128)S(6)} %copy.27.dil_ref, s32[2,4]{1,0:T(2,128)} %bitcast.36, s32[2,4]{1,0:T(2,128)} %bitcast.37, s32[109]{0:T(128)} %cnt_ref.1, s32[4,1,256]{2,1,0:T(1,128)} %bitcast.35, bf16[4,80]{1,0:T(4,128)(2,1)} %bitcast.38, ...), custom_call_target="tpu_custom_call" | custom-call | flops 10000000000 | bytes 30000000 | tf_op jit(solution)/shard_map/train_step/pallas_call | solution.py:1220
  157.2 8.1 %finish.1 = (bf16[64,1024]{1,0:T(8,128)(2,1)}, f32[1,1024,1024]{2,1,0:T(8,128)}, f32[80,1024]{1,0:T(8,128)}, f32[2,256,512]{2,1,0:T(8,128)}, f32[2,256,512]{2,1,...) custom-call(bf16[2016,1024]{1,0:T(8,128)(2,1)} %get-tuple-element.25, ...), custom_call_target="tpu_custom_call" | custom-call | tf_op jit(solution)/shard_map/finish/pallas_call | solution.py:1383

commit v7 on v6

--- a/solution.py
+++ b/solution.py
@@ -17,10 +17,11 @@
 PIECE = 128
 EXT = 96
 WIDE = 1024
-BLOCK = 32
-EXPORTS = (6,)
-LARGE_AT = 3
-LAG = 4
+BLOCK = 16
+EXPORTS = (12,)
+HEAD_GROUP = 4
+LARGE_AT = 6
+LAG = 8
 
 
 def dot(left, right):
@@ -831,7 +832,7 @@
     is_edge = (z == 0) | (z == groups - 1)
     is_mid = (z == groups // 2 - 1) | (z == groups // 2)
     distance = jnp.where(left, groups // 2 - 1 - z, z - groups // 2)
-    lag = LAG * (2 * distance + 1) + 4 * distance
+    lag = LAG * (2 * distance + 1) + 8 * distance
     base = jnp.where(is_last, main_blocks + head_blocks, main_blocks)
     helped = 2 * len(exports)
     gives = (s < helped) if exports else False
@@ -842,7 +843,7 @@
     count = base - jnp.where(gives, moved, 0) + jnp.where(takes, moved, 0)
 
     all_blocks = main_blocks + head_blocks
-    taken_at = base - 12
+    taken_at = base - 50
 
     def block_of(i):
         j = jnp.where(takes & (i >= taken_at + moved), i - moved, i)
@@ -867,8 +868,12 @@
         rows = rows_of(block_of(i))
         return remote(o_acc.at[rows], o_acc.at[rows], zo_ss.at[0], zt_rs.at[lax.rem(i, cycle)], s, outward)
 
+    def head_rows_of(j):
+        start = main_rows + j * HEAD_GROUP * BLOCK
+        return pl.ds(pl.multiple_of(start, BLOCK), HEAD_GROUP * BLOCK)
+
     def head_copy(j):
-        rows = rows_of(main_blocks + j)
+        rows = head_rows_of(j)
         return remote(o_acc.at[rows], o_acc.at[rows], hd_ss.at[0], hd_rs.at[j], s - 1, z)
 
     def send_part(i):
@@ -953,11 +958,10 @@
 
         each_export(gives, give)
 
-    last_step = main_blocks - max(exports, default=0) + lag - 1
-    head_at = lag + 2
-    own_at = jnp.minimum(22 + 9 * distance, last_step)
-    rest_at = 50
-    rest_at = jnp.minimum(rest_at + 9 * distance, last_step)
+    last_step = count + lag - 1
+    head_at = lag + 4 + HEAD_GROUP
+    own_at = jnp.minimum(40 + 18 * distance, last_step)
+    rest_at = jnp.minimum(88 + 9 * (s // 2) + 18 * distance, last_step)
 
     @pl.loop(0, count + lag)
     def _(i):
@@ -978,19 +982,25 @@
             finish_part(i - lag)
             b = block_of(i - lag)
 
-            @pl.when((b >= main_blocks) & (b < all_blocks))
+            in_group = b - main_blocks
+
+            @pl.when((b >= main_blocks) & (b < all_blocks) & (lax.rem(in_group, HEAD_GROUP) == HEAD_GROUP - 1))
             def _():
-                head_copy(b - main_blocks).start()
+                head_copy(in_group // HEAD_GROUP).start()
 
             if exports:
 
                 each_export(b == all_blocks + moved - 1, lambda amount: return_copy(amount).start())
 
-        @pl.when(jnp.logical_not(is_last) & (i >= head_at) & (i < head_at + head_blocks))
-        def _():
-            j = i - head_at
+        since = i - head_at
+
+        @pl.when(
+            jnp.logical_not(is_last) & (since >= 0) & (since < head_blocks) & (lax.rem(since, HEAD_GROUP) == 0)
+        )
+        def _():
+            j = since // HEAD_GROUP
             head_copy(j).wait_recv()
-            keep_rows(rows_of(main_blocks + j)).start()
+            keep_rows(head_rows_of(j)).start()
 
             @pl.when(s > 0)
             def _():
@@ -998,7 +1008,7 @@
 
         for hop in range(groups):
 
-            @pl.when(is_hub & (i == jnp.minimum(own_at + 8 * hop, last_step)))
+            @pl.when(is_hub & (i == jnp.minimum(own_at + 14 * hop, last_step)))
             def _():
                 def pass_on(j, step, known, far):
                     @pl.when(known)
@@ -1140,7 +1150,7 @@
         return pltpu.VMEM(shape, dtype)
 
     distance = groups // 2 - 1
-    cycle = max(LAG * (2 * distance + 1) + 4 * distance + 4, 2 * LAG + 4)
+    cycle = max(LAG * (2 * distance + 1) + 8 * distance + 4, 2 * LAG + 4)
     sends = slots if pieces > slots else 1
     taken = max(exported_blocks(dims), default=0) * BLOCK
 
@@ -1206,7 +1216,7 @@
         dma((cycle,)),
         dma((cycle,)),
         dma((1,)),
-        dma((head_blocks,)),
+        dma((head_blocks // HEAD_GROUP,)),
         dma((groups,)),
         dma((1,)),
         dma((2 * groups,)),
@@ -1277,8 +1287,8 @@
         for k, (row, rows) in enumerate(strips)
     ]
     loads.append(pltpu.make_async_copy(shared_hbm, shared, load_sem.at[3]))
-    for load in loads:
-        load.start()
+    for k in (0, 3, 1, 2):
+        loads[k].start()
     stores = []
 
     def store(source, target):
@@ -1288,11 +1298,51 @@
 
     store(gin, o_gin)
 
-    for k in range(2):
+    def dilated(k):
         loads[k].wait()
         rows = pl.ds(k * half, half)
         dil_buf[rows, :] = sums_buf[rows, :].astype(F32)
         store(dil_buf.at[rows, :], o_dil.at[0, rows, :])
+
+    dilated(0)
+
+    loads[3].wait()
+
+    def by_channel(f, loss):
+        extra = shared[f, 0, mel_rows:EXT, :].astype(F32)
+        mel_rows_buf[pl.ds(f, 1), :] = extra[0:1]
+        for h in range(2):
+            rows = pl.ds(pl.multiple_of(f * mel_rows, 16), mel_rows)
+            field[h, rows, :] = shared[f, h, 0:mel_rows, :].astype(F32)
+        return loss + extra + shared[f, 1, mel_rows:EXT, :].astype(F32)
+
+    loss = lax.fori_loop(0, frames, by_channel, jnp.zeros((EXT - mel_rows, PIECE), F32))
+    row = lax.broadcasted_iota(jnp.int32, loss.shape, 0)
+    loss = jnp.where((row >= 2) & (row < 5), loss, 0.0)
+    o_loss[...] = jnp.sum(jnp.sum(loss, axis=1, keepdims=True), axis=0, keepdims=True)
+    mel_columns[...] = jnp.transpose(mel_rows_buf[...])[0:mel_rows].astype(BF16)
+
+    parts = 4
+    channels = mel_rows // parts
+
+    def upsampling(part):
+        @pl.loop(0, channels // 10)
+        def _(group):
+            for j in range(10):
+                c = part * channels + group * 10 + j
+                rows = pl.ds(c, frames, stride=mel_rows)
+                matrix = jnp.concatenate([field[0, rows, :], field[1, rows, :]], axis=1)
+                up_buf[c] = dot(mel_columns[...], matrix.astype(BF16))
+
+        rows = pl.ds(part * channels, channels)
+        store(up_buf.at[rows], o_up.at[rows])
+
+    upsampling(0)
+    upsampling(1)
+    dilated(1)
+    upsampling(2)
+    upsampling(3)
+
     loads[2].wait()
     cond_buf[...] = sums_buf[first : first + mel_rows, :].astype(F32)
     o_bias[...] = sums_buf[first + mel_rows : first + EXT, :].astype(F32)[0:1]
@@ -1305,40 +1355,6 @@
         store(buffer, target)
         row += rows
 
-    loads[3].wait()
-
-    def by_channel(f, loss):
-        extra = shared[f, 0, mel_rows:EXT, :].astype(F32)
-        mel_rows_buf[pl.ds(f, 1), :] = extra[0:1]
-        for h in range(2):
-            rows = pl.ds(pl.multiple_of(f * mel_rows, 16), mel_rows)
-            field[h, rows, :] = shared[f, h, 0:mel_rows, :].astype(F32)
-        return loss + extra + shared[f, 1, mel_rows:EXT, :].astype(F32)
-
-    loss = lax.fori_loop(0, frames, by_channel, jnp.zeros((EXT - mel_rows, PIECE), F32))
-    row = lax.broadcasted_iota(jnp.int32, loss.shape, 0)
-    loss = jnp.where((row >= 2) & (row < 5), loss, 0.0)
-    o_loss[...] = jnp.sum(jnp.sum(loss, axis=1, keepdims=True), axis=0, keepdims=True)
-    mel_columns[...] = jnp.transpose(mel_rows_buf[...])[0:mel_rows].astype(BF16)
-
-    parts = 4
-    channels = mel_rows // parts
-
-    def upsampling(part):
-        @pl.loop(0, channels // 10)
-        def _(group):
-            for j in range(10):
-                c = part * channels + group * 10 + j
-                rows = pl.ds(c, frames, stride=mel_rows)
-                matrix = jnp.concatenate([field[0, rows, :], field[1, rows, :]], axis=1)
-                up_buf[c] = dot(mel_columns[...], matrix.astype(BF16))
-
-        rows = pl.ds(part * channels, channels)
-        store(up_buf.at[rows], o_up.at[rows])
-
-    for part in range(parts - 2):
-        upsampling(part)
-
     table[...] = jnp.zeros_like(table)
     time = lax.broadcasted_iota(jnp.int32, (2 * PIECE, PIECE), 0).astype(F32)
     number = lax.broadcasted_iota(jnp.int32, (2 * PIECE, PIECE), 1).astype(F32)
@@ -1355,9 +1371,6 @@
         table[...] += dot(jnp.concatenate(grads, axis=1), jnp.concatenate(hots, axis=0))
 
     o_table[...] = table[:, 0 : o_table.shape[1]]
-    for part in range(parts - 2, parts):
-        upsampling(part)
-
     for copy in stores:
         copy.wait()
 

time: 166 us -> 165 us (level)
  Pallas kernels: 164 us -> 162 us
    pallas_call x1, Pallas kernels: 156 us -> 154 us  [run_step(): pl.pallas_call(functools.partial(step_kernel, dims), out_shape=(jax.Shape...]
where the time goes in v7:
time: 165 us; the launch traced here: 163 us
  Pallas kernels  162 us (98%)
    pallas_call x1, Pallas kernels, run_step(): pl.pallas_call(functools.partial(step_kernel, dims), out_shape=(jax.Shape...  154 us
    pallas_call x1, Pallas kernels, finish(): pl.pallas_call(functools.partial(finish_kernel, (mel_rows, half)), out_sh...  7.46 us

profile of v7, /device:TPU:0, one launch (start us, length us, event | category | flops | bytes accessed | tf_op | source)
XLA Modules:
  0.0 163.2 jit_solution(3628306708251466332)
XLA Ops:
  1.3 154.2 %train_step.1 = (bf16[2016,1024]{1,0:T(8,128)(2,1)}, bf16[4,8,96,128]{3,2,1,0:T(8,128)(2,1)}, bf16[64,1024]{1,0:T(8,128)(2,1)}) custom-call(s32[1]{0:T(128)S(6)} %copy.27.dil_ref, s32[2,4]{1,0:T(2,128)} %bitcast.36, s32[2,4]{1,0:T(2,128)} %bitcast.37, s32[109]{0:T(128)} %cnt_ref.1, s32[4,1,256]{2,1,0:T(1,128)} %bitcast.35, bf16[4,80]{1,0:T(4,128)(2,1)} %bitcast.38, ...), custom_call_target="tpu_custom_call" | custom-call | flops 10000000000 | bytes 30000000 | tf_op jit(solution)/shard_map/train_step/pallas_call | solution.py:1230
  155.5 7.5 %finish.1 = (bf16[64,1024]{1,0:T(8,128)(2,1)}, f32[1,1024,1024]{2,1,0:T(8,128)}, f32[80,1024]{1,0:T(8,128)}, f32[2,256,512]{2,1,0:T(8,128)}, f32[2,256,512]{2,1,...) custom-call(bf16[2016,1024]{1,0:T(8,128)(2,1)} %get-tuple-element.25, ...), custom_call_target="tpu_custom_call" | custom-call | tf_op jit(solution)/shard_map/finish/pallas_call | solution.py:1396

commit v8 on v7

--- a/solution.py
+++ b/solution.py
@@ -21,7 +21,7 @@
 EXPORTS = (12,)
 HEAD_GROUP = 4
 LARGE_AT = 6
-LAG = 8
+LAG = 7
 
 
 def dot(left, right):
@@ -586,6 +586,8 @@
         def _():
             inp_buf[lax.rem(c, slots)] = jnp.transpose(grad_x)
 
+    def backward_message(m, h):
+        c = 2 * m + h
         gc_copy(c).wait_recv()
         message = cond_message(m, h)
 
@@ -613,12 +615,11 @@
             gc_buf[c, mel_rows:EXT, :] = tail.astype(BF16)
 
     def backward_pair(m):
-        grad_hidden = dot(both(sg_buf, 2 * m, (0, 1)), ws_ref[...])
-        grad_x = grad_field(m, (0, 1), grad_hidden).astype(BF16)
         for h in (1, 0):
             c = 2 * m + h
             reuse(gx_copy, c)
-            gx_out[lax.rem(c, slots)] = grad_x[h * PIECE : (h + 1) * PIECE]
+            grad_hidden = dot(sg_buf[c], ws_ref[...])
+            gx_out[lax.rem(c, slots)] = grad_field(m, (h,), grad_hidden).astype(BF16)
             gx_copy(c).start()
         for h in (1, 0):
             c = 2 * m + h
@@ -798,6 +799,8 @@
 
             backward_piece(m, 1)
             backward_piece(m, 0)
+            backward_message(m, 1)
+            backward_message(m, 0)
 
             @pl.when(is_first & (lax.rem(2 * m + 2, slots) == 0))
             def _():
@@ -960,7 +963,7 @@
 
     last_step = count + lag - 1
     head_at = lag + 4 + HEAD_GROUP
-    own_at = jnp.minimum(40 + 18 * distance, last_step)
+    own_at = jnp.minimum(48 + 18 * distance, last_step)
     rest_at = jnp.minimum(88 + 9 * (s // 2) + 18 * distance, last_step)
 
     @pl.loop(0, count + lag)

time: 165 us -> 164 us (level)
  no operation moved by 1% of the time
where the time goes in v8:
time: 164 us; the launch traced here: 163 us
  Pallas kernels  161 us (98%)
    pallas_call x1, Pallas kernels, run_step(): pl.pallas_call(functools.partial(step_kernel, dims), out_shape=(jax.Shape...  154 us
    pallas_call x1, Pallas kernels, finish(): pl.pallas_call(functools.partial(finish_kernel, (mel_rows, half)), out_sh...  7.46 us

profile of v8, /device:TPU:0, one launch (start us, length us, event | category | flops | bytes accessed | tf_op | source)
XLA Modules:
  0.0 162.8 jit_solution(18005966147920663466)
XLA Ops:
  1.3 153.9 %train_step.1 = (bf16[2016,1024]{1,0:T(8,128)(2,1)}, bf16[4,8,96,128]{3,2,1,0:T(8,128)(2,1)}, bf16[64,1024]{1,0:T(8,128)(2,1)}) custom-call(s32[1]{0:T(128)S(6)} %copy.27.dil_ref, s32[2,4]{1,0:T(2,128)} %bitcast.36, s32[2,4]{1,0:T(2,128)} %bitcast.37, s32[109]{0:T(128)} %cnt_ref.1, s32[4,1,256]{2,1,0:T(1,128)} %bitcast.35, bf16[4,80]{1,0:T(4,128)(2,1)} %bitcast.38, ...), custom_call_target="tpu_custom_call" | custom-call | flops 10000000000 | bytes 30000000 | tf_op jit(solution)/shard_map/train_step/pallas_call | solution.py:1233
  155.2 7.5 %finish.1 = (bf16[64,1024]{1,0:T(8,128)(2,1)}, f32[1,1024,1024]{2,1,0:T(8,128)}, f32[80,1024]{1,0:T(8,128)}, f32[2,256,512]{2,1,0:T(8,128)}, f32[2,256,512]{2,1,...) custom-call(bf16[2016,1024]{1,0:T(8,128)(2,1)} %get-tuple-element.25, ...), custom_call_target="tpu_custom_call" | custom-call | tf_op jit(solution)/shard_map/finish/pallas_call | solution.py:1399

commit v9 on v8

--- a/solution.py
+++ b/solution.py
@@ -968,6 +968,16 @@
 
     @pl.loop(0, count + lag)
     def _(i):
+        @pl.when(i == count - 1)
+        def _():
+            @pl.when(s > 0)
+            def _():
+                gin_arrived().wait_recv()
+
+            for c in range(pieces):
+                lanes = pl.ds(c * PIECE, PIECE)
+                pltpu.make_async_copy(gin_buf.at[c], o_gin.at[:, lanes], out_sem.at[1]).start()
+
         @pl.when(i == LARGE_AT)
         def _():
             rest_of_gradients()
@@ -1040,12 +1050,7 @@
 
                 part_next(j).start()
 
-    @pl.when(s > 0)
-    def _():
-        gin_arrived().wait_recv()
-
-    for c in range(pieces):
-        o_gin[:, c * PIECE : (c + 1) * PIECE] = gin_buf[c]
+    pltpu.make_async_copy(gin_buf, gin_buf, out_sem.at[1]).wait()
 
     @pl.when(is_first)
     def _():
@@ -1202,7 +1207,7 @@
         tile(EXT - mel_rows, PIECE, dtype=F32),
         dma((slots,)),
         dma((10,)),
-        dma((1,)),
+        dma((2,)),
         dma((1,)),
         dma((sends,)),
         dma((pieces,)),
@@ -1238,7 +1243,7 @@
             jax.ShapeDtypeStruct((share, pieces * PIECE), BF16),
         ),
         in_specs=[smem] * 4 + [vmem] * 4 + [anywhere] * 8,
-        out_specs=(anywhere, anywhere, vmem),
+        out_specs=(anywhere, anywhere, anywhere),
         scratch_shapes=scratch,
         compiler_params=pltpu.CompilerParams(
             collective_id=0, has_side_effects=True, vmem_limit_bytes=63 * 2**20

time: 164 us -> 164 us (level)
  no operation moved by 1% of the time
where the time goes in v9:
time: 164 us; the launch traced here: 162 us
  Pallas kernels  161 us (98%)
    pallas_call x1, Pallas kernels, run_step(): pl.pallas_call(functools.partial(step_kernel, dims), out_shape=(jax.Shape...  153 us
    pallas_call x1, Pallas kernels, finish(): pl.pallas_call(functools.partial(finish_kernel, (mel_rows, half)), out_sh...  7.46 us

profile of v9, /device:TPU:0, one launch (start us, length us, event | category | flops | bytes accessed | tf_op | source)
XLA Modules:
  0.0 162.3 jit_solution(3377958949801238390)
XLA Ops:
  1.3 153.4 %train_step.1 = (bf16[2016,1024]{1,0:T(8,128)(2,1)}, bf16[4,8,96,128]{3,2,1,0:T(8,128)(2,1)}, bf16[64,1024]{1,0:T(8,128)(2,1)}) custom-call(s32[1]{0:T(128)S(6)} %copy.27.dil_ref, s32[2,4]{1,0:T(2,128)} %bitcast.36, s32[2,4]{1,0:T(2,128)} %bitcast.37, s32[109]{0:T(128)} %cnt_ref.1, s32[4,1,256]{2,1,0:T(1,128)} %bitcast.35, bf16[4,80]{1,0:T(4,128)(2,1)} %bitcast.38, ...), custom_call_target="tpu_custom_call" | custom-call | flops 10000000000 | bytes 30000000 | tf_op jit(solution)/shard_map/train_step/pallas_call | solution.py:1238
  154.7 7.5 %finish.1 = (bf16[64,1024]{1,0:T(8,128)(2,1)}, f32[1,1024,1024]{2,1,0:T(8,128)}, f32[80,1024]{1,0:T(8,128)}, f32[2,256,512]{2,1,0:T(8,128)}, f32[2,256,512]{2,1,...) custom-call(bf16[2016,1024]{1,0:T(8,128)(2,1)} %get-tuple-element.25, ...), custom_call_target="tpu_custom_call" | custom-call | tf_op jit(solution)/shard_map/finish/pallas_call | solution.py:1404
